TPU v7x, 32 devices: a whole 2x2x4 slice. The times are simulated.
32 devices in a mesh: row: 16 (over z, y, core), col: 2 (over x).
Axes of the slice: x: 2, y: 2, z: 4, core: 2. Of those that a mesh axis runs over, the one named last changes fastest.
Arguments:
- positions: float32 [3, 16, 2, 128], P(None, 'row', 'col'), may hold values from 0 to 12
- species: int32 [16, 2, 128], P('row', 'col'), may hold values from 0 to 5
- counts: int32 [16, 2, 128], P('row', 'col'), may hold values from 32 to 64
- neighbours: int32 [16, 2, 64, 128], P('row', 'col'), may hold values from 0 to 1151
- ghost_index: int32 [16, 2, 8, 128], P('row', 'col'), may hold values from 0 to 127
- wave_numbers: int32 [3, 1000], replicated, may hold values from -6 to 6, as said below
- embedding: float32 [6, 128], replicated, may hold values from -6 to 6
- w_radial: float32 [16, 128], replicated, may hold values from -1.5 to 1.5
- w_mix: float32 [128, 128], replicated, may hold values from -0.5 to 0.5
- w_read: float32 [128, 128], replicated, may hold values from -0.5 to 0.5
- w_out: float32 [128], replicated, may hold values from -0.5 to 0.5
- amplitude: float32 [128], replicated, may hold values from 10 to 100
- kernel_width: float32 [128], replicated, may hold values from 0.5 to 4
- filter_gain: float32 [1000, 128], replicated, may hold values from 0.1 to 1.9
Outputs:
- forces: float32 [3, 16, 2, 128], P(None, 'row', 'col')
- virial: float32 [3, 3], replicated
Inputs may be any that keep to these rules, and one draw needn't show every extreme that they name: `wave_numbers`: the first two rows lie in -6 to 6, the third in 1 to 6. `counts`: slots at or beyond an atom's count are padding. `neighbours`: indices into the extended table of step one. `ghost_index`: local atom indices; repeats are allowed.
All inputs are finite; a program needn't handle non-finite values.
Results may differ from a plain program's by a relative error of at most 0.0003.
Values sent between devices are 32-bit elements; how exact they have to be, the bound alone decides.
No kernel may reach another device: no remote copies, remote signals or barrier semaphores. Data moves between devices by JAX's collectives and lax.ppermute only.
A program may use at most 64 MiB of HBM per device.

v0:
```python
import math

import jax
import jax.numpy as jnp
from jax import lax
from jax.sharding import PartitionSpec as P

CELL_EDGE = 12.0
HEIGHT = 36.0
EXACT = lax.Precision.HIGHEST
DIRECTIONS = ((-1, -1), (-1, 0), (-1, 1), (0, -1), (0, 1), (1, -1), (1, 0), (1, 1))


def with_halo(cells, sides, width):
    for axis, dim in sides:
        count = lax.axis_size(axis)
        head = lax.slice_in_dim(cells, 0, width, axis=dim)
        tail = lax.slice_in_dim(cells, cells.shape[dim] - width, cells.shape[dim], axis=dim)
        cells = jnp.concatenate(
            [
                lax.ppermute(tail, axis, [(i, (i + 1) % count) for i in range(count)]),
                cells,
                lax.ppermute(head, axis, [((i + 1) % count, i) for i in range(count)]),
            ],
            axis=dim,
        )
    return cells


def radial_rates(count):
    return 0.003 * jnp.exp(math.log(1.6) * jnp.arange(count, dtype=jnp.int32).astype(jnp.float32))


def block_size():
    return 125


def short_range(
    edge_vectors, own_kinds, edge_kinds, edge_valid, embedding, w_radial, w_mix, w_read, w_out
):
    slot_count, atom_count = edge_valid.shape
    species_count = embedding.shape[0]
    decay_rates = radial_rates(w_radial.shape[0])
    group_size = 4
    groups = slot_count // group_size
    vector_groups = jnp.moveaxis(edge_vectors.reshape(3, groups, group_size, atom_count), 1, 0)
    kind_groups = edge_kinds.reshape(groups, group_size, atom_count)
    mask_groups = edge_valid.reshape(groups, group_size, atom_count)
    species_ids = jnp.arange(species_count, dtype=jnp.int32)

    def one_group(running, inputs):
        vectors, neighbour_kinds, edge_mask = inputs
        squared = jnp.sum(vectors * vectors, axis=0)
        radial_basis = jnp.exp(-decay_rates[:, None, None] * squared[None])
        filters = jnp.einsum("rsa,rc->sac", radial_basis, w_radial, precision=EXACT)
        onehot = (neighbour_kinds[:, :, None] == species_ids[None, None, :]).astype(jnp.float32)
        features = jnp.einsum("sak,kc->sac", onehot, embedding, precision=EXACT)
        return (running + jnp.sum(edge_mask[:, :, None] * filters * features, axis=0), None)

    initial = jnp.zeros((atom_count, w_radial.shape[1]), jnp.float32)
    summed, _unused = lax.scan(
        jax.checkpoint(one_group), initial, (vector_groups, kind_groups, mask_groups)
    )
    aggregate = summed / slot_count
    own_onehot = (own_kinds[:, None] == species_ids[None, :]).astype(jnp.float32)
    initial_features = jnp.dot(own_onehot, embedding, precision=EXACT)
    updated = initial_features + jax.nn.silu(jnp.dot(aggregate, w_mix, precision=EXACT))
    readout = jax.nn.silu(jnp.dot(updated, w_read, precision=EXACT))
    energy = jnp.sum(jnp.dot(readout, w_out, precision=EXACT))
    return (energy, updated)


def structure_factors(coords, features, wave_vectors):
    wave_count = wave_vectors.shape[1]
    block_width = block_size()
    blocks = jnp.moveaxis(wave_vectors.reshape(3, wave_count // block_width, block_width), 1, 0)

    def one_block(wave_block):
        phases = jnp.einsum("xk,xn->kn", wave_block, coords, precision=EXACT)
        return jnp.stack(
            [
                jnp.dot(jnp.cos(phases), features, precision=EXACT),
                jnp.dot(jnp.sin(phases), features, precision=EXACT),
            ]
        )

    pieces = lax.map(jax.checkpoint(one_block), blocks)
    return jnp.moveaxis(pieces, 1, 0).reshape(2, wave_count, features.shape[1])


def wave_vectors_of(wave_numbers, row_count, col_count):
    lengths = jnp.array([CELL_EDGE * row_count, CELL_EDGE * col_count, HEIGHT], jnp.float32)
    return 2.0 * math.pi * wave_numbers.astype(jnp.float32) / lengths[:, None]


def spread_directions(payload):
    empty_cell = jnp.zeros_like(payload[:1])
    return jnp.concatenate([payload[:4], empty_cell, payload[4:]], axis=0).reshape(
        (3, 3) + payload.shape[1:]
    )


def gather_directions(padded):
    corner_cells = padded[0::2, 0::2]
    flattened = corner_cells.reshape((9,) + corner_cells.shape[2:])
    return jnp.concatenate([flattened[:4], flattened[5:]], axis=0)


def per_device(
    positions,
    species,
    counts,
    neighbours,
    ghost_index,
    wave_numbers,
    embedding,
    w_radial,
    w_mix,
    w_read,
    w_out,
    amplitude,
    kernel_width,
    filter_gain,
):
    own_coords = positions[:, 0, 0, :]
    own_kinds = species[0, 0]
    live_counts = counts[0, 0]
    neighbour_ids = neighbours[0, 0]
    ghost_list = ghost_index[0, 0]
    atom_count = own_kinds.shape[0]
    ghost_count = ghost_list.shape[1]
    direction_count = ghost_list.shape[0]
    slot_count = neighbour_ids.shape[0]
    sent_coords = jnp.moveaxis(own_coords[:, ghost_list], 1, 0)
    sent_kinds = own_kinds[ghost_list].astype(jnp.float32)[:, None, :]
    outgoing = spread_directions(jnp.concatenate([sent_coords, sent_kinds], axis=1))
    padded = with_halo(outgoing, (("row", 0), ("col", 1)), 1)
    incoming = gather_directions(padded)
    step_table = jnp.array(DIRECTIONS, jnp.float32) * CELL_EDGE
    shift_table = jnp.concatenate(
        [step_table, jnp.zeros((direction_count, 1), jnp.float32)], axis=1
    )
    ghost_coords = incoming[:, :3, :] + shift_table[:, :, None]
    ext_coords = jnp.concatenate(
        [own_coords, jnp.moveaxis(ghost_coords, 1, 0).reshape(3, -1)], axis=1
    )
    ext_kinds = jnp.concatenate([own_kinds, incoming[:, 3, :].reshape(-1).astype(jnp.int32)])
    edge_vectors = ext_coords[:, neighbour_ids] - own_coords[:, None, :]
    edge_kinds = ext_kinds[neighbour_ids]
    edge_valid = (jnp.arange(slot_count, dtype=jnp.int32)[:, None] < live_counts[None, :]).astype(
        jnp.float32
    )

    def local_short(vectors):
        return short_range(
            vectors, own_kinds, edge_kinds, edge_valid, embedding, w_radial, w_mix, w_read, w_out
        )

    (short_energy, updated), short_back = jax.vjp(local_short, edge_vectors)
    row_count = lax.axis_size("row")
    col_count = lax.axis_size("col")
    volume = CELL_EDGE * row_count * CELL_EDGE * col_count * HEIGHT
    domain_shift = jnp.stack(
        [
            lax.axis_index("row").astype(jnp.float32) * CELL_EDGE,
            lax.axis_index("col").astype(jnp.float32) * CELL_EDGE,
            jnp.zeros((), jnp.float32),
        ]
    )
    global_coords = own_coords + domain_shift[:, None]
    wave_vectors = wave_vectors_of(wave_numbers, row_count, col_count)
    local_factors, factor_back = jax.vjp(
        lambda coords, features: structure_factors(coords, features, wave_vectors),
        global_coords,
        updated,
    )
    unit_weight = jnp.ones((), jnp.float32)
    squared_norm = jnp.sum(wave_vectors * wave_vectors, axis=0)
    weights = (
        amplitude[None, :] * filter_gain * jnp.exp(-kernel_width[None, :] * squared_norm[:, None])
    )
    factors = lax.psum(local_factors, ("row", "col"))
    coefficients = weights[None] * factors / volume
    strain_terms = jnp.sum(kernel_width[None, None, :] * coefficients * factors, axis=(0, 2))
    kspace_virial = jnp.zeros((3, 3), jnp.float32)
    tail_virial = jnp.eye(3, dtype=jnp.float32) * (
        0.5 * jnp.sum(coefficients * factors)
    ) - jnp.einsum("xk,k,yk->xy", wave_vectors, strain_terms, wave_vectors, precision=EXACT)
    coord_grad, feature_grad = factor_back(coefficients)
    vector_grad = short_back((unit_weight, feature_grad))[0]
    table_size = ext_coords.shape[1]
    table_grad = (
        jnp.zeros((3, table_size), jnp.float32)
        .at[:, neighbour_ids.reshape(-1)]
        .add(vector_grad.reshape(3, -1))
    )
    own_grad = table_grad[:, :atom_count] - jnp.sum(vector_grad, axis=1) + coord_grad
    ghost_grad = jnp.moveaxis(
        table_grad[:, atom_count:].reshape(3, direction_count, ghost_count), 1, 0
    )
    returned = gather_directions(
        with_halo(spread_directions(ghost_grad), (("row", 0), ("col", 1)), 1)
    )
    own_grad = own_grad.at[:, ghost_list.reshape(-1)].add(
        jnp.moveaxis(returned, 1, 0).reshape(3, -1)
    )
    local_virial = kspace_virial - jnp.einsum(
        "xsa,ysa->xy", vector_grad, edge_vectors, precision=EXACT
    )
    virial = (lax.psum(local_virial, ("row", "col")) + tail_virial) / volume
    forces = -own_grad
    return (forces[:, None, None, :], virial)


def solution(mesh):
    return jax.shard_map(
        per_device,
        mesh=mesh,
        in_specs=(
            P(None, "row", "col", None),
            P("row", "col", None),
            P("row", "col", None),
            P("row", "col", None, None),
            P("row", "col", None, None),
            P(),
            P(),
            P(),
            P(),
            P(),
            P(),
            P(),
            P(),
            P(),
        ),
        out_specs=(P(None, "row", "col", None), P()),
        check_vma=False,
    )
```

profile of v0, /device:TPU:0, one launch (start us, length us, event | category | flops | bytes accessed | tf_op | source)
XLA Modules:
  0.0 412.6 jit_solution(2831930785269175037)
XLA Ops:
  8.9 2.8 gather_fusion
  11.9 5.9 %gather_fusion.1 = s32[1024]{0:T(1024)S(1)} fusion(s32[128]{0:T(128)} %bitcast.211, s32[1024]{0:T(1024)S(1)} %fusion.82), kind=kCustom, calls=%fused_computation.1 | custom fusion | bytes 12288 | tf_op jit(solution)/shard_map/gather | solution.py:135
  18.3 5.1 %collective-permute-start.1 = (f32[1,3,4,128]{3,2,1,0:T(4,128)S(1)}, f32[1,3,4,128]{3,2,1,0:T(4,128)S(1)}, u32[]{:S(2)}, u32[]{:S(2)}) collective-permute-start(f32[1,3,4,128]{3,2,1,0:T(4,128)S(1)} %get-tuple-element.718), channel_id=1, source_target_pairs={{2,0},{4,2},{6,4},{8,6},{10,8},{12,10},{14,12},{16,14},{18,16},{20... | collective-permute-start | bytes 18440 | tf_op jit(solution)/shard_map/ppermute | solution.py:23
  24.7 1.9 collective-permute-start.2
  27.1 1.3 collective-permute-done.2
  28.4 1.9 collective-permute-done.3
  30.7 27.9 %gather_fusion.2 = f32[8192,3]{1,0:T(8,128)} fusion(f32[3,1152]{0,1:T(8,128)S(1)} %pad_maximum_fusion, s32[8192]{0:T(1024)S(1)} %fusion.67), kind=kCustom, calls=%fused_computation.2 | custom fusion | bytes 229376 | tf_op jit(solution)/shard_map/gather | solution.py:148
  58.6 2.8 copy.110
  61.5 45.5 %gather_fusion.3 = s32[8192]{0:T(1024)S(1)} fusion(s32[1152]{0:T(1024)S(1)} %pad_add_fusion, s32[8192]{0:T(1024)S(1)} %fusion.67), kind=kCustom, calls=%fused_computation.3 | custom fusion | bytes 98304 | tf_op jit(solution)/shard_map/gather | solution.py:149
  107.1 19.2 %while.57 = (s32[]{:T(128)}, f32[128,128]{1,0:T(8,128)S(1)}, f32[16,4,128]{2,1,0:T(4,128)S(1)}, f32[16,3,4,128]{3,2,1,0:T(4,128)S(1)}, f32[16,128]{1,0:T(8,128)S...) while((s32[]{:T(128)}, f32[128,128]{1,0:T(8,128)S(1)}, ...), condition=%wide.region_4.5_spmd.clone, body=%wide.region_1.0_spmd.clone.sunk | while | flops 17528384 | bytes 820467 | solution.py:61
  126.8 9.5 %while.55 = (s32[]{:T(128)}, f32[8,2,125,128]{3,2,1,0:T(8,128)S(1)}, f32[8,3,125]{2,1,0:T(4,128)S(1)}, f32[3,128]{1,0:T(4,128)S(1)}, f32[128,128]{1,0:T(8,128)S(1)}, /*index=5*/s32[]{:T(128)}) while((s32[]{:T(128)}, f32[8,2,125,128]{3,2,1,0:T(8,128)S(1)}, f32[8,3,125]{2,1,0:T(4,128)S(1)}, f32[3,128]{1,0:T(4,128)S(1)}, ...), condition=%wide.region_6.7_spmd, body=%wide.region_5.6_spmd.sunk | while | flops 49760000 | bytes 717389 | solution.py:87
  136.4 1.1 reshape.237
  137.7 128.1 %all-reduce.3.cloned.1.call-done = f32[2,1000,128]{2,1,0:T(8,128)} async-done(((f32[2,1000,128]{2,1,0:T(8,128)}), f32[2,1000,128]{2,1,0:T(8,128)}) %all-reduce.3.cloned.1.call-update) | async-done | bytes 1024016 | tf_op jit(solution)/shard_map/psum | solution.py:182
  265.9 2.2 multiply_reduce_fusion.3
  268.2 15.1 %while.58 = (s32[]{:T(128)}, f32[3,128]{1,0:T(4,128)S(1)}, f32[128,128]{1,0:T(8,128)S(1)}, f32[8,3,125]{2,1,0:T(4,128)S(1)}, f32[8,2,125,128]{3,2,0,1:T(8,128)S(...) while((s32[]{:T(128)}, f32[3,128]{1,0:T(4,128)S(1)}, ...), condition=%wide.region_9.10_spmd.clone, body=%wide.region_8.9_spmd.clone.sunk | while | flops 99569920 | bytes 1569780 | solution.py:87
  283.8 15.3 %while.56 = (s32[]{:T(128)}, f32[128,128]{1,0:T(8,128)S(1)}, f32[16,3,4,128]{3,2,1,0:T(4,128)S(1)}, f32[16,3,4,128]{3,2,1,0:T(4,128)S(1)}, s32[16,4,128]{2,1,0:T...) while((s32[]{:T(128)}, f32[128,128]{1,0:T(8,128)S(1)}, ...), condition=%wide.region_13.14_spmd.clone, body=%wide.region_10.13_spmd.clone.sunk | while | flops 17473604 | bytes 652721 | solution.py:61
  299.2 2.6 copy.121
  301.8 44.5 %scatter_custom_fusion = f32[3,1152]{0,1:T(8,128)S(1)} fusion(s32[8192]{0:T(1024)S(1)} %bitcast.243, f32[8192,3]{1,0:T(8,128)} %copy.121, f32[]{:T(128)} %constant.154.clone.1), kind=kCustom, calls=%fused_computation.83 | custom fusion | flops 24576 | bytes 14336 | tf_op jit(solution)/shard_map/scatter-add | solution.py:195
  347.3 39.3 %psum.15 = f32[3,3]{1,0:T(4,128)S(1)} all-reduce(f32[3,3]{1,0:T(4,128)S(1)} %fusion.45), channel_id=1, replica_groups=mesh['row'=16,'col'=2] {'row','col'}, use_global_device_ids=true, to_apply=%region_17.18 | all-reduce | flops 9 | bytes 72 | tf_op jit(solution)/shard_map/psum | solution.py:210
  386.6 4.4 %collective-permute-start.5 = (f32[1,3,3,128]{3,2,1,0:T(4,128)S(1)}, f32[1,3,3,128]{3,2,1,0:T(4,128)S(1)}, u32[]{:S(2)}, u32[]{:S(2)}) collective-permute-start(f32[1,3,3,128]{3,2,1,0:T(4,128)S(1)} %get-tuple-element.726), channel_id=1, source_target_pairs={{2,0},{4,2},{6,4},{8,6},{10,8},{12,10},{14,12},{16,14},{18,16},{20... | collective-permute-start | bytes 13832 | tf_op jit(solution)/shard_map/ppermute | solution.py:23
  392.7 2.3 collective-permute-start.6
  395.2 1.5 collective-permute-done.6
  396.7 2.0 collective-permute-done.7
  399.0 6.1 %scatter_fusion = f32[3,128]{0,1:T(8,128)S(1)} fusion(f32[3,128]{0,1:T(8,128)S(1)} %copy.127, s32[1024]{0:T(1024)S(1)} %bitcast.244, f32[1024,3]{1,0:T(8,128)S(1)} %bitcast.225), kind=kCustom, calls=%fused_computation.5 | custom fusion | flops 3072 | bytes 40960 | tf_op jit(solution)/shard_map/scatter-add | solution.py:204
  (478 shorter events, 65.1 us)
Async XLA Ops:
  7.2 130.3 %copy-start = (f32[128,128]{1,0:T(8,128)S(1)}, f32[128,128]{1,0:T(8,128)}, u32[]{:S(2)}) copy-start(f32[128,128]{1,0:T(8,128)} %param.33) | copy-start | bytes 196612
  7.2 16.4 %copy-start.11 = (f32[3]{0:T(128)S(1)}, f32[3]{0:T(128)}, u32[]{:S(2)}) copy-start(f32[3]{0:T(128)} %constant.179) | copy-start | bytes 40
  7.2 23.1 %copy-start.9 = (f32[8,3]{1,0:T(8,128)S(1)}, f32[8,3]{1,0:T(8,128)}, u32[]{:S(2)}) copy-start(f32[8,3]{1,0:T(8,128)} %constant.181) | copy-start | bytes 292
  7.2 16.1 %copy-start.5 = (s32[1,1,64,128]{3,2,1,0:T(8,128)S(1)}, s32[1,1,64,128]{3,2,1,0:T(8,128)}, u32[]{:S(2)}) copy-start(s32[1,1,64,128]{3,2,1,0:T(8,128)} %param.27) | copy-start | bytes 98308
  7.2 16.3 %copy-start.13 = (f32[128]{0:T(128)S(1)}, f32[128]{0:T(128)}, u32[]{:S(2)}) copy-start(f32[128]{0:T(128)} %param.36) | copy-start | bytes 1540
  7.2 16.4 %copy-start.7 = (s32[3,1000]{1,0:T(4,128)S(1)}, s32[3,1000]{1,0:T(4,128)}, u32[]{:S(2)}) copy-start(s32[3,1000]{1,0:T(4,128)} %param.29) | copy-start | bytes 36004
  7.2 16.6 %copy-start.10 = (f32[128]{0:T(128)S(1)}, f32[128]{0:T(128)}, u32[]{:S(2)}) copy-start(f32[128]{0:T(128)} %param.35) | copy-start | bytes 1540
  7.2 16.6 %copy-start.3 = (f32[1000,128]{1,0:T(8,128)S(1)}, f32[1000,128]{1,0:T(8,128)}, u32[]{:S(2)}) copy-start(f32[1000,128]{1,0:T(8,128)} %param.37) | copy-start | bytes 1536004
  7.3 19.5 %copy-start.12 = (s32[1,1,128]{2,1,0:T(1,128)S(1)}, s32[1,1,128]{2,1,0:T(1,128)}, u32[]{:S(2)}) copy-start(s32[1,1,128]{2,1,0:T(1,128)} %param.26) | copy-start | bytes 1540
  7.3 258.6 %all-reduce.3.cloned.1.call-start = ((), (), s32[]{:S(2)}) async-start(), calls=%async_computation | async-start | bytes 2048000 | tf_op jit(solution)/shard_map/psum | solution.py:182
  17.8 6.8 %collective-permute-start = (f32[1,3,4,128]{3,2,1,0:T(4,128)S(1)}, f32[1,3,4,128]{3,2,1,0:T(4,128)S(1)}, u32[]{:S(2)}, u32[]{:S(2)}) collective-permute-start(f32[1,3,4,128]{3,2,1,0:T(4,128)S(1)} %get-tuple-element.717), channel_id=1, source_target_pairs={{0,2},{2,4},{4,6},{6,8},{8,10},{10,12},{12,14},{14,16},{16,18},{18... | collective-permute-start | bytes 18440 | tf_op jit(solution)/shard_map/ppermute | solution.py:21
  18.3 6.4 %collective-permute-start.1 = (f32[1,3,4,128]{3,2,1,0:T(4,128)S(1)}, f32[1,3,4,128]{3,2,1,0:T(4,128)S(1)}, u32[]{:S(2)}, u32[]{:S(2)}) collective-permute-start(f32[1,3,4,128]{3,2,1,0:T(4,128)S(1)} %get-tuple-element.718), channel_id=1, source_target_pairs={{2,0},{4,2},{6,4},{8,6},{10,8},{12,10},{14,12},{16,14},{18,16},{20... | collective-permute-start | bytes 18440 | tf_op jit(solution)/shard_map/ppermute | solution.py:23
  24.0 37.5 %copy-start.1 = (s32[1,1,128]{2,1,0:T(1,128)S(1)}, s32[1,1,128]{2,1,0:T(1,128)}, u32[]{:S(2)}) copy-start(s32[1,1,128]{2,1,0:T(1,128)} %param.25) | copy-start | bytes 1540
  24.7 3.7 collective-permute-start.2
  26.6 3.7 collective-permute-start.3
  61.5 45.6 %copy-start.2 = (f32[16,128]{1,0:T(8,128)S(1)}, f32[16,128]{1,0:T(8,128)}, u32[]{:S(2)}) copy-start(f32[16,128]{1,0:T(8,128)} %param.31) | copy-start | bytes 24580
  61.5 45.6 %copy-start.4 = (f32[6,128]{1,0:T(8,128)S(1)}, f32[6,128]{1,0:T(8,128)}, u32[]{:S(2)}) copy-start(f32[6,128]{1,0:T(8,128)} %param.30) | copy-start | bytes 9220
  107.1 19.3 %copy-start.6 = (f32[128,128]{1,0:T(8,128)S(1)}, f32[128,128]{1,0:T(8,128)}, u32[]{:S(2)}) copy-start(f32[128,128]{1,0:T(8,128)} %param.32) | copy-start | bytes 196612
  126.8 10.7 %copy-start.8 = (s32[1,1,8,128]{3,2,1,0:T(8,128)S(1)}, s32[1,1,8,128]{3,2,1,0:T(8,128)}, u32[]{:S(2)}) copy-start(s32[1,1,8,128]{3,2,1,0:T(8,128)} %param.28) | copy-start | bytes 12292
  268.2 15.1 %copy-start.14 = (f32[128]{0:T(128)S(1)}, f32[128]{0:T(128)}, u32[]{:S(2)}) copy-start(f32[128]{0:T(128)} %param.34) | copy-start | bytes 1540
  386.6 6.0 %collective-permute-start.4 = (f32[1,3,3,128]{3,2,1,0:T(4,128)S(1)}, f32[1,3,3,128]{3,2,1,0:T(4,128)S(1)}, u32[]{:S(2)}, u32[]{:S(2)}) collective-permute-start(f32[1,3,3,128]{3,2,1,0:T(4,128)S(1)} %get-tuple-element.725), channel_id=1, source_target_pairs={{0,2},{2,4},{4,6},{6,8},{8,10},{10,12},{12,14},{14,16},{16,18},{18... | collective-permute-start | bytes 13832 | tf_op jit(solution)/shard_map/ppermute | solution.py:21
  386.6 6.0 %collective-permute-start.5 = (f32[1,3,3,128]{3,2,1,0:T(4,128)S(1)}, f32[1,3,3,128]{3,2,1,0:T(4,128)S(1)}, u32[]{:S(2)}, u32[]{:S(2)}) collective-permute-start(f32[1,3,3,128]{3,2,1,0:T(4,128)S(1)} %get-tuple-element.726), channel_id=1, source_target_pairs={{2,0},{4,2},{6,4},{8,6},{10,8},{12,10},{14,12},{16,14},{18,16},{20... | collective-permute-start | bytes 13832 | tf_op jit(solution)/shard_map/ppermute | solution.py:23
  392.7 4.0 collective-permute-start.6
  395.0 3.7 collective-permute-start.7
Sparse Core Ops, SparseCore 0:
  137.6 128.2 all-reduce.2
where the time goes:
time: 413 us
  waiting for transfers between devices  135 us (33%)
  local copies, waits for them, and re-layouts  92.9 us (22%)
  matrix products  56.2 us (14%)
  other arithmetic  55.9 us (14%)
  blocking collectives  39.3 us (10%)
  between operations  15.3 us (4%)
  starting transfers between devices  14.5 us (4%)
    psum x1, waiting for transfers between devices, per_device(): factors = lax.psum(local_factors, ('row', 'col'))  128 us
    gather x1, local copies, waits for them, and re-layouts, per_device(): edge_kinds = ext_kinds[neighbour_ids]  45.5 us
    scatter-add x1, other arithmetic, per_device(): table_grad = jnp.zeros((3, table_size), jnp.float32).at[:, neighbour_ids....  44.5 us
    psum x1, blocking collectives, per_device(): virial = (lax.psum(local_virial, ('row', 'col')) + tail_virial) / volume  39.3 us
    gather x2, local copies, waits for them, and re-layouts, per_device(): edge_vectors = ext_coords[:, neighbour_ids] - own_coords[:, None, :]  30.7 us
    dot_general x32, matrix products, one_group(): filters = jnp.einsum('rsa,rc->sac', radial_basis, w_radial, precision=EXACT)  16.1 us
    dot_general x32, matrix products, one_group(): features = jnp.einsum('sak,kc->sac', onehot, embedding, precision=EXACT)  14 us
    ppermute x4, starting transfers between devices, with_halo(): lax.ppermute(head, axis, [((i + 1) % count, i) for i in range(count)])  9.69 us
  transfers between devices with their start and end apart: 9, of which 7 were waited for; matrix products, arithmetic and copies ran while one was open for 1% of the time, Pallas kernels for 0%

commit v1 on v0

v1 whole, which is shorter than its diff:
```python
import functools
import math

import jax
import jax.numpy as jnp
from jax import lax
from jax.experimental import pallas as pl
from jax.experimental.pallas import tpu as pltpu
from jax.sharding import PartitionSpec as P

CELL_EDGE = 12.0
HEIGHT = 36.0
KMAX = 6
HARMONICS = 8
EXACT = lax.Precision.HIGHEST
GOOD = lax.Precision.HIGH
DIRECTIONS = ((-1, -1), (-1, 0), (-1, 1), (0, -1), (0, 1), (1, -1), (1, 0), (1, 1))
F32 = jnp.float32
BF16 = jnp.bfloat16
AXES = ("row", "col")


def radial_rate(order):
    return 0.003 * 1.6**order


def round_up(value, step):
    return -(-value // step) * step


def direction_slots(row_count, col_count):
    seen = {}
    slots = []
    for row_step, col_step in DIRECTIONS:
        key = (row_step % row_count, col_step % col_count)
        slots.append(seen.get(key, 0))
        seen[key] = slots[-1] + 1
    return slots, max(seen.values())


def dot(lhs, rhs, lhs_dim, rhs_dim, precision=None):
    return lax.dot_general(
        lhs,
        rhs,
        (((lhs_dim,), (rhs_dim,)), ((), ())),
        precision=precision,
        preferred_element_type=F32,
    )


def split(values):
    high = values.astype(BF16).astype(F32)
    return high, values - high


def gain_kernel(dims, gain_ref, waves_ref, amp_ref, width_ref, phi_ref, width_out_ref):
    device_count, channel_count, own_channels, lengths, volume = dims
    me = lax.axis_index("row") * lax.axis_size("col") + lax.axis_index("col")
    wave_count = gain_ref.shape[0]
    rows = (KMAX + 1) * HARMONICS
    lanes = own_channels * HARMONICS
    place = lax.broadcasted_iota(jnp.int32, (8, channel_count), 0) * device_count + me
    chosen = (lax.broadcasted_iota(jnp.int32, (8, channel_count), 1) == place).astype(F32)
    own_gain = dot(chosen, gain_ref[...], 1, 1, EXACT)
    first, second, third = waves_ref[0:1, :], waves_ref[1:2, :], waves_ref[2:3, :]
    sign = jnp.where(first < 0, 2, 0) + jnp.where(second < 0, 1, 0)
    key = sign * rows + jnp.abs(first) * HARMONICS + jnp.abs(second)
    spots = lax.broadcasted_iota(jnp.int32, (4 * rows, wave_count), 0) == key
    onehot = jnp.where(spots, 1.0, 0.0).astype(BF16)
    heights = lax.broadcasted_iota(jnp.int32, (HARMONICS, wave_count), 0) + 1 == third
    blocks = [
        jnp.where(heights, own_gain[q : q + 1, :], 0.0) for q in range(own_channels)
    ]
    wide = jnp.concatenate(blocks, axis=0)
    high = wide.astype(BF16)
    rest = wide - high.astype(F32)
    middle = rest.astype(BF16)
    low = (rest - middle.astype(F32)).astype(BF16)
    summed = dot(onehot, high, 1, 1) + (dot(onehot, middle, 1, 1) + dot(onehot, low, 1, 1))
    lane = lax.broadcasted_iota(jnp.int32, (8, channel_count), 1)
    wanted = jnp.minimum((lane // HARMONICS) * device_count + me, channel_count - 1)
    amp = jnp.take_along_axis(jnp.broadcast_to(amp_ref[...], (8, channel_count)), wanted, axis=1)
    width = jnp.take_along_axis(
        jnp.broadcast_to(width_ref[...], (8, channel_count)), wanted, axis=1
    )
    amp, width = amp[0:1, :lanes], width[0:1, :lanes]
    k1, k2, k3 = grid_numbers(rows, lanes, lengths)
    squared = k1 * k1 + k2 * k2 + k3 * k3
    base = amp * jnp.exp(-width * squared) * (1.0 / volume)
    for sign_id in range(4):
        phi_ref[sign_id] = base * summed[sign_id * rows : (sign_id + 1) * rows, :]
    width_out_ref[...] = jnp.broadcast_to(width, (8, lanes))


def grid_numbers(rows, lanes, lengths):
    row_id = lax.broadcasted_iota(jnp.int32, (rows, lanes), 0)
    lane_id = lax.broadcasted_iota(jnp.int32, (rows, lanes), 1)
    k1 = (row_id // HARMONICS).astype(F32) * (2.0 * math.pi / lengths[0])
    k2 = (row_id % HARMONICS).astype(F32) * (2.0 * math.pi / lengths[1])
    k3 = (lane_id % HARMONICS + 1).astype(F32) * (2.0 * math.pi / lengths[2])
    return k1, k2, k3


def short_forward_kernel(
    own_channels,
    own_ref,
    prev_ref,
    next_ref,
    left_ref,
    right_ref,
    counts_ref,
    ids_ref,
    radial_ref,
    embed_ref,
    mix_ref,
    read_ref,
    out_ref,
    send_ref,
    vec_ref,
    kind_ref,
    dupd_ref,
    slope_ref,
    table,
    base,
    pooled,
    weights,
    kinds8,
):
    slot_count, atom_count = ids_ref.shape
    species_count, channel_count = embed_ref.shape
    radial_count = radial_ref.shape[0]
    device_count = send_ref.shape[0]

    def cell(row_step, col_step):
        if col_step == 0:
            return {0: own_ref, -1: prev_ref, 1: next_ref}[row_step]
        side = left_ref if col_step < 0 else right_ref
        return side.at[{0: 0, -1: 1, 1: 2}[row_step]]

    for order, (row_step, col_step) in enumerate(DIRECTIONS):
        block = cell(row_step, col_step)
        source = len(DIRECTIONS) - 1 - order
        base[0, order : order + 1, :] = block[0:1, :] + row_step * CELL_EDGE
        base[1, order : order + 1, :] = block[1:2, :] + col_step * CELL_EDGE
        base[2, order : order + 1, :] = block[2:3, :]
        base[3, order : order + 1, :] = block[3:4, :]
        base[4, order : order + 1, :] = block[4 + source : 5 + source, :]
    picks = base[4].astype(jnp.int32)
    for part in range(4):
        table[part, 0:1, :] = own_ref[part : part + 1, :]
        table[part, 8:16, :] = jnp.take_along_axis(base[part], picks, axis=1)

    ids = ids_ref[...]
    lane = ids & (atom_count - 1)
    source = ids // atom_count
    gathered = []
    for part in range(4):
        wide = jnp.broadcast_to(table[part, 0:1, :], ids.shape)
        values = jnp.take_along_axis(wide, lane, axis=1)
        for order in range(len(DIRECTIONS)):
            wide = jnp.broadcast_to(table[part, 8 + order : 9 + order, :], ids.shape)
            values = jnp.where(
                source == order + 1, jnp.take_along_axis(wide, lane, axis=1), values
            )
        gathered.append(values)
    slot = lax.broadcasted_iota(jnp.int32, ids.shape, 0)
    kind = jnp.where(slot < counts_ref[...], gathered[3], -1.0)
    kind_ref[...] = kind
    squared = jnp.zeros(ids.shape, F32)
    for part in range(3):
        vector = gathered[part] - own_ref[part : part + 1, :]
        vec_ref[part] = vector
        squared = squared + vector * vector
    masks = [kind == float(k) for k in range(species_count)]
    for order in range(radial_count):
        basis = jnp.exp(squared * (-radial_rate(order)))
        for k in range(species_count):
            spot = k * radial_count + order
            pooled[spot : spot + 1, :] = jnp.sum(
                jnp.where(masks[k], basis, 0.0), axis=0, keepdims=True
            )
    for k in range(species_count):
        weights[k * radial_count : (k + 1) * radial_count, :] = (
            radial_ref[...] * embed_ref[k : k + 1, :]
        )
    aggregate = dot(weights[...], pooled[...], 0, 0, EXACT) * (1.0 / slot_count)
    kinds8[...] = jnp.zeros_like(kinds8)
    kinds8[0:species_count, :] = embed_ref[...]
    own_hot = (
        lax.broadcasted_iota(jnp.int32, kinds8.shape, 0).astype(F32) == own_ref[3:4, :]
    ).astype(F32)
    initial = dot(kinds8[...], own_hot, 0, 0, EXACT)
    before = dot(mix_ref[...], aggregate, 0, 0, EXACT)
    gate = 1.0 / (1.0 + jnp.exp(-before))
    updated = initial + before * gate
    slope_ref[...] = gate + before * gate * (1.0 - gate)
    for q in range(own_channels):
        low, high = q * device_count, min(channel_count, (q + 1) * device_count)
        send_ref[0 : high - low, q, :] = updated[low:high, :]
        if high - low < device_count:
            send_ref[high - low :, q, :] = jnp.zeros(
                (device_count - (high - low), atom_count), F32
            )
    for part in range(3):
        send_ref[:, own_channels + part, :] = jnp.broadcast_to(
            own_ref[part : part + 1, :], (device_count, atom_count)
        )
    readout = dot(read_ref[...], updated, 0, 0, EXACT)
    gate = 1.0 / (1.0 + jnp.exp(-readout))
    scale = jnp.broadcast_to(out_ref[...], (channel_count, channel_count)).T
    dread = scale[:, 0:atom_count] * (gate + readout * gate * (1.0 - gate))
    dupd_ref[...] = dot(read_ref[...], dread, 1, 0, EXACT)


def turn_tables(turns, multiples):
    angle = turns * multiples
    halves = jnp.floor(2.0 * angle + 0.5)
    rest = angle - 0.5 * halves
    sign = 1.0 - 2.0 * (halves - 2.0 * jnp.floor(0.5 * halves))
    square = rest * rest

    def series(first, last):
        terms = [
            (-1.0) ** (p // 2) * (2.0 * math.pi) ** p / math.factorial(p)
            for p in range(first, last + 1, 2)
        ]
        total = jnp.full_like(square, terms[-1])
        for term in reversed(terms[:-1]):
            total = total * square + term
        return total

    return sign * series(0, 12), sign * rest * series(1, 13)


def wave_kernel(
    dims, recv_ref, phi_ref, width_ref, send_ref, virial_ref, planes, lifted, heights
):
    own_channels, col_count, chunk, lengths = dims
    device_count, _, atom_count = recv_ref.shape
    rows = (KMAX + 1) * HARMONICS
    lanes = own_channels * HARMONICS
    chunk_count = device_count // chunk
    multiples = lax.broadcasted_iota(jnp.int32, (HARMONICS, atom_count), 0).astype(F32)

    def fill(chunk_id):
        def one(index, _):
            device = chunk_id * chunk + index
            spot = pl.ds(pl.multiple_of(index * atom_count, atom_count), atom_count)
            block = recv_ref[device]
            corner_row = (device // col_count).astype(F32) * CELL_EDGE
            corner_col = (device % col_count).astype(F32) * CELL_EDGE
            turns_x = (block[own_channels : own_channels + 1] + corner_row) * (1.0 / lengths[0])
            turns_y = (block[own_channels + 1 : own_channels + 2] + corner_col) * (1.0 / lengths[1])
            turns_z = block[own_channels + 2 : own_channels + 3] * (1.0 / lengths[2])
            cos_x, sin_x = turn_tables(turns_x, multiples)
            cos_y, sin_y = turn_tables(turns_y, multiples)
            cos_z, sin_z = turn_tables(turns_z, multiples + 1.0)
            for m in range(KMAX + 1):
                cos_row, sin_row = cos_x[m : m + 1, :], sin_x[m : m + 1, :]
                for p, (first, second) in enumerate(
                    ((cos_row, cos_y), (cos_row, sin_y), (sin_row, cos_y), (sin_row, sin_y))
                ):
                    low = p * rows + m * HARMONICS
                    planes[low : low + HARMONICS, spot] = first * second
            heights[0, :, spot] = cos_z
            heights[1, :, spot] = sin_z
            for q in range(own_channels):
                feature = block[q : q + 1, :]
                lifted[q * HARMONICS : (q + 1) * HARMONICS, spot] = feature * cos_z
                lifted[lanes + q * HARMONICS : lanes + (q + 1) * HARMONICS, spot] = feature * sin_z
            return 0

        lax.fori_loop(0, chunk, one, 0, unroll=2)

    def project(chunk_id):
        fill(chunk_id)
        return dot(planes[...], lifted[...], 1, 1, GOOD)

    if chunk_count == 1:
        sums = project(0)
    else:
        sums = lax.fori_loop(
            0,
            chunk_count,
            lambda c, total: total + project(c),
            jnp.zeros((4 * rows, 2 * lanes), F32),
        )
    cos_part, sin_part = sums[:, :lanes], sums[:, lanes:]
    blocks = [(cos_part[p * rows : (p + 1) * rows], sin_part[p * rows : (p + 1) * rows]) for p in range(4)]
    (cc_c, cc_s), (cs_c, cs_s), (sc_c, sc_s), (ss_c, ss_s) = blocks
    zero = jnp.zeros((rows, lanes), F32)
    d_cc_c = d_cc_s = d_cs_c = d_cs_s = d_sc_c = d_sc_s = d_ss_c = d_ss_s = zero
    total = even = first_odd = second_odd = both_odd = zero
    for sign_id, (s1, s2) in enumerate(((1.0, 1.0), (1.0, -1.0), (-1.0, 1.0), (-1.0, -1.0))):
        real = cc_c - s1 * s2 * ss_c - s1 * sc_s - s2 * cs_s
        imag = cc_s - s1 * s2 * ss_s + s1 * sc_c + s2 * cs_c
        phi = phi_ref[sign_id]
        dreal, dimag = phi * real, phi * imag
        power = dreal * real + dimag * imag
        d_cc_c, d_ss_c = d_cc_c + dreal, d_ss_c - s1 * s2 * dreal
        d_sc_s, d_cs_s = d_sc_s - s1 * dreal, d_cs_s - s2 * dreal
        d_cc_s, d_ss_s = d_cc_s + dimag, d_ss_s - s1 * s2 * dimag
        d_sc_c, d_cs_c = d_sc_c + s1 * dimag, d_cs_c + s2 * dimag
        even = even + power
        first_odd = first_odd + s1 * power
        second_odd = second_odd + s2 * power
        both_odd = both_odd + s1 * s2 * power
    width = width_ref[0:1, :]
    k1, k2, k3 = grid_numbers(rows, lanes, lengths)

    def total_of(values):
        return jnp.sum(jnp.sum(values, axis=0, keepdims=True), axis=1, keepdims=True)

    energy = 0.5 * total_of(even)
    scaled = width * even
    terms = {
        (0, 0): energy - total_of(k1 * k1 * scaled),
        (1, 1): energy - total_of(k2 * k2 * scaled),
        (2, 2): energy - total_of(k3 * k3 * scaled),
        (0, 1): -total_of(k1 * k2 * width * both_odd),
        (0, 2): -total_of(k1 * k3 * width * first_odd),
        (1, 2): -total_of(k2 * k3 * width * second_odd),
    }
    virial_ref[...] = virial_row(terms, virial_ref.shape)

    values = jnp.concatenate(
        [
            jnp.concatenate(pair, axis=1)
            for pair in ((d_cc_c, d_cc_s), (d_cs_c, d_cs_s), (d_sc_c, d_sc_s), (d_ss_c, d_ss_s))
        ],
        axis=0,
    )
    cc, cs, sc, ss = (values[p * rows : (p + 1) * rows] for p in range(4))
    row_id = lax.broadcasted_iota(jnp.int32, (rows, 2 * lanes), 0)
    m1 = (row_id // HARMONICS).astype(F32)
    m2 = (row_id % HARMONICS).astype(F32)
    along_x = jnp.concatenate([m1 * sc, m1 * ss, -m1 * cc, -m1 * cs], axis=0)
    along_y = jnp.concatenate([m2 * cs, -m2 * cc, m2 * ss, -m2 * sc], axis=0)
    stacked = jnp.concatenate([values, along_x, along_y], axis=1)

    numbers = multiples + 1.0

    def back(chunk_id):
        if chunk_count > 1:
            fill(chunk_id)
        result = dot(stacked, planes[...], 0, 0, GOOD)
        for index in range(chunk):
            low, high = index * atom_count, (index + 1) * atom_count
            device = chunk_id * chunk + index
            cos_z, sin_z = heights[0, :, low:high], heights[1, :, low:high]
            part = result[:, low:high]
            grad_x = jnp.zeros((HARMONICS, atom_count), F32)
            grad_y = grad_x
            grad_z = grad_x
            pieces = []
            for q in range(own_channels):
                a, b = q * HARMONICS, lanes + q * HARMONICS
                on_cos, on_sin = part[a : a + HARMONICS], part[b : b + HARMONICS]
                pieces.append(on_cos * cos_z + on_sin * sin_z)
                lift_cos = lifted[a : a + HARMONICS, low:high]
                lift_sin = lifted[b : b + HARMONICS, low:high]
                grad_z = grad_z + on_sin * lift_cos - on_cos * lift_sin
                a, b = a + 2 * lanes, b + 2 * lanes
                grad_x = grad_x + part[a : a + HARMONICS] * lift_cos + part[b : b + HARMONICS] * lift_sin
                a, b = a + 2 * lanes, b + 2 * lanes
                grad_y = grad_y + part[a : a + HARMONICS] * lift_cos + part[b : b + HARMONICS] * lift_sin
            pieces.append(grad_x * (2.0 * math.pi / lengths[0]))
            pieces.append(grad_y * (2.0 * math.pi / lengths[1]))
            pieces.append(grad_z * numbers * (2.0 * math.pi / lengths[2]))
            for spot, piece in enumerate(pieces):
                send_ref[device, spot : spot + 1, :] = jnp.sum(piece, axis=0, keepdims=True)

    if chunk_count == 1:
        back(0)
    else:

        def step(chunk_id, carry):
            back(chunk_id)
            return carry

        lax.fori_loop(0, chunk_count, step, 0)


def virial_row(terms, shape):
    lane = lax.broadcasted_iota(jnp.int32, shape, 1)
    row = jnp.zeros(shape, F32)
    for (i, j), value in terms.items():
        spots = (lane == 3 * i + j) | (lane == 3 * j + i)
        row = jnp.where(spots, value, row)
    return row


def short_back_kernel(
    dims,
    recv_ref,
    vec_ref,
    kind_ref,
    dupd_ref,
    slope_ref,
    ids_ref,
    radial_ref,
    embed_ref,
    mix_ref,
    wave_virial_ref,
    send_ref,
    own_ref,
    fgrad,
    weights,
    dpool,
    parts,
):
    own_channels, row_count, col_count = dims
    slot_count, atom_count = ids_ref.shape
    species_count, channel_count = embed_ref.shape
    radial_count = radial_ref.shape[0]
    device_count = send_ref.shape[0]
    table_rows = round_up(len(DIRECTIONS) + 1, 16)
    for q in range(own_channels):
        low, high = q * device_count, min(channel_count, (q + 1) * device_count)
        fgrad[low:high, :] = recv_ref[0 : high - low, q, :]
    total = jnp.sum(recv_ref[...], axis=0)
    dbefore = (fgrad[...] + dupd_ref[...]) * slope_ref[...]
    daggregate = dot(mix_ref[...], dbefore, 1, 0, EXACT)
    for k in range(species_count):
        weights[k * radial_count : (k + 1) * radial_count, :] = (
            radial_ref[...] * embed_ref[k : k + 1, :]
        )
    dpool[...] = dot(weights[...], daggregate, 1, 0, EXACT)
    vectors = [vec_ref[part] for part in range(3)]
    squared = vectors[0] * vectors[0] + vectors[1] * vectors[1] + vectors[2] * vectors[2]
    kind = kind_ref[...]
    sums = [jnp.zeros(kind.shape, F32) for _ in range(species_count)]
    for order in range(radial_count):
        rate = radial_rate(order)
        basis = jnp.exp(squared * (-rate)) * (-2.0 * rate / slot_count)
        for k in range(species_count):
            spot = k * radial_count + order
            sums[k] = sums[k] + basis * dpool[spot : spot + 1, :]
    slope = jnp.zeros(kind.shape, F32)
    for k in range(species_count):
        slope = jnp.where(kind == float(k), sums[k], slope)
    grads = [slope * vector for vector in vectors]

    def total_of(values):
        return jnp.sum(jnp.sum(values, axis=0, keepdims=True), axis=1, keepdims=True)

    terms = {
        (i, j): -total_of(grads[i] * vectors[j]) for i in range(3) for j in range(i, 3)
    }
    virial = virial_row(terms, (1, atom_count)) + wave_virial_ref[0:1, :]
    for part in range(3):
        parts[2 * part], parts[2 * part + 1] = split(grads[part])

    sublane = lax.broadcasted_iota(jnp.int32, (atom_count, atom_count), 0)
    table_id = lax.broadcasted_iota(jnp.int32, (table_rows, atom_count), 0)
    group = 8
    scattered = jnp.zeros((atom_count, 6 * table_rows), F32)
    for low in range(0, slot_count, group):
        hots, columns = [], []
        for s in range(low, low + group):
            ids = ids_ref[s : s + 1, :]
            hots.append(jnp.where(sublane == (ids & (atom_count - 1)), 1.0, 0.0).astype(BF16))
            mine = table_id == ids // atom_count
            columns.append(
                jnp.concatenate(
                    [
                        jnp.where(mine, parts[p, s : s + 1, :], 0.0).astype(BF16)
                        for p in range(6)
                    ],
                    axis=0,
                )
            )
        scattered = scattered + dot(
            jnp.concatenate(hots, axis=1), jnp.concatenate(columns, axis=1), 1, 1
        )
    rows = scattered.T
    me_row, me_col = lax.axis_index("row"), lax.axis_index("col")
    slots, _ = direction_slots(row_count, col_count)
    send_ref[...] = jnp.zeros_like(send_ref)
    send_ref[:, 0, :] = jnp.broadcast_to(virial, (device_count, atom_count))
    own_ref[...] = jnp.zeros_like(own_ref)
    for part in range(3):
        low = 2 * part * table_rows
        both = rows[low : low + table_rows] + rows[low + table_rows : low + 2 * table_rows]
        own_ref[part : part + 1, :] = (
            both[0:1, :]
            - jnp.sum(grads[part], axis=0, keepdims=True)
            + total[own_channels + part : own_channels + part + 1, :]
        )
        for order, (row_step, col_step) in enumerate(DIRECTIONS):
            target = lax.rem(me_row + row_step + row_count, row_count) * col_count + lax.rem(
                me_col + col_step + col_count, col_count
            )
            send_ref[target, 1 + 3 * slots[order] + part, :] = both[1 + order, :]


def final_kernel(dims, recv_ref, own_ref, ghost_ref, forces_ref, virial_ref, parts):
    row_count, col_count, volume = dims
    atom_count = own_ref.shape[1]
    slots, _ = direction_slots(row_count, col_count)
    me_row, me_col = lax.axis_index("row"), lax.axis_index("col")
    sublane = lax.broadcasted_iota(jnp.int32, (atom_count, ghost_ref.shape[1]), 0)
    hots = []
    parts[...] = jnp.zeros_like(parts)
    for order, (row_step, col_step) in enumerate(DIRECTIONS):
        source = lax.rem(me_row - row_step + row_count, row_count) * col_count + lax.rem(
            me_col - col_step + col_count, col_count
        )
        opposite = len(DIRECTIONS) - 1 - order
        hots.append(
            jnp.where(sublane == ghost_ref[opposite : opposite + 1, :], 1.0, 0.0).astype(BF16)
        )
        low, high = order * ghost_ref.shape[1], (order + 1) * ghost_ref.shape[1]
        for part in range(3):
            row = recv_ref[source, 1 + 3 * slots[order] + part, :].reshape(1, -1)
            parts[2 * part : 2 * part + 1, low:high], parts[2 * part + 1 : 2 * part + 2, low:high] = split(row)
    returned = dot(jnp.concatenate(hots, axis=1), parts[...].astype(BF16), 1, 1).T
    for part in range(3):
        forces_ref[part : part + 1, :] = -(
            own_ref[part : part + 1, :]
            + (returned[2 * part : 2 * part + 1, :] + returned[2 * part + 1 : 2 * part + 2, :])
        )
    virial = jnp.sum(recv_ref[:, 0, :], axis=0, keepdims=True) * (1.0 / volume)
    for i in range(3):
        virial_ref[i : i + 1, :] = virial[:, 3 * i : 3 * i + 3]


def sides(block, axis):
    count = lax.axis_size(axis)
    before = lax.ppermute(block, axis, [(i, (i + 1) % count) for i in range(count)])
    if count == 2:
        return before, before
    return before, lax.ppermute(block, axis, [((i + 1) % count, i) for i in range(count)])


def per_device(
    positions,
    species,
    counts,
    neighbours,
    ghost_index,
    wave_numbers,
    embedding,
    w_radial,
    w_mix,
    w_read,
    w_out,
    amplitude,
    kernel_width,
    filter_gain,
):
    row_count = lax.axis_size("row")
    col_count = lax.axis_size("col")
    device_count = row_count * col_count
    atom_count = positions.shape[3]
    slot_count = neighbours.shape[2]
    direction_count, ghost_count = ghost_index.shape[2:]
    species_count, channel_count = embedding.shape
    radial_count = w_radial.shape[0]
    own_channels = -(-channel_count // device_count)
    lengths = (CELL_EDGE * row_count, CELL_EDGE * col_count, HEIGHT)
    volume = lengths[0] * lengths[1] * lengths[2]
    rows = (KMAX + 1) * HARMONICS
    lanes = own_channels * HARMONICS
    slab = round_up(own_channels + 3, 8)
    _, shared = direction_slots(row_count, col_count)
    slab_back = round_up(1 + 3 * shared, 8)
    chunk = math.gcd(device_count, 32)

    def shape(*dims):
        return jax.ShapeDtypeStruct(dims, F32)

    def scratch(*dims):
        return pltpu.VMEM(dims, F32)

    ids = neighbours.reshape(slot_count, atom_count)
    ghosts = ghost_index.reshape(direction_count, ghost_count)
    raw = jnp.concatenate(
        [
            positions.reshape(3, atom_count),
            species.reshape(1, atom_count).astype(F32),
            ghosts.astype(F32),
        ],
        axis=0,
    )
    before, after = sides(raw, "row")
    column = jnp.stack([raw, before, after])
    left, right = sides(column, "col")

    phi, width = pl.pallas_call(
        functools.partial(
            gain_kernel, (device_count, channel_count, own_channels, lengths, volume)
        ),
        out_shape=(shape(4, rows, lanes), shape(8, lanes)),
        cost_estimate=pl.CostEstimate(
            flops=2 * 4 * rows * filter_gain.shape[0] * 3 * lanes,
            bytes_accessed=4 * filter_gain.size,
            transcendentals=0,
        ),
        name="wave_weights",
    )(filter_gain, wave_numbers, amplitude.reshape(1, -1), kernel_width.reshape(1, -1))

    send, vectors, kinds, dupd, slope = pl.pallas_call(
        functools.partial(short_forward_kernel, own_channels),
        out_shape=(
            shape(device_count, slab, atom_count),
            shape(3, slot_count, atom_count),
            shape(slot_count, atom_count),
            shape(channel_count, atom_count),
            shape(channel_count, atom_count),
        ),
        scratch_shapes=[
            scratch(4, 16, atom_count),
            scratch(5, direction_count, atom_count),
            scratch(species_count * radial_count, atom_count),
            scratch(species_count * radial_count, channel_count),
            scratch(round_up(species_count, 8), channel_count),
        ],
        name="short_forward",
    )(
        raw,
        before,
        after,
        left,
        right,
        counts.reshape(1, atom_count),
        ids,
        w_radial,
        embedding,
        w_mix,
        w_read,
        w_out.reshape(1, -1),
    )
    features = lax.all_to_all(send, AXES, 0, 0, tiled=True)

    send, wave_virial = pl.pallas_call(
        functools.partial(wave_kernel, (own_channels, col_count, chunk, lengths)),
        out_shape=(shape(device_count, slab, atom_count), shape(8, atom_count)),
        scratch_shapes=[
            scratch(4 * rows, chunk * atom_count),
            scratch(2 * lanes, chunk * atom_count),
            scratch(2, HARMONICS, chunk * atom_count),
        ],
        compiler_params=pltpu.CompilerParams(vmem_limit_bytes=40 * 1024 * 1024),
        name="waves",
    )(features, phi, width)
    gradients = lax.all_to_all(send, AXES, 0, 0, tiled=True)

    send, own = pl.pallas_call(
        functools.partial(short_back_kernel, (own_channels, row_count, col_count)),
        out_shape=(shape(device_count, slab_back, atom_count), shape(8, atom_count)),
        scratch_shapes=[
            scratch(channel_count, atom_count),
            scratch(species_count * radial_count, channel_count),
            scratch(species_count * radial_count, atom_count),
            scratch(6, slot_count, atom_count),
        ],
        name="short_back",
    )(gradients, vectors, kinds, dupd, slope, ids, w_radial, embedding, w_mix, wave_virial)
    returned = lax.all_to_all(send, AXES, 0, 0, tiled=True)

    forces, virial = pl.pallas_call(
        functools.partial(final_kernel, (row_count, col_count, volume)),
        out_shape=(shape(3, atom_count), shape(3, 3)),
        scratch_shapes=[scratch(16, direction_count * ghost_count)],
        name="returned_ghosts",
    )(returned, own, ghosts)
    return (forces[:, None, None, :], virial)


def solution(mesh):
    return jax.shard_map(
        per_device,
        mesh=mesh,
        in_specs=(
            P(None, "row", "col", None),
            P("row", "col", None),
            P("row", "col", None),
            P("row", "col", None, None),
            P("row", "col", None, None),
            P(),
            P(),
            P(),
            P(),
            P(),
            P(),
            P(),
            P(),
            P(),
        ),
        out_specs=(P(None, "row", "col", None), P()),
        check_vma=False,
    )
```

time: 413 us -> 69.5 us (0.17)
  waiting for transfers between devices: 135 us -> 9.08 us
  local copies, waits for them, and re-layouts: 92.9 us -> 4.68 us
  matrix products: 56.2 us -> 0 us
  other arithmetic: 55.9 us -> 0.72 us
  Pallas kernels: 0 us -> 18.6 us
  blocking collectives: 39.3 us -> 22.9 us
  between operations: 15.3 us -> 0.69 us
    psum x1 -> x0, waiting for transfers between devices: 128 us -> none  [per_device(): factors = lax.psum(local_factors, ('row', 'col'))]
    gather x6 -> x0, local copies, waits for them, and re-layouts: 85.1 us -> none  [the longest x1 45.5 us: per_device(): edge_kinds = ext_kinds[neighbour_ids]]
    dot_general x143 -> x0, matrix products: 56.2 us -> none  [the longest x32 16.1 us: one_group(): filters = jnp.einsum('rsa,rc->sac', radial_basis, w_radial, precision=EXACT)]
    scatter-add x2 -> x0, other arithmetic: 50.5 us -> none  [the longest x1 44.5 us: per_device(): table_grad = jnp.zeros((3, table_size), jnp.float32).at[:, neighbour_ids....]
    psum x1 -> x0, blocking collectives: 39.3 us -> none  [per_device(): virial = (lax.psum(local_virial, ('row', 'col')) + tail_virial) / volume]
    all_to_all x0 -> x2, blocking collectives: none -> 22.9 us  [the longest x1 11.9 us: per_device(): returned = lax.all_to_all(send, AXES, 0, 0, tiled=True)]
    pallas_call x0 -> x5, Pallas kernels: none -> 18.6 us  [the longest x1 6.94 us: per_device(): pl.pallas_call(functools.partial(wave_kernel, (own_channels, col_count, c...]
    ppermute x8 -> x3, starting transfers between devices: 14.5 us -> 7.43 us  [the longest x1 5.06 us: sides(): lax.ppermute(block, axis, [((i + 1) % count, i) for i in range(count)])]
  transfers between devices with their start and end apart: 9 -> 4, of which waited for: 7 -> 4; matrix products, arithmetic and copies ran while one was open for 1% -> 0% of each run, Pallas kernels for 0% -> 4%
where the time goes in v1:
time: 69.5 us; the launch traced here: 69 us
  blocking collectives  22.9 us (33%)
  Pallas kernels  18.6 us (27%)
  starting transfers between devices  12.4 us (18%)
  waiting for transfers between devices  9.08 us (13%)
  local copies, waits for them, and re-layouts  4.68 us (7%)
  other arithmetic  0.72 us (1%)
    all_to_all x1, blocking collectives, per_device(): returned = lax.all_to_all(send, AXES, 0, 0, tiled=True)  11.9 us
    all_to_all x1, blocking collectives, per_device(): gradients = lax.all_to_all(send, AXES, 0, 0, tiled=True)  11 us
    pallas_call x1, Pallas kernels, per_device(): pl.pallas_call(functools.partial(wave_kernel, (own_channels, col_count, c...  6.94 us
    all_to_all x1, waiting for transfers between devices, per_device(): features = lax.all_to_all(send, AXES, 0, 0, tiled=True)  5.76 us
    ppermute x1, starting transfers between devices, sides(): lax.ppermute(block, axis, [((i + 1) % count, i) for i in range(count)])  5.06 us
    all_to_all x1, starting transfers between devices, per_device(): features = lax.all_to_all(send, AXES, 0, 0, tiled=True)  4.93 us
    unnamed x22, local copies, waits for them, and re-layouts  4.68 us
    pallas_call x1, Pallas kernels, per_device(): pl.pallas_call(functools.partial(short_forward_kernel, own_channels), out...  3.69 us
  transfers between devices with their start and end apart: 4, of which 4 were waited for; matrix products, arithmetic and copies ran while one was open for 0% of the time, Pallas kernels for 4%

profile of v1, /device:TPU:0, one launch (start us, length us, event | category | flops | bytes accessed | tf_op | source)
XLA Modules:
  0.0 69.0 jit_solution(5496803246138992870)
XLA Ops:
  0.6 0.7 %bitcast_convert_fusion = f32[8,128]{1,0:T(8,128)S(1)} fusion(s32[1,1,8,128]{3,2,1,0:T(8,128)} %param.18), kind=kLoop, calls=%fused_computation.4 | loop fusion | flops 1024 | bytes 8192 | tf_op jit(solution)/shard_map/convert_element_type | solution.py:582
  1.3 0.7 copy-done.9
  2.0 0.5 collective-permute-start
  2.5 5.1 %collective-permute-start.1 = (f32[12,128]{1,0:T(8,128)S(1)}, f32[12,128]{1,0:T(8,128)S(1)}, u32[]{:S(2)}, u32[]{:S(2)}) collective-permute-start(f32[12,128]{1,0:T(8,128)S(1)} %get-tuple-element.31.own_ref), channel_id=1, source_target_pairs={{2,0},{4,2},{6,4},{8,6},{10,8},{12,10},{14,12},{16,14},{18,16},{20... | collective-permute-start | bytes 18440 | tf_op jit(solution)/shard_map/ppermute | solution.py:533
  7.6 1.3 %collective-permute-done.prev_ref = f32[12,128]{1,0:T(8,128)S(1)} collective-permute-done((f32[12,128]{1,0:T(8,128)S(1)}, f32[12,128]{1,0:T(8,128)S(1)}, u32[]{:S(2)}, u32[]{:S(2)}) %collective-permute-start) | collective-permute-done | bytes 6176 | tf_op jit(solution)/shard_map/ppermute | solution.py:530
  8.9 0.1 collective-permute-done.1.next_ref
  9.0 0.5 copy-done.5
  9.4 0.1 copy-done.6
  9.5 1.9 %collective-permute-start.2 = (f32[3,12,128]{2,1,0:T(8,128)S(1)}, f32[3,12,128]{2,1,0:T(8,128)S(1)}, u32[]{:S(2)}, u32[]{:S(2)}) collective-permute-start(f32[3,12,128]{2,1,0:T(8,128)S(1)} %pad_maximum_fusion), channel_id=1, source_target_pairs={{0,1},{1,0},{2,3},{3,2},{4,5},{5,4},{6,7},{7,6},{8,9},{9,8},{10,11... | collective-permute-start | bytes 55304 | tf_op jit(solution)/shard_map/ppermute | solution.py:530
  11.4 2.0 %collective-permute-done.2.left_ref.right_ref = f32[3,12,128]{2,1,0:T(8,128)S(1)} collective-permute-done((f32[3,12,128]{2,1,0:T(8,128)S(1)}, f32[3,12,128]{2,1,0:T(8,128)S(1)}, u32[]{:S(2)}, u32[]{:S(2)}) %collective-permute-start.2) | collective-permute-done | bytes 18464 | tf_op jit(solution)/shard_map/ppermute | solution.py:530
  13.4 0.6 copy-done.3
  14.0 3.7 %short_forward.1 = (f32[32,8,128]{2,1,0:T(8,128)}, f32[3,64,128]{2,1,0:T(8,128)}, f32[64,128]{1,0:T(8,128)}, f32[128,128]{1,0:T(8,128)}, f32[128,128]{1,0:T(8,128)}) custom-call(f32[12,128]{1,0:T(8,128)} %copy-done.4, f32[12,128]{1,0:T(8,128)} %copy-done.5, f32[12,128]{1,0:T(8,128)} %copy-done.6, f32[3,12,128]{2,1,0:T(8,128)} %copy-done.3, ...), custom_call_target="tpu_custom_call" | custom-call | tf_op jit(solution)/shard_map/short_forward/pallas_call | solution.py:603
  17.7 4.9 %all-to-all-start = ((f32[32,8,128]{2,1,0:T(8,128)}), f32[32,8,128]{2,1,0:T(8,128)S(1)}, u32[]{:S(2)}, u32[]{:S(2)}) async-start(f32[32,8,128]{2,1,0:T(8,128)} %get-tuple-element.15), calls=%async_computation | async-start | bytes 262144 | tf_op jit(solution)/shard_map/all_to_all | solution.py:634
  22.6 2.9 %wave_weights.1 = (f32[4,56,32]{2,1,0:T(8,128)}, f32[8,32]{1,0:T(8,128)}) custom-call(f32[1000,128]{1,0:T(8,128)} %gain_ref.1, s32[3,1000]{1,0:T(4,128)} %waves_ref.1, f32[1,128]{1,0:T(1,128)} %bitcast.26, f32[1,128]{1,0:T(1,128)} %bitcast.27), custom_call_target="tpu_custom_call" | custom-call | flops 43008000 | bytes 512000 | tf_op jit(solution)/shard_map/wave_weights/pallas_call | solution.py:590
  25.5 5.8 %all-to-all-done.recv_ref = f32[32,8,128]{2,1,0:T(8,128)S(1)} async-done(((f32[32,8,128]{2,1,0:T(8,128)}), f32[32,8,128]{2,1,0:T(8,128)S(1)}, u32[]{:S(2)}, u32[]{:S(2)}) %all-to-all-start) | async-done | bytes 131104 | tf_op jit(solution)/shard_map/all_to_all | solution.py:634
  31.2 0.9 %copy-done = f32[4,56,32]{2,1,0:T(8,128)S(1)} copy-done((f32[4,56,32]{2,1,0:T(8,128)S(1)}, f32[4,56,32]{2,1,0:T(8,128)}, u32[]{:S(2)}) %copy-start) | copy-done | bytes 28696
  32.1 0.7 copy-done.2
  32.8 6.9 %waves.1 = (f32[32,8,128]{2,1,0:T(8,128)S(1)}, f32[8,128]{1,0:T(8,128)S(1)}) custom-call(f32[32,8,128]{2,1,0:T(8,128)S(1)} %all-to-all-done.recv_ref, f32[4,56,32]{2,1,0:T(8,128)S(1)} %copy-done, f32[8,32]{1,0:T(8,128)S(1)} %copy-done.2), custom_call_target="tpu_custom_call" | custom-call | tf_op jit(solution)/shard_map/waves/pallas_call | solution.py:636
  39.8 11.0 %all_to_all.15.recv_ref = f32[32,8,128]{2,1,0:T(8,128)} all-to-all(f32[32,8,128]{2,1,0:T(8,128)S(1)} %get-tuple-element.18), channel_id=1, replica_groups=mesh['row'=16,'col'=2] {'row','col'}, dimensions={0} | all-to-all | bytes 262144 | tf_op jit(solution)/shard_map/all_to_all | solution.py:647
  50.8 3.3 %short_back.1 = (f32[32,8,128]{2,1,0:T(8,128)}, f32[8,128]{1,0:T(8,128)}) custom-call(f32[32,8,128]{2,1,0:T(8,128)} %all_to_all.15.recv_ref, f32[3,64,128]{2,1,0:T(8,128)} %get-tuple-element.19.vec_ref, f32[64,128]{1,0:T(8,128)} %get-tuple-element.20.kind_ref, f32[128,128]{1,0:T(8,128)} %get-tuple-element.21.dupd_ref, ...), custom_call_target="tpu_custom_call" | custom-call | tf_op jit(solution)/shard_map/short_back/pallas_call | solution.py:649
  54.1 11.9 %all_to_all.16.recv_ref = f32[32,8,128]{2,1,0:T(8,128)} all-to-all(f32[32,8,128]{2,1,0:T(8,128)} %get-tuple-element.24), channel_id=1, replica_groups=mesh['row'=16,'col'=2] {'row','col'}, dimensions={0} | all-to-all | bytes 262144 | tf_op jit(solution)/shard_map/all_to_all | solution.py:660
  66.0 1.8 %returned_ghosts.1 = (f32[3,128]{1,0:T(4,128)}, f32[3,3]{1,0:T(4,128)}) custom-call(f32[32,8,128]{2,1,0:T(8,128)} %all_to_all.16.recv_ref, f32[8,128]{1,0:T(8,128)} %get-tuple-element.25.own_ref, s32[8,128]{1,0:T(8,128)} %bitcast.21), custom_call_target="tpu_custom_call" | custom-call | tf_op jit(solution)/shard_map/returned_ghosts/pallas_call | solution.py:662
  67.8 0.7 copy-done.7
  68.5 0.6 copy.16
  (17 shorter events, 0.0 us)
Async XLA Ops:
  0.6 0.7 %copy-start.8 = (f32[3,1,1,128]{3,2,1,0:T(1,128)S(1)}, f32[3,1,1,128]{3,2,1,0:T(1,128)}, u32[]{:S(2)}) copy-start(f32[3,1,1,128]{3,2,1,0:T(1,128)} %param.14) | copy-start | bytes 4612
  1.3 0.7 copy-start.9
  2.0 6.9 %copy-start.4 = (f32[12,128]{1,0:T(8,128)}, f32[12,128]{1,0:T(8,128)S(1)}, u32[]{:S(2)}) copy-start(f32[12,128]{1,0:T(8,128)S(1)} %get-tuple-element.31.own_ref) | copy-start | bytes 18436
  2.0 6.8 %collective-permute-start = (f32[12,128]{1,0:T(8,128)S(1)}, f32[12,128]{1,0:T(8,128)S(1)}, u32[]{:S(2)}, u32[]{:S(2)}) collective-permute-start(f32[12,128]{1,0:T(8,128)S(1)} %get-tuple-element.31.own_ref), channel_id=1, source_target_pairs={{0,2},{2,4},{4,6},{6,8},{8,10},{10,12},{12,14},{14,16},{16,18},{18... | collective-permute-start | bytes 18440 | tf_op jit(solution)/shard_map/ppermute | solution.py:530
  2.5 6.4 %collective-permute-start.1 = (f32[12,128]{1,0:T(8,128)S(1)}, f32[12,128]{1,0:T(8,128)S(1)}, u32[]{:S(2)}, u32[]{:S(2)}) collective-permute-start(f32[12,128]{1,0:T(8,128)S(1)} %get-tuple-element.31.own_ref), channel_id=1, source_target_pairs={{2,0},{4,2},{6,4},{8,6},{10,8},{12,10},{14,12},{16,14},{18,16},{20... | collective-permute-start | bytes 18440 | tf_op jit(solution)/shard_map/ppermute | solution.py:533
  8.8 0.6 copy-start.5
  8.9 0.6 copy-start.6
  9.5 3.8 %collective-permute-start.2 = (f32[3,12,128]{2,1,0:T(8,128)S(1)}, f32[3,12,128]{2,1,0:T(8,128)S(1)}, u32[]{:S(2)}, u32[]{:S(2)}) collective-permute-start(f32[3,12,128]{2,1,0:T(8,128)S(1)} %pad_maximum_fusion), channel_id=1, source_target_pairs={{0,1},{1,0},{2,3},{3,2},{4,5},{5,4},{6,7},{7,6},{8,9},{9,8},{10,11... | collective-permute-start | bytes 55304 | tf_op jit(solution)/shard_map/ppermute | solution.py:530
  13.4 0.6 copy-start.3
  17.7 13.6 %all-to-all-start = ((f32[32,8,128]{2,1,0:T(8,128)}), f32[32,8,128]{2,1,0:T(8,128)S(1)}, u32[]{:S(2)}, u32[]{:S(2)}) async-start(f32[32,8,128]{2,1,0:T(8,128)} %get-tuple-element.15), calls=%async_computation | async-start | bytes 262144 | tf_op jit(solution)/shard_map/all_to_all | solution.py:634
  31.2 0.9 %copy-start = (f32[4,56,32]{2,1,0:T(8,128)S(1)}, f32[4,56,32]{2,1,0:T(8,128)}, u32[]{:S(2)}) copy-start(f32[4,56,32]{2,1,0:T(8,128)} %get-tuple-element.16.phi_ref) | copy-start | bytes 86020
  32.1 0.7 copy-start.2
  39.8 11.0 %copy-start.1 = (f32[8,128]{1,0:T(8,128)}, f32[8,128]{1,0:T(8,128)S(1)}, u32[]{:S(2)}) copy-start(f32[8,128]{1,0:T(8,128)S(1)} %get-tuple-element.23.wave_virial_ref) | copy-start | bytes 12292
  67.8 0.7 copy-start.7

commit v2 on v1

v2 whole, which is shorter than its diff:
```python
import functools
import math

import jax
import jax.numpy as jnp
from jax import lax
from jax.experimental import pallas as pl
from jax.experimental.pallas import tpu as pltpu
from jax.sharding import PartitionSpec as P

CELL_EDGE = 12.0
HEIGHT = 36.0
KMAX = 6
HARMONICS = 8
SUBLANES = 8
EXACT = lax.Precision.HIGHEST
GOOD = lax.Precision.HIGH
DIRECTIONS = ((-1, -1), (-1, 0), (-1, 1), (0, -1), (0, 1), (1, -1), (1, 0), (1, 1))
F32 = jnp.float32
BF16 = jnp.bfloat16
AXES = ("row", "col")


def radial_rate(order):
    return 0.003 * 1.6**order


def round_up(value, step):
    return -(-value // step) * step


def direction_slots(row_count, col_count):
    seen = {}
    slots = []
    for row_step, col_step in DIRECTIONS:
        key = (row_step % row_count, col_step % col_count)
        slots.append(seen.get(key, 0))
        seen[key] = slots[-1] + 1
    return slots, max(seen.values())


def dot(lhs, rhs, lhs_dim, rhs_dim, precision=None):
    return lax.dot_general(
        lhs,
        rhs,
        (((lhs_dim,), (rhs_dim,)), ((), ())),
        precision=precision,
        preferred_element_type=F32,
    )


def split(values):
    high = values.astype(BF16).astype(F32)
    return high, values - high


def wave_weights(dims, gain_ref, waves_ref, amp_ref, width_ref, phi_ref, width_out_ref):
    device_count, channel_count, own_channels, lengths, volume = dims
    me = lax.axis_index("row") * lax.axis_size("col") + lax.axis_index("col")
    wave_count = gain_ref.shape[0]
    rows = (KMAX + 1) * HARMONICS
    lanes = own_channels * HARMONICS
    place = lax.broadcasted_iota(jnp.int32, (8, channel_count), 0) * device_count + me
    chosen = (lax.broadcasted_iota(jnp.int32, (8, channel_count), 1) == place).astype(F32)
    own_gain = dot(chosen, gain_ref[...], 1, 1, EXACT)
    first, second, third = waves_ref[0:1, :], waves_ref[1:2, :], waves_ref[2:3, :]
    sign = jnp.where(first < 0, 2, 0) + jnp.where(second < 0, 1, 0)
    key = sign * rows + jnp.abs(first) * HARMONICS + jnp.abs(second)
    spots = lax.broadcasted_iota(jnp.int32, (4 * rows, wave_count), 0) == key
    onehot = jnp.where(spots, 1.0, 0.0).astype(BF16)
    heights = lax.broadcasted_iota(jnp.int32, (HARMONICS, wave_count), 0) + 1 == third
    blocks = [
        jnp.where(heights, own_gain[q : q + 1, :], 0.0) for q in range(own_channels)
    ]
    wide = jnp.concatenate(blocks, axis=0)
    high = wide.astype(BF16)
    rest = wide - high.astype(F32)
    middle = rest.astype(BF16)
    low = (rest - middle.astype(F32)).astype(BF16)
    summed = dot(onehot, high, 1, 1) + (dot(onehot, middle, 1, 1) + dot(onehot, low, 1, 1))
    lane = lax.broadcasted_iota(jnp.int32, (8, channel_count), 1)
    wanted = jnp.minimum((lane // HARMONICS) * device_count + me, channel_count - 1)
    amp = jnp.take_along_axis(jnp.broadcast_to(amp_ref[...], (8, channel_count)), wanted, axis=1)
    width = jnp.take_along_axis(
        jnp.broadcast_to(width_ref[...], (8, channel_count)), wanted, axis=1
    )
    amp, width = amp[0:1, :lanes], width[0:1, :lanes]
    k1, k2, k3 = grid_numbers(rows, lanes, lengths)
    squared = k1 * k1 + k2 * k2 + k3 * k3
    base = amp * jnp.exp(-width * squared) * (1.0 / volume)
    for sign_id in range(4):
        phi_ref[sign_id] = base * summed[sign_id * rows : (sign_id + 1) * rows, :]
    width_out_ref[...] = jnp.broadcast_to(width, (8, lanes))


def grid_numbers(rows, lanes, lengths):
    row_id = lax.broadcasted_iota(jnp.int32, (rows, lanes), 0)
    lane_id = lax.broadcasted_iota(jnp.int32, (rows, lanes), 1)
    k1 = (row_id // HARMONICS).astype(F32) * (2.0 * math.pi / lengths[0])
    k2 = (row_id % HARMONICS).astype(F32) * (2.0 * math.pi / lengths[1])
    k3 = (lane_id % HARMONICS + 1).astype(F32) * (2.0 * math.pi / lengths[2])
    return k1, k2, k3


def neighbour_of(step, row_count, col_count):
    row = lax.rem(lax.axis_index("row") + step[0] + row_count, row_count)
    col = lax.rem(lax.axis_index("col") + step[1] + col_count, col_count)
    return row * col_count + col


def pack_kernel(counts, positions_ref, species_ref, ghosts_ref, send_ref, kinds_ref, positions, species, ghosts, sems):
    row_count, col_count = counts
    fetch(((positions_ref, positions), (species_ref, species), (ghosts_ref, ghosts)), sems)
    device_count, _, atom_count = send_ref.shape
    slots, _ = direction_slots(row_count, col_count)
    kinds = species[...].astype(F32)
    kinds_ref[...] = kinds
    for part in range(3):
        send_ref[:, part, :] = jnp.broadcast_to(positions[part], (device_count, atom_count))
    send_ref[:, 3, :] = jnp.broadcast_to(kinds, (device_count, atom_count))
    for order, step in enumerate(DIRECTIONS):
        target = neighbour_of(step, row_count, col_count)
        send_ref[target, 4 + slots[order], :] = ghosts[order, :].astype(F32)


def fetch(pairs, sems):
    copies = [
        pltpu.make_async_copy(source, target, sems.at[spot])
        for spot, (source, target) in enumerate(pairs)
    ]
    for copy in copies:
        copy.start()
    for copy in copies:
        copy.wait()


def prepare_kernel(dims, kinds_ref, *refs):
    copied = 7
    sources, refs = refs[: copied + 4], refs[copied + 4 :]
    counts_ref, ids_ref, radial_ref, embed_ref, mix_ref, read_ref, out_ref = refs[:copied]
    phi_ref, width_out_ref, pool_ref, back_ref, mix_turned_ref, initial_ref = refs[copied : copied + 6]
    gain, waves, amp, width, weights, kinds8, sems = refs[copied + 6 :]
    fetch(tuple(zip(sources, (*refs[:copied], gain, waves, amp, width))), sems)
    slot_count = ids_ref.shape[0]
    species_count, channel_count = embed_ref.shape
    radial_count = radial_ref.shape[0]
    atom_count = kinds_ref.shape[1]
    mix_turned_ref[...] = mix_ref[...].T
    kinds8[...] = jnp.zeros_like(kinds8)
    kinds8[0:species_count, :] = embed_ref[...]
    own_hot = (
        lax.broadcasted_iota(jnp.int32, (kinds8.shape[0], atom_count), 0).astype(F32) == kinds_ref[...]
    ).astype(F32)
    initial_ref[...] = dot(kinds8[...], own_hot, 0, 0, EXACT)
    rates = [radial_rate(order) for order in range(radial_count)]
    order_id = lax.broadcasted_iota(jnp.int32, (radial_count, channel_count), 0)
    factor = jnp.zeros((radial_count, channel_count), F32)
    for order, rate in enumerate(rates):
        factor = jnp.where(order_id == order, -2.0 * rate / slot_count, factor)
    weights[...] = jnp.zeros_like(weights)
    for k in range(species_count):
        block = radial_ref[...] * embed_ref[k : k + 1, :]
        weights[k * radial_count : (k + 1) * radial_count, :] = block * (1.0 / slot_count)
        back_ref[k * radial_count : (k + 1) * radial_count, :] = block * factor
    turned = weights[...].T
    lane = lax.broadcasted_iota(jnp.int32, turned.shape, 1)
    for tile in range(pool_ref.shape[1] // lane.shape[1]):
        picks = lane // SUBLANES + tile * (lane.shape[1] // SUBLANES)
        pool_ref[:, tile * lane.shape[1] : (tile + 1) * lane.shape[1]] = jnp.take_along_axis(
            turned, picks, axis=1
        )
    wave_weights(dims, gain, waves, amp, width, phi_ref, width_out_ref)


def short_forward_kernel(
    dims,
    cells_ref,
    counts_ref,
    ids_ref,
    pool_ref,
    mix_ref,
    initial_ref,
    send_ref,
    vec_ref,
    kind_ref,
    upd_ref,
    slope_ref,
    table,
    base,
    pooled,
):
    own_channels, row_count, col_count = dims[:3]
    slot_count, atom_count = ids_ref.shape
    species_count, radial_count = dims[3:]
    channel_count = mix_ref.shape[0]
    device_count = send_ref.shape[0]
    slots, _ = direction_slots(row_count, col_count)
    own = cells_ref[neighbour_of((0, 0), row_count, col_count)]
    for order, step in enumerate(DIRECTIONS):
        source = neighbour_of(step, row_count, col_count)
        list_row = 4 + slots[len(DIRECTIONS) - 1 - order]
        block = cells_ref[source]
        base[0, order : order + 1, :] = block[0:1] + step[0] * CELL_EDGE
        base[1, order : order + 1, :] = block[1:2] + step[1] * CELL_EDGE
        base[2, order : order + 1, :] = block[2:3]
        base[3, order : order + 1, :] = block[3:4]
        base[4, order : order + 1, :] = block[list_row : list_row + 1]
    picks = base[4].astype(jnp.int32)
    for part in range(4):
        table[part, 0:1, :] = own[part : part + 1]
        table[part, 8:16, :] = jnp.take_along_axis(base[part], picks, axis=1)

    ids = ids_ref[...]
    lane = ids & (atom_count - 1)
    source = ids // atom_count
    gathered = []
    for part in range(4):
        wide = jnp.broadcast_to(table[part, 0:1, :], ids.shape)
        values = jnp.take_along_axis(wide, lane, axis=1)
        for order in range(len(DIRECTIONS)):
            wide = jnp.broadcast_to(table[part, 8 + order : 9 + order, :], ids.shape)
            values = jnp.where(
                source == order + 1, jnp.take_along_axis(wide, lane, axis=1), values
            )
        gathered.append(values)
    slot = lax.broadcasted_iota(jnp.int32, ids.shape, 0)
    kind = jnp.where(slot < counts_ref[...], gathered[3], -1.0)
    kind_ref[...] = kind
    squared = jnp.zeros(ids.shape, F32)
    for part in range(3):
        vector = gathered[part] - own[part : part + 1]
        vec_ref[part] = vector
        squared = squared + vector * vector
    masks = [kind == float(k) for k in range(species_count)]
    for order in range(radial_count):
        basis = jnp.exp(squared * (-radial_rate(order)))
        for k in range(species_count):
            spot = (k * radial_count + order) * SUBLANES
            chosen = jnp.where(masks[k], basis, 0.0)
            pooled[spot : spot + SUBLANES, :] = jnp.sum(
                chosen.reshape(slot_count // SUBLANES, SUBLANES, atom_count), axis=0
            )
    aggregate = dot(pool_ref[...], pooled[...], 1, 0, GOOD)
    before = dot(mix_ref[...], aggregate, 1, 0, GOOD)
    gate = 1.0 / (1.0 + jnp.exp(-before))
    updated = initial_ref[...] + before * gate
    slope_ref[...] = gate + before * gate * (1.0 - gate)
    for q in range(own_channels):
        low, high = q * device_count, min(channel_count, (q + 1) * device_count)
        send_ref[0 : high - low, q, :] = updated[low:high, :]
        if high - low < device_count:
            send_ref[high - low :, q, :] = jnp.zeros(
                (device_count - (high - low), atom_count), F32
            )
    upd_ref[...] = updated


def readout_kernel(upd_ref, read_ref, out_ref, dupd_ref):
    channel_count, atom_count = upd_ref.shape
    readout = dot(read_ref[...], upd_ref[...], 0, 0, GOOD)
    gate = 1.0 / (1.0 + jnp.exp(-readout))
    scale = jnp.broadcast_to(out_ref[...], (channel_count, channel_count)).T
    dread = scale[:, 0:atom_count] * (gate + readout * gate * (1.0 - gate))
    dupd_ref[...] = dot(read_ref[...], dread, 1, 0, GOOD)


def turn_tables(turns, multiples):
    angle = turns * multiples
    halves = jnp.floor(2.0 * angle + 0.5)
    rest = angle - 0.5 * halves
    sign = 1.0 - 2.0 * (halves - 2.0 * jnp.floor(0.5 * halves))
    square = rest * rest

    def series(first, last):
        terms = [
            (-1.0) ** (p // 2) * (2.0 * math.pi) ** p / math.factorial(p)
            for p in range(first, last + 1, 2)
        ]
        total = jnp.full_like(square, terms[-1])
        for term in reversed(terms[:-1]):
            total = total * square + term
        return total

    return sign * series(0, 12), sign * rest * series(1, 13)


def table_kernel(dims, cells_ref, axes_ref):
    col_count, chunk_count, lengths = dims
    chunk, _, atom_count = cells_ref.shape
    first_device = pl.program_id(0) * chunk if chunk_count > 1 else 0
    multiples = lax.broadcasted_iota(jnp.int32, (HARMONICS, atom_count), 0).astype(F32)

    def one(index, _):
        device = first_device + index
        spot = pl.ds(pl.multiple_of(index * atom_count, atom_count), atom_count)
        block = cells_ref[index]
        corner_row = (device // col_count).astype(F32) * CELL_EDGE
        corner_col = (device % col_count).astype(F32) * CELL_EDGE
        turns = (
            (block[0:1] + corner_row) * (1.0 / lengths[0]),
            (block[1:2] + corner_col) * (1.0 / lengths[1]),
            block[2:3] * (1.0 / lengths[2]),
        )
        for axis in range(3):
            numbers = multiples + 1.0 if axis == 2 else multiples
            cos, sin = turn_tables(turns[axis], numbers)
            axes_ref[2 * axis, :, spot] = cos
            axes_ref[2 * axis + 1, :, spot] = sin
        return 0

    lax.fori_loop(0, chunk, one, 0, unroll=4)


def wave_kernel(
    dims,
    recv_ref,
    axes_ref,
    phi_ref,
    width_ref,
    send_ref,
    virial_ref,
    high,
    low,
    lifted,
    sums,
    coefficients,
):
    own_channels, chunk_count, lengths = dims
    planes = (high, low, axes_ref, lifted)
    if chunk_count == 1:
        sums[...] = wave_sums(own_channels, recv_ref, *planes)
        wave_coefficients(lengths, sums, phi_ref, width_ref, virial_ref, coefficients)
        wave_back(own_channels, lengths, *planes, coefficients, send_ref)
        return
    phase, chunk_id = pl.program_id(0), pl.program_id(1)

    @pl.when((phase == 0) & (chunk_id == 0))
    def _():
        sums[...] = jnp.zeros_like(sums)

    part = wave_sums(own_channels, recv_ref, *planes)

    @pl.when(phase == 0)
    def _():
        sums[...] += part

    @pl.when((phase == 1) & (chunk_id == 0))
    def _():
        wave_coefficients(lengths, sums, phi_ref, width_ref, virial_ref, coefficients)

    @pl.when(phase == 1)
    def _():
        wave_back(own_channels, lengths, *planes, coefficients, send_ref)


def wave_sums(own_channels, recv_ref, high_ref, low_ref, axes_ref, lifted):
    chunk, _, atom_count = recv_ref.shape
    lanes = own_channels * HARMONICS
    group = math.gcd(chunk, 8)
    total = 0.0
    for first in range(0, chunk, group):
        for index in range(first, first + group):
            spot = slice(index * atom_count, (index + 1) * atom_count)
            for q in range(own_channels):
                feature = recv_ref[index, q : q + 1, :]
                for part in range(2):
                    row = part * lanes + q * HARMONICS
                    lifted[row : row + HARMONICS, spot] = feature * axes_ref[4 + part, :, spot]
            products = [
                axes_ref[first_axis, m : m + 1, spot] * axes_ref[second_axis, :, spot]
                for first_axis, second_axis in ((0, 2), (0, 3), (1, 2), (1, 3))
                for m in range(KMAX + 1)
            ]
            for pair in range(len(products) // 2):
                both = jnp.concatenate(products[2 * pair : 2 * pair + 2], axis=0)
                high = both.astype(BF16)
                rows = slice(2 * HARMONICS * pair, 2 * HARMONICS * (pair + 1))
                high_ref[rows, spot] = high
                low_ref[rows, spot] = (both - high.astype(F32)).astype(BF16)
        spot = slice(first * atom_count, (first + group) * atom_count)
        values = lifted[:, spot]
        high = values.astype(BF16)
        low = (values - high.astype(F32)).astype(BF16)
        main = dot(high_ref[:, spot], jnp.concatenate([high, low], axis=0), 1, 1)
        total = total + main[:, : 2 * lanes] + (main[:, 2 * lanes :] + dot(low_ref[:, spot], high, 1, 1))
    return total


def wave_coefficients(lengths, sums_ref, phi_ref, width_ref, virial_ref, coefficients_ref):
    _, rows, lanes = phi_ref.shape
    sums = sums_ref[...]
    cos_part, sin_part = sums[:, :lanes], sums[:, lanes:]
    blocks = [(cos_part[p * rows : (p + 1) * rows], sin_part[p * rows : (p + 1) * rows]) for p in range(4)]
    (cc_c, cc_s), (cs_c, cs_s), (sc_c, sc_s), (ss_c, ss_s) = blocks
    zero = jnp.zeros((rows, lanes), F32)
    d_cc_c = d_cc_s = d_cs_c = d_cs_s = d_sc_c = d_sc_s = d_ss_c = d_ss_s = zero
    total = even = first_odd = second_odd = both_odd = zero
    for sign_id, (s1, s2) in enumerate(((1.0, 1.0), (1.0, -1.0), (-1.0, 1.0), (-1.0, -1.0))):
        real = cc_c - s1 * s2 * ss_c - s1 * sc_s - s2 * cs_s
        imag = cc_s - s1 * s2 * ss_s + s1 * sc_c + s2 * cs_c
        phi = phi_ref[sign_id]
        dreal, dimag = phi * real, phi * imag
        power = dreal * real + dimag * imag
        d_cc_c, d_ss_c = d_cc_c + dreal, d_ss_c - s1 * s2 * dreal
        d_sc_s, d_cs_s = d_sc_s - s1 * dreal, d_cs_s - s2 * dreal
        d_cc_s, d_ss_s = d_cc_s + dimag, d_ss_s - s1 * s2 * dimag
        d_sc_c, d_cs_c = d_sc_c + s1 * dimag, d_cs_c + s2 * dimag
        even = even + power
        first_odd = first_odd + s1 * power
        second_odd = second_odd + s2 * power
        both_odd = both_odd + s1 * s2 * power
    width = width_ref[0:1, :]
    k1, k2, k3 = grid_numbers(rows, lanes, lengths)

    def total_of(values):
        return jnp.sum(jnp.sum(values, axis=0, keepdims=True), axis=1, keepdims=True)

    energy = 0.5 * total_of(even)
    scaled = width * even
    terms = {
        (0, 0): energy - total_of(k1 * k1 * scaled),
        (1, 1): energy - total_of(k2 * k2 * scaled),
        (2, 2): energy - total_of(k3 * k3 * scaled),
        (0, 1): -total_of(k1 * k2 * width * both_odd),
        (0, 2): -total_of(k1 * k3 * width * first_odd),
        (1, 2): -total_of(k2 * k3 * width * second_odd),
    }
    virial_ref[...] = virial_row(terms, virial_ref.shape)

    values = jnp.concatenate(
        [
            jnp.concatenate(pair, axis=1)
            for pair in ((d_cc_c, d_cc_s), (d_cs_c, d_cs_s), (d_sc_c, d_sc_s), (d_ss_c, d_ss_s))
        ],
        axis=0,
    )
    cc, cs, sc, ss = (values[p * rows : (p + 1) * rows] for p in range(4))
    row_id = lax.broadcasted_iota(jnp.int32, (rows, 2 * lanes), 0)
    m1 = (row_id // HARMONICS).astype(F32)
    m2 = (row_id % HARMONICS).astype(F32)
    along_x = jnp.concatenate([m1 * sc, m1 * ss, -m1 * cc, -m1 * cs], axis=0)
    along_y = jnp.concatenate([m2 * cs, -m2 * cc, m2 * ss, -m2 * sc], axis=0)
    stacked = jnp.concatenate([values, along_x, along_y], axis=1).T
    high = stacked.astype(BF16)
    coefficients_ref[0 : 6 * lanes, :] = high
    coefficients_ref[6 * lanes :, :] = (stacked - high.astype(F32)).astype(BF16)


def wave_back(own_channels, lengths, high_ref, low_ref, axes_ref, lifted, coefficients, send_ref):
    chunk, _, atom_count = send_ref.shape
    lanes = own_channels * HARMONICS
    numbers = lax.broadcasted_iota(jnp.int32, (HARMONICS, atom_count), 0).astype(F32) + 1.0
    values = coefficients[...]
    main = dot(values, high_ref[...], 1, 0)
    result = main[: 6 * lanes] + (main[6 * lanes :] + dot(values[: 6 * lanes], low_ref[...], 1, 0))
    for index in range(chunk):
        low, high = index * atom_count, (index + 1) * atom_count
        cos_z, sin_z = axes_ref[4, :, low:high], axes_ref[5, :, low:high]
        part = result[:, low:high]
        grad_x = jnp.zeros((HARMONICS, atom_count), F32)
        grad_y = grad_x
        grad_z = grad_x
        pieces = []
        for q in range(own_channels):
            a, b = q * HARMONICS, lanes + q * HARMONICS
            on_cos, on_sin = part[a : a + HARMONICS], part[b : b + HARMONICS]
            pieces.append(on_cos * cos_z + on_sin * sin_z)
            lift_cos = lifted[a : a + HARMONICS, low:high]
            lift_sin = lifted[b : b + HARMONICS, low:high]
            grad_z = grad_z + on_sin * lift_cos - on_cos * lift_sin
            a, b = a + 2 * lanes, b + 2 * lanes
            grad_x = grad_x + part[a : a + HARMONICS] * lift_cos + part[b : b + HARMONICS] * lift_sin
            a, b = a + 2 * lanes, b + 2 * lanes
            grad_y = grad_y + part[a : a + HARMONICS] * lift_cos + part[b : b + HARMONICS] * lift_sin
        pieces.append(grad_x * (2.0 * math.pi / lengths[0]))
        pieces.append(grad_y * (2.0 * math.pi / lengths[1]))
        pieces.append(grad_z * numbers * (2.0 * math.pi / lengths[2]))
        for spot, piece in enumerate(pieces):
            send_ref[index, spot : spot + 1, :] = jnp.sum(piece, axis=0, keepdims=True)


def virial_row(terms, shape):
    lane = lax.broadcasted_iota(jnp.int32, shape, 1)
    row = jnp.zeros(shape, F32)
    for (i, j), value in terms.items():
        spots = (lane == 3 * i + j) | (lane == 3 * j + i)
        row = jnp.where(spots, value, row)
    return row


def short_back_kernel(
    dims,
    recv_ref,
    vec_ref,
    kind_ref,
    dupd_ref,
    slope_ref,
    ids_ref,
    back_ref,
    mix_ref,
    wave_virial_ref,
    send_ref,
    own_ref,
    fgrad,
    dpool,
    parts,
):
    own_channels, row_count, col_count, species_count, radial_count = dims
    slot_count, atom_count = ids_ref.shape
    channel_count = mix_ref.shape[0]
    device_count = send_ref.shape[0]
    table_rows = round_up(len(DIRECTIONS) + 1, 16)
    for q in range(own_channels):
        low, high = q * device_count, min(channel_count, (q + 1) * device_count)
        fgrad[low:high, :] = recv_ref[0 : high - low, q, :]
    total = jnp.sum(recv_ref[...], axis=0)
    dbefore = (fgrad[...] + dupd_ref[...]) * slope_ref[...]
    daggregate = dot(mix_ref[...], dbefore, 1, 0, GOOD)
    dpool[...] = dot(back_ref[...], daggregate, 1, 0, GOOD)
    vectors = [vec_ref[part] for part in range(3)]
    squared = vectors[0] * vectors[0] + vectors[1] * vectors[1] + vectors[2] * vectors[2]
    kind = kind_ref[...]
    sums = [jnp.zeros(kind.shape, F32) for _ in range(species_count)]
    for order in range(radial_count):
        basis = jnp.exp(squared * (-radial_rate(order)))
        for k in range(species_count):
            spot = k * radial_count + order
            sums[k] = sums[k] + basis * dpool[spot : spot + 1, :]
    slope = jnp.zeros(kind.shape, F32)
    for k in range(species_count):
        slope = jnp.where(kind == float(k), sums[k], slope)
    grads = [slope * vector for vector in vectors]

    def total_of(values):
        return jnp.sum(jnp.sum(values, axis=0, keepdims=True), axis=1, keepdims=True)

    terms = {
        (i, j): -total_of(grads[i] * vectors[j]) for i in range(3) for j in range(i, 3)
    }
    virial = virial_row(terms, (1, atom_count)) + wave_virial_ref[0:1, :]
    for part in range(3):
        parts[2 * part], parts[2 * part + 1] = split(grads[part])

    sublane = lax.broadcasted_iota(jnp.int32, (atom_count, atom_count), 0)
    table_id = lax.broadcasted_iota(jnp.int32, (table_rows, atom_count), 0)
    group = 8
    scattered = jnp.zeros((atom_count, 6 * table_rows), F32)
    for low in range(0, slot_count, group):
        hots, columns = [], []
        for s in range(low, low + group):
            ids = ids_ref[s : s + 1, :]
            hots.append(jnp.where(sublane == (ids & (atom_count - 1)), 1.0, 0.0).astype(BF16))
            mine = table_id == ids // atom_count
            columns.append(
                jnp.concatenate(
                    [
                        jnp.where(mine, parts[p, s : s + 1, :], 0.0).astype(BF16)
                        for p in range(6)
                    ],
                    axis=0,
                )
            )
        scattered = scattered + dot(
            jnp.concatenate(hots, axis=1), jnp.concatenate(columns, axis=1), 1, 1
        )
    rows = scattered.T
    slots, _ = direction_slots(row_count, col_count)
    send_ref[...] = jnp.zeros_like(send_ref)
    send_ref[:, 0, :] = jnp.broadcast_to(virial, (device_count, atom_count))
    own_ref[...] = jnp.zeros_like(own_ref)
    for part in range(3):
        low = 2 * part * table_rows
        both = rows[low : low + table_rows] + rows[low + table_rows : low + 2 * table_rows]
        own_ref[part : part + 1, :] = (
            both[0:1, :]
            - jnp.sum(grads[part], axis=0, keepdims=True)
            + total[own_channels + part : own_channels + part + 1, :]
        )
        for order, step in enumerate(DIRECTIONS):
            target = neighbour_of(step, row_count, col_count)
            send_ref[target, 1 + 3 * slots[order] + part, :] = both[1 + order, :]


def final_kernel(dims, recv_ref, own_ref, ghost_ref, forces_ref, virial_ref, parts):
    row_count, col_count, volume = dims
    atom_count = own_ref.shape[1]
    slots, _ = direction_slots(row_count, col_count)
    sublane = lax.broadcasted_iota(jnp.int32, (atom_count, ghost_ref.shape[1]), 0)
    hots = []
    parts[...] = jnp.zeros_like(parts)
    for order, step in enumerate(DIRECTIONS):
        source = neighbour_of((-step[0], -step[1]), row_count, col_count)
        opposite = len(DIRECTIONS) - 1 - order
        hots.append(
            jnp.where(sublane == ghost_ref[opposite : opposite + 1, :], 1.0, 0.0).astype(BF16)
        )
        low, high = order * ghost_ref.shape[1], (order + 1) * ghost_ref.shape[1]
        for part in range(3):
            row = recv_ref[source, 1 + 3 * slots[order] + part, :].reshape(1, -1)
            parts[2 * part : 2 * part + 1, low:high], parts[2 * part + 1 : 2 * part + 2, low:high] = split(row)
    returned = dot(jnp.concatenate(hots, axis=1), parts[...].astype(BF16), 1, 1).T
    for part in range(3):
        forces_ref[part] = -(
            own_ref[part : part + 1, :]
            + (returned[2 * part : 2 * part + 1, :] + returned[2 * part + 1 : 2 * part + 2, :])
        )
    virial = jnp.sum(recv_ref[:, 0, :], axis=0, keepdims=True) * (1.0 / volume)
    for i in range(3):
        virial_ref[i : i + 1, :] = virial[:, 3 * i : 3 * i + 3]


def per_device(
    positions,
    species,
    counts,
    neighbours,
    ghost_index,
    wave_numbers,
    embedding,
    w_radial,
    w_mix,
    w_read,
    w_out,
    amplitude,
    kernel_width,
    filter_gain,
):
    row_count = lax.axis_size("row")
    col_count = lax.axis_size("col")
    device_count = row_count * col_count
    atom_count = positions.shape[3]
    slot_count = neighbours.shape[2]
    direction_count, ghost_count = ghost_index.shape[2:]
    species_count, channel_count = embedding.shape
    radial_count = w_radial.shape[0]
    own_channels = -(-channel_count // device_count)
    lengths = (CELL_EDGE * row_count, CELL_EDGE * col_count, HEIGHT)
    volume = lengths[0] * lengths[1] * lengths[2]
    rows = (KMAX + 1) * HARMONICS
    lanes = own_channels * HARMONICS
    slab = round_up(own_channels + 3, 8)
    _, shared = direction_slots(row_count, col_count)
    slab_back = round_up(1 + 3 * shared, 8)
    slab_first = round_up(4 + shared, 8)
    slab_features = round_up(own_channels, 4)
    chunk = math.gcd(device_count, 32)
    chunk_count = device_count // chunk

    def exchange(slabs):
        return lax.all_to_all(slabs, AXES, 0, 0, tiled=True)

    def shape(*dims):
        return jax.ShapeDtypeStruct(dims, F32)

    def scratch(*dims):
        return pltpu.VMEM(dims, F32)

    def call(kernel, out_shape, vmem=16, **options):
        return pl.pallas_call(
            kernel,
            out_shape=out_shape,
            compiler_params=pltpu.CompilerParams(vmem_limit_bytes=vmem * 1024 * 1024),
            **options,
        )

    ids = neighbours.reshape(slot_count, atom_count)
    ghosts = ghost_index.reshape(direction_count, ghost_count)
    mesh_counts = (row_count, col_count)
    def fetched(*arrays):
        return [pltpu.with_memory_space_constraint(x, pltpu.HBM) for x in arrays]

    kept = pl.BlockSpec(memory_space=pltpu.HBM)
    near = pl.BlockSpec(memory_space=pltpu.VMEM)
    send, own_kinds = call(
        functools.partial(pack_kernel, mesh_counts),
        (shape(device_count, slab_first, atom_count), shape(1, atom_count)),
        in_specs=[kept] * 3,
        scratch_shapes=[
            scratch(3, 1, atom_count),
            pltpu.VMEM((1, atom_count), jnp.int32),
            pltpu.VMEM(ghosts.shape, jnp.int32),
            pltpu.SemaphoreType.DMA((3,)),
        ],
        name="pack",
    )(*fetched(positions.reshape(3, 1, atom_count), species.reshape(1, atom_count), ghosts))
    cells = exchange(send)

    short_inputs = (
        counts.reshape(1, atom_count),
        ids,
        w_radial,
        embedding,
        w_mix,
        w_read,
        w_out.reshape(1, -1),
    )
    wave_inputs = (filter_gain, wave_numbers, amplitude.reshape(1, -1), kernel_width.reshape(1, -1))
    pooled_rows = species_count * radial_count
    live, ids, _, _, w_mix, w_read, w_out, phi, width, pool, back, mix_turned, initial = call(
        functools.partial(
            prepare_kernel, (device_count, channel_count, own_channels, lengths, volume)
        ),
        tuple(jax.ShapeDtypeStruct(x.shape, x.dtype) for x in short_inputs)
        + (
            shape(4, rows, lanes),
            shape(8, lanes),
            shape(channel_count, round_up(pooled_rows * SUBLANES, channel_count)),
            shape(pooled_rows, channel_count),
            shape(channel_count, channel_count),
            shape(channel_count, atom_count),
        ),
        in_specs=[near] + [kept] * (len(short_inputs) + len(wave_inputs)),
        scratch_shapes=[pltpu.VMEM(x.shape, x.dtype) for x in wave_inputs]
        + [
            scratch(round_up(pooled_rows, 128), channel_count),
            scratch(round_up(species_count, 8), channel_count),
            pltpu.SemaphoreType.DMA((len(short_inputs) + len(wave_inputs),)),
        ],
        cost_estimate=pl.CostEstimate(
            flops=2 * 4 * rows * filter_gain.shape[0] * 3 * lanes,
            bytes_accessed=4 * filter_gain.size,
            transcendentals=0,
        ),
        name="prepare",
    )(own_kinds, *fetched(*short_inputs, *wave_inputs))

    send, vectors, kinds, updated, slope = call(
        functools.partial(
            short_forward_kernel, (own_channels,) + mesh_counts + (species_count, radial_count)
        ),
        (
            shape(device_count, slab_features, atom_count),
            shape(3, slot_count, atom_count),
            shape(slot_count, atom_count),
            shape(channel_count, atom_count),
            shape(channel_count, atom_count),
        ),
        scratch_shapes=[
            scratch(4, 16, atom_count),
            scratch(5, direction_count, atom_count),
            scratch(pooled_rows * SUBLANES, atom_count),
        ],
        name="short_forward",
    )(cells, live, ids, pool, mix_turned, initial)
    send, cells, updated = lax.optimization_barrier((send, cells, updated))
    features = exchange(send)

    axes_block = (6, HARMONICS, chunk * atom_count)
    if chunk_count == 1:
        table_options = {}
    else:
        table_options = dict(
            grid=(chunk_count,),
            in_specs=[pl.BlockSpec((chunk, slab_first, atom_count), lambda i: (i, 0, 0))],
            out_specs=pl.BlockSpec(axes_block, lambda i: (0, 0, i)),
        )
    axes = call(
        functools.partial(table_kernel, (col_count, chunk_count, lengths)),
        shape(6, HARMONICS, device_count * atom_count),
        cost_estimate=pl.CostEstimate(
            flops=2000 * device_count * atom_count, bytes_accessed=200 * device_count * atom_count, transcendentals=0
        ),
        name="tables",
        **table_options,
    )(cells)
    dupd = call(readout_kernel, shape(channel_count, atom_count), name="readout")(
        updated, w_read, w_out
    )

    wave = functools.partial(wave_kernel, (own_channels, chunk_count, lengths))
    wave_shapes = (shape(device_count, slab, atom_count), shape(8, atom_count))
    wave_scratch = [
        pltpu.VMEM((4 * rows, chunk * atom_count), BF16),
        pltpu.VMEM((4 * rows, chunk * atom_count), BF16),
        scratch(2 * lanes, chunk * atom_count),
        scratch(4 * rows, 2 * lanes),
        pltpu.VMEM((12 * lanes, 4 * rows), BF16),
    ]
    if chunk_count == 1:
        wave_options = {}
    else:
        wave_options = dict(
            grid=(2, chunk_count),
            in_specs=[
                pl.BlockSpec((chunk, slab_features, atom_count), lambda p, i: (i, 0, 0)),
                pl.BlockSpec(axes_block, lambda p, i: (0, 0, i)),
                pl.BlockSpec((4, rows, lanes), lambda p, i: (0, 0, 0)),
                pl.BlockSpec((8, lanes), lambda p, i: (0, 0)),
            ],
            out_specs=(
                pl.BlockSpec((chunk, slab, atom_count), lambda p, i: (i * p, 0, 0)),
                pl.BlockSpec((8, atom_count), lambda p, i: (0, 0)),
            ),
        )
    send, wave_virial = call(
        wave, wave_shapes, vmem=20, scratch_shapes=wave_scratch, name="waves", **wave_options
    )(features, axes, phi, width)
    gradients = exchange(send)

    send, own = call(
        functools.partial(
            short_back_kernel, (own_channels,) + mesh_counts + (species_count, radial_count)
        ),
        out_shape=(shape(device_count, slab_back, atom_count), shape(8, atom_count)),
        scratch_shapes=[
            scratch(channel_count, atom_count),
            scratch(pooled_rows, atom_count),
            scratch(6, slot_count, atom_count),
        ],
        name="short_back",
    )(gradients, vectors, kinds, dupd, slope, ids, back, w_mix, wave_virial)
    returned = exchange(send)

    forces, virial = call(
        functools.partial(final_kernel, (row_count, col_count, volume)),
        out_shape=(shape(3, 1, atom_count), shape(3, 3)),
        scratch_shapes=[scratch(16, direction_count * ghost_count)],
        name="returned_ghosts",
    )(returned, own, ghosts)
    return (forces[:, None], virial)


def solution(mesh):
    return jax.shard_map(
        per_device,
        mesh=mesh,
        in_specs=(
            P(None, "row", "col", None),
            P("row", "col", None),
            P("row", "col", None),
            P("row", "col", None, None),
            P("row", "col", None, None),
            P(),
            P(),
            P(),
            P(),
            P(),
            P(),
            P(),
            P(),
            P(),
        ),
        out_specs=(P(None, "row", "col", None), P()),
        check_vma=False,
    )
```

time: 69.5 us -> 58.8 us (0.85)
  blocking collectives: 22.9 us -> 10.3 us
  waiting for transfers between devices: 9.08 us -> 20.6 us
  local copies, waits for them, and re-layouts: 4.68 us -> 0.01 us
  Pallas kernels: 18.6 us -> 14.5 us
  other arithmetic: 0.72 us -> 0 us
    all_to_all x1 -> x3, waiting for transfers between devices: 5.76 us -> 20.6 us  [exchange(): return lax.all_to_all(slabs, AXES, 0, 0, tiled=True)]
    all_to_all x2 -> x1, blocking collectives: 22.9 us -> 10.3 us  [exchange(): return lax.all_to_all(slabs, AXES, 0, 0, tiled=True)]
    all_to_all x1 -> x3, starting transfers between devices: 4.93 us -> 12.4 us  [exchange(): return lax.all_to_all(slabs, AXES, 0, 0, tiled=True)]
    ppermute x3 -> x0, starting transfers between devices: 7.43 us -> none  [the longest x1 5.06 us: sides(): lax.ppermute(block, axis, [((i + 1) % count, i) for i in range(count)])]
    unnamed x22 -> x2, local copies, waits for them, and re-layouts: 4.68 us -> 0.01 us
    pallas_call x5 -> x8, Pallas kernels: 18.6 us -> 14.5 us  [the longest x1 4.35 us: per_device(): call(wave, wave_shapes, vmem=20, scratch_shapes=wave_scratch, name='waves...]
    ppermute x3 -> x0, waiting for transfers between devices: 3.32 us -> none  [the longest x2 3.23 us: sides(): lax.ppermute(block, axis, [(i, (i + 1) % count) for i in range(count)])]
    convert_element_type x2 -> x0, other arithmetic: 0.7 us -> none  [the longest x1 0.7 us: per_device(): ghosts.astype(F32)]
  transfers between devices with their start and end apart: 4 -> 3, of which waited for: 4 -> 3; matrix products, arithmetic and copies ran while one was open for 0% -> 0% of each run, Pallas kernels for 4% -> 7%
where the time goes in v2:
time: 58.8 us; the launch traced here: 58.5 us
  waiting for transfers between devices  20.6 us (35%)
  Pallas kernels  14.5 us (25%)
  starting transfers between devices  12.4 us (21%)
  blocking collectives  10.3 us (18%)
  between operations  0.7 us (1%)
    all_to_all x3, waiting for transfers between devices, exchange(): return lax.all_to_all(slabs, AXES, 0, 0, tiled=True)  20.6 us
    all_to_all x3, starting transfers between devices, exchange(): return lax.all_to_all(slabs, AXES, 0, 0, tiled=True)  12.4 us
    all_to_all x1, blocking collectives, exchange(): return lax.all_to_all(slabs, AXES, 0, 0, tiled=True)  10.3 us
    pallas_call x1, Pallas kernels, per_device(): call(wave, wave_shapes, vmem=20, scratch_shapes=wave_scratch, name='waves...  4.35 us
    pallas_call x1, Pallas kernels, per_device(): call(functools.partial(prepare_kernel, (device_count, channel_count, own_...  3.19 us
    pallas_call x1, Pallas kernels, per_device(): call(functools.partial(short_forward_kernel, (own_channels,) + mesh_count...  2.12 us
    pallas_call x1, Pallas kernels, per_device(): call(functools.partial(pack_kernel, mesh_counts), (shape(device_count, sl...  1.44 us
    pallas_call x1, Pallas kernels, per_device(): call(functools.partial(short_back_kernel, (own_channels,) + mesh_counts +...  1.42 us
  transfers between devices with their start and end apart: 3, of which 3 were waited for; matrix products, arithmetic and copies ran while one was open for 0% of the time, Pallas kernels for 7%

profile of v2, /device:TPU:0, one launch (start us, length us, event | category | flops | bytes accessed | tf_op | source)
XLA Modules:
  0.0 58.5 jit_solution(5667812827465348900)
XLA Ops:
  0.6 1.4 %pack.1 = (f32[32,8,128]{2,1,0:T(8,128)}, f32[1,128]{1,0:T(1,128)S(1)}) custom-call(f32[3,1,128]{2,1,0:T(1,128)} %bitcast.14, s32[1,128]{1,0:T(1,128)} %bitcast.19, s32[8,128]{1,0:T(8,128)} %bitcast.11), custom_call_target="tpu_custom_call" | custom-call | tf_op jit(solution)/shard_map/pack/pallas_call | solution.py:674
  2.1 7.3 %all-to-all-start = ((f32[32,8,128]{2,1,0:T(8,128)}), f32[32,8,128]{2,1,0:T(8,128)S(1)}, u32[]{:S(2)}, u32[]{:S(2)}) async-start(f32[32,8,128]{2,1,0:T(8,128)} %get-tuple-element.29), calls=%async_computation | async-start | bytes 262144 | tf_op jit(solution)/shard_map/all_to_all | solution.py:650
  9.4 3.2 %prepare.1 = (s32[1,128]{1,0:T(1,128)S(1)}, s32[64,128]{1,0:T(8,128)S(1)}, f32[16,128]{1,0:T(8,128)}, f32[6,128]{1,0:T(8,128)}, f32[128,128]{1,0:T(8,128)S(1)}, ...) custom-call(f32[1,128]{1,0:T(1,128)S(1)} %get-tuple-element.30.kinds, ...), custom_call_target="tpu_custom_call" | custom-call | flops 43008000 | bytes 512000 | tf_op jit(solution)/shard_map/prepare/pallas_call | solution.py:699
  12.6 5.4 %all-to-all-done.cells_ref = f32[32,8,128]{2,1,0:T(8,128)S(1)} async-done(((f32[32,8,128]{2,1,0:T(8,128)}), f32[32,8,128]{2,1,0:T(8,128)S(1)}, u32[]{:S(2)}, u32[]{:S(2)}) %all-to-all-start) | async-done | bytes 131104 | tf_op jit(solution)/shard_map/all_to_all | solution.py:650
  18.0 2.1 %short_forward.1 = (f32[32,4,128]{2,1,0:T(4,128)}, f32[3,64,128]{2,1,0:T(8,128)S(1)}, f32[64,128]{1,0:T(8,128)S(1)}, f32[128,128]{1,0:T(8,128)S(1)}, f32[128,128]{1,0:T(8,128)S(1)}) custom-call(f32[32,8,128]{2,1,0:T(8,128)S(1)} %all-to-all-done.cells_ref, s32[1,128]{1,0:T(1,128)S(1)} %get-tuple-element.31.counts_ref, ...), custom_call_target="tpu_custom_call" | custom-call | tf_op jit(solution)/shard_map/short_forward/pallas_call | solution.py:727
  20.1 2.5 %all-to-all-start.1 = ((f32[32,4,128]{2,1,0:T(4,128)}), f32[32,4,128]{2,1,0:T(4,128)S(1)}, u32[]{:S(2)}, u32[]{:S(2)}) async-start(f32[32,4,128]{2,1,0:T(4,128)} %get-tuple-element.38), calls=%async_computation.1 | async-start | bytes 131072 | tf_op jit(solution)/shard_map/all_to_all | solution.py:650
  22.7 0.6 %tables.1.axes_ref = f32[6,8,4096]{2,1,0:T(8,128)S(1)} custom-call(f32[32,8,128]{2,1,0:T(8,128)S(1)} %all-to-all-done.cells_ref), custom_call_target="tpu_custom_call" | custom-call | flops 8192000 | bytes 819200 | tf_op jit(solution)/shard_map/tables/pallas_call | solution.py:757
  23.3 7.0 %all-to-all-done.1.recv_ref = f32[32,4,128]{2,1,0:T(4,128)S(1)} async-done(((f32[32,4,128]{2,1,0:T(4,128)}), f32[32,4,128]{2,1,0:T(4,128)S(1)}, u32[]{:S(2)}, u32[]{:S(2)}) %all-to-all-start.1) | async-done | bytes 65568 | tf_op jit(solution)/shard_map/all_to_all | solution.py:650
  30.3 4.3 %waves.1 = (f32[32,8,128]{2,1,0:T(8,128)}, f32[8,128]{1,0:T(8,128)S(1)}) custom-call(f32[32,4,128]{2,1,0:T(4,128)S(1)} %all-to-all-done.1.recv_ref, f32[6,8,4096]{2,1,0:T(8,128)S(1)} %tables.1.axes_ref, f32[4,56,32]{2,1,0:T(8,128)S(1)} %get-tuple-element.40.phi_ref, f32[8,32]{1,0:T(8,128)S(1)} %get-tuple-element.41.width_ref), custom_call_target="tpu_custom_call" | custom-call | tf_op jit(solution)/shard_map/waves/pallas_call | solution.py:795
  34.6 2.6 %all-to-all-start.2 = ((f32[32,8,128]{2,1,0:T(8,128)}), f32[32,8,128]{2,1,0:T(8,128)S(1)}, u32[]{:S(2)}, u32[]{:S(2)}) async-start(f32[32,8,128]{2,1,0:T(8,128)} %get-tuple-element.42), calls=%async_computation.2 | async-start | bytes 262144 | tf_op jit(solution)/shard_map/all_to_all | solution.py:650
  37.2 0.4 readout.1.dupd_ref
  37.6 8.2 %all-to-all-done.2.recv_ref = f32[32,8,128]{2,1,0:T(8,128)S(1)} async-done(((f32[32,8,128]{2,1,0:T(8,128)}), f32[32,8,128]{2,1,0:T(8,128)S(1)}, u32[]{:S(2)}, u32[]{:S(2)}) %all-to-all-start.2) | async-done | bytes 131104 | tf_op jit(solution)/shard_map/all_to_all | solution.py:650
  45.8 1.4 %short_back.1 = (f32[32,8,128]{2,1,0:T(8,128)S(1)}, f32[8,128]{1,0:T(8,128)S(1)}) custom-call(f32[32,8,128]{2,1,0:T(8,128)S(1)} %all-to-all-done.2.recv_ref, f32[3,64,128]{2,1,0:T(8,128)S(1)} %get-tuple-element.43.vec_ref, f32[64,128]{1,0:T(8,128)S(1)} %get-tuple-element.44.kind_ref, f32[128,128]{1,0:T(8,128)S(1)} %readout.1.dupd_ref, ...), custom_call_target="tpu_custom_call" | custom-call | tf_op jit(solution)/shard_map/short_back/pallas_call | solution.py:800
  47.3 0.0 copy-start
  47.3 10.3 %all_to_all.20.recv_ref = f32[32,8,128]{2,1,0:T(8,128)S(1)} all-to-all(f32[32,8,128]{2,1,0:T(8,128)S(1)} %get-tuple-element.52), channel_id=1, replica_groups=mesh['row'=16,'col'=2] {'row','col'}, dimensions={0} | all-to-all | bytes 262144 | tf_op jit(solution)/shard_map/all_to_all | solution.py:650
  57.6 0.0 copy-done
  57.6 0.9 %returned_ghosts.1 = (f32[3,1,128]{2,1,0:T(1,128)}, f32[3,3]{1,0:T(4,128)}) custom-call(f32[32,8,128]{2,1,0:T(8,128)S(1)} %all_to_all.20.recv_ref, f32[8,128]{1,0:T(8,128)S(1)} %get-tuple-element.53.own_ref, s32[8,128]{1,0:T(8,128)S(1)} %bitcast.12), custom_call_target="tpu_custom_call" | custom-call | tf_op jit(solution)/shard_map/returned_ghosts/pallas_call | solution.py:814
Async XLA Ops:
  2.1 15.9 %all-to-all-start = ((f32[32,8,128]{2,1,0:T(8,128)}), f32[32,8,128]{2,1,0:T(8,128)S(1)}, u32[]{:S(2)}, u32[]{:S(2)}) async-start(f32[32,8,128]{2,1,0:T(8,128)} %get-tuple-element.29), calls=%async_computation | async-start | bytes 262144 | tf_op jit(solution)/shard_map/all_to_all | solution.py:650
  20.1 10.2 %all-to-all-start.1 = ((f32[32,4,128]{2,1,0:T(4,128)}), f32[32,4,128]{2,1,0:T(4,128)S(1)}, u32[]{:S(2)}, u32[]{:S(2)}) async-start(f32[32,4,128]{2,1,0:T(4,128)} %get-tuple-element.38), calls=%async_computation.1 | async-start | bytes 131072 | tf_op jit(solution)/shard_map/all_to_all | solution.py:650
  34.6 11.2 %all-to-all-start.2 = ((f32[32,8,128]{2,1,0:T(8,128)}), f32[32,8,128]{2,1,0:T(8,128)S(1)}, u32[]{:S(2)}, u32[]{:S(2)}) async-start(f32[32,8,128]{2,1,0:T(8,128)} %get-tuple-element.42), calls=%async_computation.2 | async-start | bytes 262144 | tf_op jit(solution)/shard_map/all_to_all | solution.py:650
  47.3 10.3 %copy-start = (s32[1,1,8,128]{3,2,1,0:T(8,128)S(1)}, s32[1,1,8,128]{3,2,1,0:T(8,128)}, u32[]{:S(2)}) copy-start(s32[1,1,8,128]{3,2,1,0:T(8,128)} %param.18) | copy-start | bytes 12292

commit v3 on v2

--- a/solution.py
+++ b/solution.py
@@ -183,10 +183,11 @@
     send_ref,
     vec_ref,
     kind_ref,
+    owner_ref,
     upd_ref,
     slope_ref,
     table,
-    base,
+    lists,
     pooled,
 ):
     own_channels, row_count, col_count = dims[:3]
@@ -196,33 +197,38 @@
     device_count = send_ref.shape[0]
     slots, _ = direction_slots(row_count, col_count)
     own = cells_ref[neighbour_of((0, 0), row_count, col_count)]
+    for part in range(4):
+        table[part, 0:1, :] = own[part : part + 1]
     for order, step in enumerate(DIRECTIONS):
         source = neighbour_of(step, row_count, col_count)
         list_row = 4 + slots[len(DIRECTIONS) - 1 - order]
         block = cells_ref[source]
-        base[0, order : order + 1, :] = block[0:1] + step[0] * CELL_EDGE
-        base[1, order : order + 1, :] = block[1:2] + step[1] * CELL_EDGE
-        base[2, order : order + 1, :] = block[2:3]
-        base[3, order : order + 1, :] = block[3:4]
-        base[4, order : order + 1, :] = block[list_row : list_row + 1]
-    picks = base[4].astype(jnp.int32)
-    for part in range(4):
-        table[part, 0:1, :] = own[part : part + 1]
-        table[part, 8:16, :] = jnp.take_along_axis(base[part], picks, axis=1)
+        row = 8 + order
+        table[0, row : row + 1, :] = block[0:1] + step[0] * CELL_EDGE
+        table[1, row : row + 1, :] = block[1:2] + step[1] * CELL_EDGE
+        table[2, row : row + 1, :] = block[2:3]
+        table[3, row : row + 1, :] = block[3:4]
+        lists[order : order + 1, :] = block[list_row : list_row + 1].astype(jnp.int32)
 
     ids = ids_ref[...]
     lane = ids & (atom_count - 1)
     source = ids // atom_count
+    here = [source == order + 1 for order in range(len(DIRECTIONS))]
+
+    def picked(ref, first, places, start):
+        values = start
+        for order in range(len(DIRECTIONS)):
+            wide = jnp.broadcast_to(ref[first + order : first + order + 1, :], ids.shape)
+            values = jnp.where(here[order], jnp.take_along_axis(wide, places, axis=1), values)
+        return values
+
+    owner = picked(lists, 0, lane, lane)
+    owner_ref[...] = owner + source * atom_count
     gathered = []
     for part in range(4):
         wide = jnp.broadcast_to(table[part, 0:1, :], ids.shape)
-        values = jnp.take_along_axis(wide, lane, axis=1)
-        for order in range(len(DIRECTIONS)):
-            wide = jnp.broadcast_to(table[part, 8 + order : 9 + order, :], ids.shape)
-            values = jnp.where(
-                source == order + 1, jnp.take_along_axis(wide, lane, axis=1), values
-            )
-        gathered.append(values)
+        first = jnp.take_along_axis(wide, owner, axis=1)
+        gathered.append(picked(table.at[part], 8, owner, first))
     slot = lax.broadcasted_iota(jnp.int32, ids.shape, 0)
     kind = jnp.where(slot < counts_ref[...], gathered[3], -1.0)
     kind_ref[...] = kind
@@ -311,26 +317,13 @@
     lax.fori_loop(0, chunk, one, 0, unroll=4)
 
 
-def wave_kernel(
-    dims,
-    recv_ref,
-    axes_ref,
-    phi_ref,
-    width_ref,
-    send_ref,
-    virial_ref,
-    high,
-    low,
-    lifted,
-    sums,
-    coefficients,
-):
+def wave_kernel(dims, recv_ref, axes_ref, phi_ref, send_ref, sums, high, low, lifted, coefficients):
     own_channels, chunk_count, lengths = dims
     planes = (high, low, axes_ref, lifted)
     if chunk_count == 1:
         sums[...] = wave_sums(own_channels, recv_ref, *planes)
-        wave_coefficients(lengths, sums, phi_ref, width_ref, virial_ref, coefficients)
-        wave_back(own_channels, lengths, *planes, coefficients, send_ref)
+        wave_coefficients(sums, phi_ref, coefficients)
+        wave_features(own_channels, *planes, coefficients, send_ref)
         return
     phase, chunk_id = pl.program_id(0), pl.program_id(1)
 
@@ -346,11 +339,53 @@
 
     @pl.when((phase == 1) & (chunk_id == 0))
     def _():
-        wave_coefficients(lengths, sums, phi_ref, width_ref, virial_ref, coefficients)
+        wave_coefficients(sums, phi_ref, coefficients)
 
     @pl.when(phase == 1)
     def _():
-        wave_back(own_channels, lengths, *planes, coefficients, send_ref)
+        wave_features(own_channels, *planes, coefficients, send_ref)
+
+
+def wave_force_kernel(
+    dims, recv_ref, axes_ref, phi_ref, width_ref, sums, push_ref, high, low, lifted, coefficients
+):
+    own_channels, chunk_count, lengths = dims
+    planes = (high, low, axes_ref, lifted)
+    wave_planes(own_channels, recv_ref, *planes)
+    if chunk_count == 1:
+        wave_coefficients(sums, phi_ref, coefficients, True)
+    else:
+
+        @pl.when(pl.program_id(0) == 0)
+        def _():
+            wave_coefficients(sums, phi_ref, coefficients, True)
+
+    wave_back(own_channels, lengths, *planes, coefficients, push_ref)
+    virial = wave_virial(lengths, sums, phi_ref, width_ref, (1, push_ref.shape[2]))
+    push_ref[:, 3, :] = jnp.broadcast_to(virial, (push_ref.shape[0], push_ref.shape[2]))
+
+
+def wave_planes(own_channels, recv_ref, high_ref, low_ref, axes_ref, lifted, devices=None):
+    chunk, _, atom_count = recv_ref.shape
+    lanes = own_channels * HARMONICS
+    for index in devices or range(chunk):
+        spot = slice(index * atom_count, (index + 1) * atom_count)
+        for q in range(own_channels):
+            feature = recv_ref[index, q : q + 1, :]
+            for part in range(2):
+                row = part * lanes + q * HARMONICS
+                lifted[row : row + HARMONICS, spot] = feature * axes_ref[4 + part, :, spot]
+        products = [
+            axes_ref[first_axis, m : m + 1, spot] * axes_ref[second_axis, :, spot]
+            for first_axis, second_axis in ((0, 2), (0, 3), (1, 2), (1, 3))
+            for m in range(KMAX + 1)
+        ]
+        for pair in range(len(products) // 2):
+            both = jnp.concatenate(products[2 * pair : 2 * pair + 2], axis=0)
+            high = both.astype(BF16)
+            rows = slice(2 * HARMONICS * pair, 2 * HARMONICS * (pair + 1))
+            high_ref[rows, spot] = high
+            low_ref[rows, spot] = (both - high.astype(F32)).astype(BF16)
 
 
 def wave_sums(own_channels, recv_ref, high_ref, low_ref, axes_ref, lifted):
@@ -359,24 +394,8 @@
     group = math.gcd(chunk, 8)
     total = 0.0
     for first in range(0, chunk, group):
-        for index in range(first, first + group):
-            spot = slice(index * atom_count, (index + 1) * atom_count)
-            for q in range(own_channels):
-                feature = recv_ref[index, q : q + 1, :]
-                for part in range(2):
-                    row = part * lanes + q * HARMONICS
-                    lifted[row : row + HARMONICS, spot] = feature * axes_ref[4 + part, :, spot]
-            products = [
-                axes_ref[first_axis, m : m + 1, spot] * axes_ref[second_axis, :, spot]
-                for first_axis, second_axis in ((0, 2), (0, 3), (1, 2), (1, 3))
-                for m in range(KMAX + 1)
-            ]
-            for pair in range(len(products) // 2):
-                both = jnp.concatenate(products[2 * pair : 2 * pair + 2], axis=0)
-                high = both.astype(BF16)
-                rows = slice(2 * HARMONICS * pair, 2 * HARMONICS * (pair + 1))
-                high_ref[rows, spot] = high
-                low_ref[rows, spot] = (both - high.astype(F32)).astype(BF16)
+        devices = range(first, first + group)
+        wave_planes(own_channels, recv_ref, high_ref, low_ref, axes_ref, lifted, devices)
         spot = slice(first * atom_count, (first + group) * atom_count)
         values = lifted[:, spot]
         high = values.astype(BF16)
@@ -386,25 +405,27 @@
     return total
 
 
-def wave_coefficients(lengths, sums_ref, phi_ref, width_ref, virial_ref, coefficients_ref):
+SIGNS = ((1.0, 1.0), (1.0, -1.0), (-1.0, 1.0), (-1.0, -1.0))
+
+
+def wave_blocks(sums_ref, phi_ref):
     _, rows, lanes = phi_ref.shape
     sums = sums_ref[...]
     cos_part, sin_part = sums[:, :lanes], sums[:, lanes:]
-    blocks = [(cos_part[p * rows : (p + 1) * rows], sin_part[p * rows : (p + 1) * rows]) for p in range(4)]
-    (cc_c, cc_s), (cs_c, cs_s), (sc_c, sc_s), (ss_c, ss_s) = blocks
-    zero = jnp.zeros((rows, lanes), F32)
-    d_cc_c = d_cc_s = d_cs_c = d_cs_s = d_sc_c = d_sc_s = d_ss_c = d_ss_s = zero
-    total = even = first_odd = second_odd = both_odd = zero
-    for sign_id, (s1, s2) in enumerate(((1.0, 1.0), (1.0, -1.0), (-1.0, 1.0), (-1.0, -1.0))):
+    cc_c, cs_c, sc_c, ss_c = (cos_part[p * rows : (p + 1) * rows] for p in range(4))
+    cc_s, cs_s, sc_s, ss_s = (sin_part[p * rows : (p + 1) * rows] for p in range(4))
+    for sign_id, (s1, s2) in enumerate(SIGNS):
         real = cc_c - s1 * s2 * ss_c - s1 * sc_s - s2 * cs_s
         imag = cc_s - s1 * s2 * ss_s + s1 * sc_c + s2 * cs_c
         phi = phi_ref[sign_id]
-        dreal, dimag = phi * real, phi * imag
+        yield s1, s2, phi * real, phi * imag, real, imag
+
+
+def wave_virial(lengths, sums_ref, phi_ref, width_ref, shape):
+    _, rows, lanes = phi_ref.shape
+    even = first_odd = second_odd = both_odd = jnp.zeros((rows, lanes), F32)
+    for s1, s2, dreal, dimag, real, imag in wave_blocks(sums_ref, phi_ref):
         power = dreal * real + dimag * imag
-        d_cc_c, d_ss_c = d_cc_c + dreal, d_ss_c - s1 * s2 * dreal
-        d_sc_s, d_cs_s = d_sc_s - s1 * dreal, d_cs_s - s2 * dreal
-        d_cc_s, d_ss_s = d_cc_s + dimag, d_ss_s - s1 * s2 * dimag
-        d_sc_c, d_cs_c = d_sc_c + s1 * dimag, d_cs_c + s2 * dimag
         even = even + power
         first_odd = first_odd + s1 * power
         second_odd = second_odd + s2 * power
@@ -425,8 +446,18 @@
         (0, 2): -total_of(k1 * k3 * width * first_odd),
         (1, 2): -total_of(k2 * k3 * width * second_odd),
     }
-    virial_ref[...] = virial_row(terms, virial_ref.shape)
-
+    return virial_row(terms, shape)
+
+
+def wave_coefficients(sums_ref, phi_ref, coefficients_ref, gradients=False):
+    _, rows, lanes = phi_ref.shape
+    zero = jnp.zeros((rows, lanes), F32)
+    d_cc_c = d_cc_s = d_cs_c = d_cs_s = d_sc_c = d_sc_s = d_ss_c = d_ss_s = zero
+    for s1, s2, dreal, dimag, _, _ in wave_blocks(sums_ref, phi_ref):
+        d_cc_c, d_ss_c = d_cc_c + dreal, d_ss_c - s1 * s2 * dreal
+        d_sc_s, d_cs_s = d_sc_s - s1 * dreal, d_cs_s - s2 * dreal
+        d_cc_s, d_ss_s = d_cc_s + dimag, d_ss_s - s1 * s2 * dimag
+        d_sc_c, d_cs_c = d_sc_c + s1 * dimag, d_cs_c + s2 * dimag
     values = jnp.concatenate(
         [
             jnp.concatenate(pair, axis=1)
@@ -434,49 +465,68 @@
         ],
         axis=0,
     )
-    cc, cs, sc, ss = (values[p * rows : (p + 1) * rows] for p in range(4))
-    row_id = lax.broadcasted_iota(jnp.int32, (rows, 2 * lanes), 0)
-    m1 = (row_id // HARMONICS).astype(F32)
-    m2 = (row_id % HARMONICS).astype(F32)
-    along_x = jnp.concatenate([m1 * sc, m1 * ss, -m1 * cc, -m1 * cs], axis=0)
-    along_y = jnp.concatenate([m2 * cs, -m2 * cc, m2 * ss, -m2 * sc], axis=0)
-    stacked = jnp.concatenate([values, along_x, along_y], axis=1).T
-    high = stacked.astype(BF16)
-    coefficients_ref[0 : 6 * lanes, :] = high
-    coefficients_ref[6 * lanes :, :] = (stacked - high.astype(F32)).astype(BF16)
-
-
-def wave_back(own_channels, lengths, high_ref, low_ref, axes_ref, lifted, coefficients, send_ref):
+    if gradients:
+        cc, cs, sc, ss = (values[p * rows : (p + 1) * rows] for p in range(4))
+        row_id = lax.broadcasted_iota(jnp.int32, (rows, 2 * lanes), 0)
+        m1 = (row_id // HARMONICS).astype(F32)
+        m2 = (row_id % HARMONICS).astype(F32)
+        along_x = jnp.concatenate([m1 * sc, m1 * ss, -m1 * cc, -m1 * cs], axis=0)
+        along_y = jnp.concatenate([m2 * cs, -m2 * cc, m2 * ss, -m2 * sc], axis=0)
+        values = jnp.concatenate([values, along_x, along_y], axis=1)
+    turned = values.T
+    high = turned.astype(BF16)
+    count = turned.shape[0]
+    coefficients_ref[0:count, :] = high
+    coefficients_ref[count:, :] = (turned - high.astype(F32)).astype(BF16)
+
+
+def wave_spread(high_ref, low_ref, coefficients):
+    values = coefficients[...]
+    count = values.shape[0] // 2
+    main = dot(values, high_ref[...], 1, 0)
+    return main[:count] + (main[count:] + dot(values[:count], low_ref[...], 1, 0))
+
+
+def wave_features(own_channels, high_ref, low_ref, axes_ref, lifted, coefficients, send_ref):
     chunk, _, atom_count = send_ref.shape
     lanes = own_channels * HARMONICS
+    result = wave_spread(high_ref, low_ref, coefficients)
+    for index in range(chunk):
+        spot = slice(index * atom_count, (index + 1) * atom_count)
+        cos_z, sin_z = axes_ref[4, :, spot], axes_ref[5, :, spot]
+        for q in range(own_channels):
+            a, b = q * HARMONICS, lanes + q * HARMONICS
+            piece = result[a : a + HARMONICS, spot] * cos_z + result[b : b + HARMONICS, spot] * sin_z
+            send_ref[index, q : q + 1, :] = jnp.sum(piece, axis=0, keepdims=True)
+
+
+def wave_back(own_channels, lengths, high_ref, low_ref, axes_ref, lifted, coefficients, push_ref):
+    chunk, _, atom_count = push_ref.shape
+    lanes = own_channels * HARMONICS
     numbers = lax.broadcasted_iota(jnp.int32, (HARMONICS, atom_count), 0).astype(F32) + 1.0
-    values = coefficients[...]
-    main = dot(values, high_ref[...], 1, 0)
-    result = main[: 6 * lanes] + (main[6 * lanes :] + dot(values[: 6 * lanes], low_ref[...], 1, 0))
+    result = wave_spread(high_ref, low_ref, coefficients)
     for index in range(chunk):
-        low, high = index * atom_count, (index + 1) * atom_count
-        cos_z, sin_z = axes_ref[4, :, low:high], axes_ref[5, :, low:high]
-        part = result[:, low:high]
+        spot = slice(index * atom_count, (index + 1) * atom_count)
+        part = result[:, spot]
         grad_x = jnp.zeros((HARMONICS, atom_count), F32)
         grad_y = grad_x
         grad_z = grad_x
-        pieces = []
         for q in range(own_channels):
             a, b = q * HARMONICS, lanes + q * HARMONICS
-            on_cos, on_sin = part[a : a + HARMONICS], part[b : b + HARMONICS]
-            pieces.append(on_cos * cos_z + on_sin * sin_z)
-            lift_cos = lifted[a : a + HARMONICS, low:high]
-            lift_sin = lifted[b : b + HARMONICS, low:high]
-            grad_z = grad_z + on_sin * lift_cos - on_cos * lift_sin
+            lift_cos = lifted[a : a + HARMONICS, spot]
+            lift_sin = lifted[b : b + HARMONICS, spot]
+            grad_z = grad_z + part[b : b + HARMONICS] * lift_cos - part[a : a + HARMONICS] * lift_sin
             a, b = a + 2 * lanes, b + 2 * lanes
             grad_x = grad_x + part[a : a + HARMONICS] * lift_cos + part[b : b + HARMONICS] * lift_sin
             a, b = a + 2 * lanes, b + 2 * lanes
             grad_y = grad_y + part[a : a + HARMONICS] * lift_cos + part[b : b + HARMONICS] * lift_sin
-        pieces.append(grad_x * (2.0 * math.pi / lengths[0]))
-        pieces.append(grad_y * (2.0 * math.pi / lengths[1]))
-        pieces.append(grad_z * numbers * (2.0 * math.pi / lengths[2]))
-        for spot, piece in enumerate(pieces):
-            send_ref[index, spot : spot + 1, :] = jnp.sum(piece, axis=0, keepdims=True)
+        pieces = (
+            grad_x * (2.0 * math.pi / lengths[0]),
+            grad_y * (2.0 * math.pi / lengths[1]),
+            grad_z * numbers * (2.0 * math.pi / lengths[2]),
+        )
+        for row, piece in enumerate(pieces):
+            push_ref[index, row : row + 1, :] = jnp.sum(piece, axis=0, keepdims=True)
 
 
 def virial_row(terms, shape):
@@ -495,25 +545,23 @@
     kind_ref,
     dupd_ref,
     slope_ref,
-    ids_ref,
+    owner_ref,
     back_ref,
     mix_ref,
-    wave_virial_ref,
+    push_ref,
     send_ref,
-    own_ref,
     fgrad,
     dpool,
     parts,
 ):
     own_channels, row_count, col_count, species_count, radial_count = dims
-    slot_count, atom_count = ids_ref.shape
+    slot_count, atom_count = owner_ref.shape
     channel_count = mix_ref.shape[0]
     device_count = send_ref.shape[0]
     table_rows = round_up(len(DIRECTIONS) + 1, 16)
     for q in range(own_channels):
         low, high = q * device_count, min(channel_count, (q + 1) * device_count)
         fgrad[low:high, :] = recv_ref[0 : high - low, q, :]
-    total = jnp.sum(recv_ref[...], axis=0)
     dbefore = (fgrad[...] + dupd_ref[...]) * slope_ref[...]
     daggregate = dot(mix_ref[...], dbefore, 1, 0, GOOD)
     dpool[...] = dot(back_ref[...], daggregate, 1, 0, GOOD)
@@ -537,7 +585,7 @@
     terms = {
         (i, j): -total_of(grads[i] * vectors[j]) for i in range(3) for j in range(i, 3)
     }
-    virial = virial_row(terms, (1, atom_count)) + wave_virial_ref[0:1, :]
+    virial = virial_row(terms, (1, atom_count))
     for part in range(3):
         parts[2 * part], parts[2 * part + 1] = split(grads[part])
 
@@ -548,7 +596,7 @@
     for low in range(0, slot_count, group):
         hots, columns = [], []
         for s in range(low, low + group):
-            ids = ids_ref[s : s + 1, :]
+            ids = owner_ref[s : s + 1, :]
             hots.append(jnp.where(sublane == (ids & (atom_count - 1)), 1.0, 0.0).astype(BF16))
             mine = table_id == ids // atom_count
             columns.append(
@@ -564,47 +612,23 @@
             jnp.concatenate(hots, axis=1), jnp.concatenate(columns, axis=1), 1, 1
         )
     rows = scattered.T
-    slots, _ = direction_slots(row_count, col_count)
-    send_ref[...] = jnp.zeros_like(send_ref)
-    send_ref[:, 0, :] = jnp.broadcast_to(virial, (device_count, atom_count))
-    own_ref[...] = jnp.zeros_like(own_ref)
+    send_ref[...] = push_ref[...]
+    send_ref[:, 3, :] += jnp.broadcast_to(virial, (device_count, atom_count))
+    me = neighbour_of((0, 0), row_count, col_count)
     for part in range(3):
         low = 2 * part * table_rows
         both = rows[low : low + table_rows] + rows[low + table_rows : low + 2 * table_rows]
-        own_ref[part : part + 1, :] = (
-            both[0:1, :]
-            - jnp.sum(grads[part], axis=0, keepdims=True)
-            + total[own_channels + part : own_channels + part + 1, :]
-        )
+        send_ref[me, part, :] += both[0, :] - jnp.sum(grads[part], axis=0)
         for order, step in enumerate(DIRECTIONS):
             target = neighbour_of(step, row_count, col_count)
-            send_ref[target, 1 + 3 * slots[order] + part, :] = both[1 + order, :]
-
-
-def final_kernel(dims, recv_ref, own_ref, ghost_ref, forces_ref, virial_ref, parts):
-    row_count, col_count, volume = dims
-    atom_count = own_ref.shape[1]
-    slots, _ = direction_slots(row_count, col_count)
-    sublane = lax.broadcasted_iota(jnp.int32, (atom_count, ghost_ref.shape[1]), 0)
-    hots = []
-    parts[...] = jnp.zeros_like(parts)
-    for order, step in enumerate(DIRECTIONS):
-        source = neighbour_of((-step[0], -step[1]), row_count, col_count)
-        opposite = len(DIRECTIONS) - 1 - order
-        hots.append(
-            jnp.where(sublane == ghost_ref[opposite : opposite + 1, :], 1.0, 0.0).astype(BF16)
-        )
-        low, high = order * ghost_ref.shape[1], (order + 1) * ghost_ref.shape[1]
-        for part in range(3):
-            row = recv_ref[source, 1 + 3 * slots[order] + part, :].reshape(1, -1)
-            parts[2 * part : 2 * part + 1, low:high], parts[2 * part + 1 : 2 * part + 2, low:high] = split(row)
-    returned = dot(jnp.concatenate(hots, axis=1), parts[...].astype(BF16), 1, 1).T
+            send_ref[target, part, :] += both[1 + order, :]
+
+
+def final_kernel(volume, recv_ref, forces_ref, virial_ref):
+    total = jnp.sum(recv_ref[...], axis=0)
     for part in range(3):
-        forces_ref[part] = -(
-            own_ref[part : part + 1, :]
-            + (returned[2 * part : 2 * part + 1, :] + returned[2 * part + 1 : 2 * part + 2, :])
-        )
-    virial = jnp.sum(recv_ref[:, 0, :], axis=0, keepdims=True) * (1.0 / volume)
+        forces_ref[part] = -total[part : part + 1, :]
+    virial = total[3:4, :] * (1.0 / volume)
     for i in range(3):
         virial_ref[i : i + 1, :] = virial[:, 3 * i : 3 * i + 3]
 
@@ -638,9 +662,7 @@
     volume = lengths[0] * lengths[1] * lengths[2]
     rows = (KMAX + 1) * HARMONICS
     lanes = own_channels * HARMONICS
-    slab = round_up(own_channels + 3, 8)
     _, shared = direction_slots(row_count, col_count)
-    slab_back = round_up(1 + 3 * shared, 8)
     slab_first = round_up(4 + shared, 8)
     slab_features = round_up(own_channels, 4)
     chunk = math.gcd(device_count, 32)
@@ -724,7 +746,7 @@
         name="prepare",
     )(own_kinds, *fetched(*short_inputs, *wave_inputs))
 
-    send, vectors, kinds, updated, slope = call(
+    send, vectors, kinds, owners, updated, slope = call(
         functools.partial(
             short_forward_kernel, (own_channels,) + mesh_counts + (species_count, radial_count)
         ),
@@ -732,12 +754,13 @@
             shape(device_count, slab_features, atom_count),
             shape(3, slot_count, atom_count),
             shape(slot_count, atom_count),
+            jax.ShapeDtypeStruct((slot_count, atom_count), jnp.int32),
             shape(channel_count, atom_count),
             shape(channel_count, atom_count),
         ),
         scratch_shapes=[
             scratch(4, 16, atom_count),
-            scratch(5, direction_count, atom_count),
+            pltpu.VMEM((direction_count, atom_count), jnp.int32),
             scratch(pooled_rows * SUBLANES, atom_count),
         ],
         name="short_forward",
@@ -767,56 +790,81 @@
         updated, w_read, w_out
     )
 
-    wave = functools.partial(wave_kernel, (own_channels, chunk_count, lengths))
-    wave_shapes = (shape(device_count, slab, atom_count), shape(8, atom_count))
-    wave_scratch = [
-        pltpu.VMEM((4 * rows, chunk * atom_count), BF16),
-        pltpu.VMEM((4 * rows, chunk * atom_count), BF16),
-        scratch(2 * lanes, chunk * atom_count),
-        scratch(4 * rows, 2 * lanes),
-        pltpu.VMEM((12 * lanes, 4 * rows), BF16),
-    ]
-    if chunk_count == 1:
-        wave_options = {}
-    else:
+    features, dupd = lax.optimization_barrier((features, dupd))
+
+    plane = pltpu.VMEM((4 * rows, chunk * atom_count), BF16)
+    wave_scratch = [plane, plane, scratch(2 * lanes, chunk * atom_count)]
+    sums_shape = (4 * rows, 2 * lanes)
+    features_block = (chunk, slab_features, atom_count)
+    wave_options, force_options = {}, {}
+    if chunk_count > 1:
         wave_options = dict(
             grid=(2, chunk_count),
             in_specs=[
-                pl.BlockSpec((chunk, slab_features, atom_count), lambda p, i: (i, 0, 0)),
+                pl.BlockSpec(features_block, lambda p, i: (i, 0, 0)),
                 pl.BlockSpec(axes_block, lambda p, i: (0, 0, i)),
                 pl.BlockSpec((4, rows, lanes), lambda p, i: (0, 0, 0)),
-                pl.BlockSpec((8, lanes), lambda p, i: (0, 0)),
             ],
             out_specs=(
-                pl.BlockSpec((chunk, slab, atom_count), lambda p, i: (i * p, 0, 0)),
-                pl.BlockSpec((8, atom_count), lambda p, i: (0, 0)),
+                pl.BlockSpec(features_block, lambda p, i: (i * p, 0, 0)),
+                pl.BlockSpec(sums_shape, lambda p, i: (0, 0)),
             ),
         )
-    send, wave_virial = call(
-        wave, wave_shapes, vmem=20, scratch_shapes=wave_scratch, name="waves", **wave_options
-    )(features, axes, phi, width)
+        force_options = dict(
+            grid=(chunk_count,),
+            in_specs=[
+                pl.BlockSpec(features_block, lambda i: (i, 0, 0)),
+                pl.BlockSpec(axes_block, lambda i: (0, 0, i)),
+                pl.BlockSpec((4, rows, lanes), lambda i: (0, 0, 0)),
+                pl.BlockSpec((8, lanes), lambda i: (0, 0)),
+                pl.BlockSpec(sums_shape, lambda i: (0, 0)),
+            ],
+            out_specs=pl.BlockSpec((chunk, 4, atom_count), lambda i: (i, 0, 0)),
+        )
+    wave_dims = (own_channels, chunk_count, lengths)
+    send, sums = call(
+        functools.partial(wave_kernel, wave_dims),
+        (shape(device_count, slab_features, atom_count), shape(*sums_shape)),
+        vmem=20,
+        scratch_shapes=wave_scratch + [pltpu.VMEM((4 * lanes, 4 * rows), BF16)],
+        name="waves",
+        **wave_options,
+    )(features, axes, phi)
     gradients = exchange(send)
 
-    send, own = call(
+    push = call(
+        functools.partial(wave_force_kernel, wave_dims),
+        shape(device_count, 4, atom_count),
+        vmem=32,
+        scratch_shapes=wave_scratch + [pltpu.VMEM((12 * lanes, 4 * rows), BF16)],
+        cost_estimate=pl.CostEstimate(
+            flops=24 * lanes * 4 * rows * device_count * atom_count,
+            bytes_accessed=200 * device_count * atom_count,
+            transcendentals=0,
+        ),
+        name="wave_forces",
+        **force_options,
+    )(features, axes, phi, width, sums)
+
+    send = call(
         functools.partial(
             short_back_kernel, (own_channels,) + mesh_counts + (species_count, radial_count)
         ),
-        out_shape=(shape(device_count, slab_back, atom_count), shape(8, atom_count)),
+        shape(device_count, 4, atom_count),
         scratch_shapes=[
             scratch(channel_count, atom_count),
             scratch(pooled_rows, atom_count),
             scratch(6, slot_count, atom_count),
         ],
         name="short_back",
-    )(gradients, vectors, kinds, dupd, slope, ids, back, w_mix, wave_virial)
+    )(gradients, vectors, kinds, dupd, slope, owners, back, w_mix, push)
     returned = exchange(send)
 
     forces, virial = call(
-        functools.partial(final_kernel, (row_count, col_count, volume)),
-        out_shape=(shape(3, 1, atom_count), shape(3, 3)),
-        scratch_shapes=[scratch(16, direction_count * ghost_count)],
-        name="returned_ghosts",
-    )(returned, own, ghosts)
+        functools.partial(final_kernel, volume),
+        (shape(3, 1, atom_count), shape(3, 3)),
+        name="total",
+    )(returned)
     return (forces[:, None], virial)
 
 

time: 58.8 us -> 55.9 us (0.951)
  waiting for transfers between devices: 20.6 us -> 17.1 us
  Pallas kernels: 14.5 us -> 16.1 us
  blocking collectives: 10.3 us -> 9.3 us
    all_to_all x3, waiting for transfers between devices: 20.6 us -> 17.1 us  [exchange(): return lax.all_to_all(slabs, AXES, 0, 0, tiled=True)]
    pallas_call x2 -> x3, Pallas kernels: 5.22 us -> 6.6 us  [the longest x1 3.41 us: per_device(): call(functools.partial(wave_kernel, wave_dims), (shape(device_count, slab...]
    all_to_all x1, blocking collectives: 10.3 us -> 9.3 us  [exchange(): return lax.all_to_all(slabs, AXES, 0, 0, tiled=True)]
  transfers between devices with their start and end apart: 3 -> 3, of which waited for: 3 -> 3; matrix products, arithmetic and copies ran while one was open for 0% -> 0% of each run, Pallas kernels for 7% -> 12%
where the time goes in v3:
time: 55.9 us; the launch traced here: 55.5 us
  waiting for transfers between devices  17.1 us (31%)
  Pallas kernels  16.1 us (29%)
  starting transfers between devices  12.4 us (22%)
  blocking collectives  9.3 us (17%)
  between operations  0.7 us (1%)
    all_to_all x3, waiting for transfers between devices, exchange(): return lax.all_to_all(slabs, AXES, 0, 0, tiled=True)  17.1 us
    all_to_all x3, starting transfers between devices, exchange(): return lax.all_to_all(slabs, AXES, 0, 0, tiled=True)  12.4 us
    all_to_all x1, blocking collectives, exchange(): return lax.all_to_all(slabs, AXES, 0, 0, tiled=True)  9.3 us
    pallas_call x1, Pallas kernels, per_device(): call(functools.partial(wave_kernel, wave_dims), (shape(device_count, slab...  3.41 us
    pallas_call x1, Pallas kernels, per_device(): call(functools.partial(prepare_kernel, (device_count, channel_count, own_...  3.18 us
    pallas_call x1, Pallas kernels, per_device(): call(functools.partial(wave_force_kernel, wave_dims), shape(device_count,...  2.5 us
    pallas_call x1, Pallas kernels, per_device(): call(functools.partial(short_forward_kernel, (own_channels,) + mesh_count...  2.3 us
    pallas_call x1, Pallas kernels, per_device(): call(functools.partial(short_back_kernel, (own_channels,) + mesh_counts +...  1.51 us
  transfers between devices with their start and end apart: 3, of which 3 were waited for; matrix products, arithmetic and copies ran while one was open for 0% of the time, Pallas kernels for 12%

profile of v3, /device:TPU:0, one launch (start us, length us, event | category | flops | bytes accessed | tf_op | source)
XLA Modules:
  0.0 55.5 jit_solution(9851072469261178366)
XLA Ops:
  0.6 1.4 %pack.1 = (f32[32,8,128]{2,1,0:T(8,128)}, f32[1,128]{1,0:T(1,128)S(1)}) custom-call(f32[3,1,128]{2,1,0:T(1,128)} %bitcast.13, s32[1,128]{1,0:T(1,128)} %bitcast.18, s32[8,128]{1,0:T(8,128)} %bitcast.12), custom_call_target="tpu_custom_call" | custom-call | tf_op jit(solution)/shard_map/pack/pallas_call | solution.py:696
  2.1 7.3 %all-to-all-start = ((f32[32,8,128]{2,1,0:T(8,128)}), f32[32,8,128]{2,1,0:T(8,128)S(1)}, u32[]{:S(2)}, u32[]{:S(2)}) async-start(f32[32,8,128]{2,1,0:T(8,128)} %get-tuple-element.30), calls=%async_computation | async-start | bytes 262144 | tf_op jit(solution)/shard_map/all_to_all | solution.py:672
  9.4 3.2 %prepare.1 = (s32[1,128]{1,0:T(1,128)S(1)}, s32[64,128]{1,0:T(8,128)S(1)}, f32[16,128]{1,0:T(8,128)}, f32[6,128]{1,0:T(8,128)}, f32[128,128]{1,0:T(8,128)S(1)}, ...) custom-call(f32[1,128]{1,0:T(1,128)S(1)} %get-tuple-element.31.kinds, ...), custom_call_target="tpu_custom_call" | custom-call | flops 43008000 | bytes 512000 | tf_op jit(solution)/shard_map/prepare/pallas_call | solution.py:721
  12.6 5.4 %all-to-all-done.cells_ref = f32[32,8,128]{2,1,0:T(8,128)S(1)} async-done(((f32[32,8,128]{2,1,0:T(8,128)}), f32[32,8,128]{2,1,0:T(8,128)S(1)}, u32[]{:S(2)}, u32[]{:S(2)}) %all-to-all-start) | async-done | bytes 131104 | tf_op jit(solution)/shard_map/all_to_all | solution.py:672
  18.0 2.3 %short_forward.1 = (f32[32,4,128]{2,1,0:T(4,128)}, f32[3,64,128]{2,1,0:T(8,128)S(1)}, f32[64,128]{1,0:T(8,128)S(1)}, s32[64,128]{1,0:T(8,128)S(1)}, f32[128,128]{1,0:T(8,128)S(1)}, /*index=5*/f32[128,128]{1,0:T(8,128)S(1)}) custom-call(f32[32,8,128]{2,1,0:T(8,128)S(1)} %all-to-all-done.cells_ref, s32[1,128]{1,0:T(1,128)S(1)} %get-tuple-element.32.counts_ref, ...), custom_call_target="tpu_custom_call" | custom-call | tf_op jit(solution)/shard_map/short_forward/pallas_call | solution.py:749
  20.3 2.6 %all-to-all-start.1 = ((f32[32,4,128]{2,1,0:T(4,128)}), f32[32,4,128]{2,1,0:T(4,128)S(1)}, u32[]{:S(2)}, u32[]{:S(2)}) async-start(f32[32,4,128]{2,1,0:T(4,128)} %get-tuple-element.39), calls=%async_computation.1 | async-start | bytes 131072 | tf_op jit(solution)/shard_map/all_to_all | solution.py:672
  22.9 0.4 readout.1.dupd_ref
  23.3 0.6 %tables.1.axes_ref = f32[6,8,4096]{2,1,0:T(8,128)S(1)} custom-call(f32[32,8,128]{2,1,0:T(8,128)S(1)} %all-to-all-done.cells_ref), custom_call_target="tpu_custom_call" | custom-call | flops 8192000 | bytes 819200 | tf_op jit(solution)/shard_map/tables/pallas_call | solution.py:780
  23.9 6.5 %all-to-all-done.1.recv_ref = f32[32,4,128]{2,1,0:T(4,128)S(1)} async-done(((f32[32,4,128]{2,1,0:T(4,128)}), f32[32,4,128]{2,1,0:T(4,128)S(1)}, u32[]{:S(2)}, u32[]{:S(2)}) %all-to-all-start.1) | async-done | bytes 65568 | tf_op jit(solution)/shard_map/all_to_all | solution.py:672
  30.5 3.4 %waves.1 = (f32[32,4,128]{2,1,0:T(4,128)}, f32[224,64]{1,0:T(8,128)S(1)}) custom-call(f32[32,4,128]{2,1,0:T(4,128)S(1)} %all-to-all-done.1.recv_ref, f32[6,8,4096]{2,1,0:T(8,128)S(1)} %tables.1.axes_ref, f32[4,56,32]{2,1,0:T(8,128)S(1)} %get-tuple-element.45.phi_ref), custom_call_target="tpu_custom_call" | custom-call | tf_op jit(solution)/shard_map/waves/pallas_call | solution.py:825
  33.9 2.6 %all-to-all-start.2 = ((f32[32,4,128]{2,1,0:T(4,128)}), f32[32,4,128]{2,1,0:T(4,128)S(1)}, u32[]{:S(2)}, u32[]{:S(2)}) async-start(f32[32,4,128]{2,1,0:T(4,128)} %get-tuple-element.46), calls=%async_computation.2 | async-start | bytes 131072 | tf_op jit(solution)/shard_map/all_to_all | solution.py:672
  36.4 2.5 %wave_forces.1.push_ref = f32[32,4,128]{2,1,0:T(4,128)S(1)} custom-call(f32[32,4,128]{2,1,0:T(4,128)S(1)} %all-to-all-done.1.recv_ref, f32[6,8,4096]{2,1,0:T(8,128)S(1)} %tables.1.axes_ref, f32[4,56,32]{2,1,0:T(8,128)S(1)} %get-tuple-element.45.phi_ref, f32[8,32]{1,0:T(8,128)S(1)} %get-tuple-element.54.width_ref, f32[224,64]{1,0:T(8,128)S(1)} %get-tuple-element.55.sums), custom_call_target="tpu_custom_call" | custom-call | flops 704643072 | bytes 819200 | tf_op jit(solution)/shard_map/wave_forces/pallas_call | solution.py:835
  39.0 5.1 %all-to-all-done.2.recv_ref = f32[32,4,128]{2,1,0:T(4,128)S(1)} async-done(((f32[32,4,128]{2,1,0:T(4,128)}), f32[32,4,128]{2,1,0:T(4,128)S(1)}, u32[]{:S(2)}, u32[]{:S(2)}) %all-to-all-start.2) | async-done | bytes 65568 | tf_op jit(solution)/shard_map/all_to_all | solution.py:672
  44.1 1.5 %short_back.1 = f32[32,4,128]{2,1,0:T(4,128)S(1)} custom-call(f32[32,4,128]{2,1,0:T(4,128)S(1)} %all-to-all-done.2.recv_ref, f32[3,64,128]{2,1,0:T(8,128)S(1)} %get-tuple-element.47.vec_ref, f32[64,128]{1,0:T(8,128)S(1)} %get-tuple-element.48.kind_ref, f32[128,128]{1,0:T(8,128)S(1)} %readout.1.dupd_ref, f32[128,128]{1,0:T(8,128)S(1)} %get-tuple-element.50.slope_ref, ...), custom_call_target="tpu_custom_call" | custom-call | tf_op jit(solution)/shard_map/short_back/pallas_call | solution.py:849
  45.6 9.3 %all_to_all.20.recv_ref = f32[32,4,128]{2,1,0:T(4,128)S(1)} all-to-all(f32[32,4,128]{2,1,0:T(4,128)S(1)} %short_back.1), channel_id=1, replica_groups=mesh['row'=16,'col'=2] {'row','col'}, dimensions={0} | all-to-all | bytes 131072 | tf_op jit(solution)/shard_map/all_to_all | solution.py:672
  54.9 0.7 %total.1 = (f32[3,1,128]{2,1,0:T(1,128)}, f32[3,3]{1,0:T(4,128)}) custom-call(f32[32,4,128]{2,1,0:T(4,128)S(1)} %all_to_all.20.recv_ref), custom_call_target="tpu_custom_call" | custom-call | tf_op jit(solution)/shard_map/total/pallas_call | solution.py:863
Async XLA Ops:
  2.1 15.9 %all-to-all-start = ((f32[32,8,128]{2,1,0:T(8,128)}), f32[32,8,128]{2,1,0:T(8,128)S(1)}, u32[]{:S(2)}, u32[]{:S(2)}) async-start(f32[32,8,128]{2,1,0:T(8,128)} %get-tuple-element.30), calls=%async_computation | async-start | bytes 262144 | tf_op jit(solution)/shard_map/all_to_all | solution.py:672
  20.3 10.2 %all-to-all-start.1 = ((f32[32,4,128]{2,1,0:T(4,128)}), f32[32,4,128]{2,1,0:T(4,128)S(1)}, u32[]{:S(2)}, u32[]{:S(2)}) async-start(f32[32,4,128]{2,1,0:T(4,128)} %get-tuple-element.39), calls=%async_computation.1 | async-start | bytes 131072 | tf_op jit(solution)/shard_map/all_to_all | solution.py:672
  33.9 10.2 %all-to-all-start.2 = ((f32[32,4,128]{2,1,0:T(4,128)}), f32[32,4,128]{2,1,0:T(4,128)S(1)}, u32[]{:S(2)}, u32[]{:S(2)}) async-start(f32[32,4,128]{2,1,0:T(4,128)} %get-tuple-element.46), calls=%async_computation.2 | async-start | bytes 131072 | tf_op jit(solution)/shard_map/all_to_all | solution.py:672

commit v4 on v3

--- a/solution.py
+++ b/solution.py
@@ -12,7 +12,6 @@
 HEIGHT = 36.0
 KMAX = 6
 HARMONICS = 8
-SUBLANES = 8
 EXACT = lax.Precision.HIGHEST
 GOOD = lax.Precision.HIGH
 DIRECTIONS = ((-1, -1), (-1, 0), (-1, 1), (0, -1), (0, 1), (1, -1), (1, 0), (1, 1))
@@ -108,68 +107,66 @@
     return row * col_count + col
 
 
-def pack_kernel(counts, positions_ref, species_ref, ghosts_ref, send_ref, kinds_ref, positions, species, ghosts, sems):
+def slab_rows(slab, rows, atom_count):
+    width = slab.shape[-1] // atom_count
+    return [
+        slab[row // width : row // width + 1, row % width * atom_count : (row % width + 1) * atom_count]
+        for row in rows
+    ]
+
+
+def pack_kernel(counts, copied, positions_ref, species_ref, ghosts_ref, *refs):
     row_count, col_count = counts
-    fetch(((positions_ref, positions), (species_ref, species), (ghosts_ref, ghosts)), sems)
-    device_count, _, atom_count = send_ref.shape
+    sources, (send_ref, *targets) = refs[:copied], refs[copied : 2 * copied + 1]
+    positions, species, ghosts, first_sems, sems = refs[2 * copied + 1 :]
+    firsts = ((positions_ref, positions), (species_ref, species), (ghosts_ref, ghosts))
+    firsts = start_copies(firsts, first_sems)
+    others = start_copies(tuple(zip(sources, targets)), sems)
+    device_count = send_ref.shape[0]
+    atom_count = species.shape[1]
+    width = send_ref.shape[2] // atom_count
     slots, _ = direction_slots(row_count, col_count)
-    kinds = species[...].astype(F32)
-    kinds_ref[...] = kinds
-    for part in range(3):
-        send_ref[:, part, :] = jnp.broadcast_to(positions[part], (device_count, atom_count))
-    send_ref[:, 3, :] = jnp.broadcast_to(kinds, (device_count, atom_count))
+    for copy in firsts:
+        copy.wait()
+    rows = [positions[0], positions[1], positions[2], species[...].astype(F32)]
+    for row, values in enumerate(rows):
+        low = row % width * atom_count
+        send_ref[:, row // width, low : low + atom_count] = jnp.broadcast_to(
+            values, (device_count, atom_count)
+        )
     for order, step in enumerate(DIRECTIONS):
         target = neighbour_of(step, row_count, col_count)
-        send_ref[target, 4 + slots[order], :] = ghosts[order, :].astype(F32)
-
-
-def fetch(pairs, sems):
+        row = 4 + slots[order]
+        low = row % width * atom_count
+        send_ref[target, row // width, low : low + atom_count] = ghosts[order, :].astype(F32)
+    for copy in others:
+        copy.wait()
+
+
+def start_copies(pairs, sems):
     copies = [
         pltpu.make_async_copy(source, target, sems.at[spot])
         for spot, (source, target) in enumerate(pairs)
     ]
     for copy in copies:
         copy.start()
-    for copy in copies:
-        copy.wait()
-
-
-def prepare_kernel(dims, kinds_ref, *refs):
-    copied = 7
-    sources, refs = refs[: copied + 4], refs[copied + 4 :]
-    counts_ref, ids_ref, radial_ref, embed_ref, mix_ref, read_ref, out_ref = refs[:copied]
-    phi_ref, width_out_ref, pool_ref, back_ref, mix_turned_ref, initial_ref = refs[copied : copied + 6]
-    gain, waves, amp, width, weights, kinds8, sems = refs[copied + 6 :]
-    fetch(tuple(zip(sources, (*refs[:copied], gain, waves, amp, width))), sems)
-    slot_count = ids_ref.shape[0]
+    return copies
+
+
+def weights_kernel(
+    dims, slot_count, gain_ref, waves_ref, amp_ref, width_ref, radial_ref, embed_ref, phi_ref, width_out_ref, back_ref
+):
     species_count, channel_count = embed_ref.shape
     radial_count = radial_ref.shape[0]
-    atom_count = kinds_ref.shape[1]
-    mix_turned_ref[...] = mix_ref[...].T
-    kinds8[...] = jnp.zeros_like(kinds8)
-    kinds8[0:species_count, :] = embed_ref[...]
-    own_hot = (
-        lax.broadcasted_iota(jnp.int32, (kinds8.shape[0], atom_count), 0).astype(F32) == kinds_ref[...]
-    ).astype(F32)
-    initial_ref[...] = dot(kinds8[...], own_hot, 0, 0, EXACT)
-    rates = [radial_rate(order) for order in range(radial_count)]
     order_id = lax.broadcasted_iota(jnp.int32, (radial_count, channel_count), 0)
     factor = jnp.zeros((radial_count, channel_count), F32)
-    for order, rate in enumerate(rates):
-        factor = jnp.where(order_id == order, -2.0 * rate / slot_count, factor)
-    weights[...] = jnp.zeros_like(weights)
+    for order in range(radial_count):
+        factor = jnp.where(order_id == order, -2.0 * radial_rate(order) / slot_count, factor)
     for k in range(species_count):
-        block = radial_ref[...] * embed_ref[k : k + 1, :]
-        weights[k * radial_count : (k + 1) * radial_count, :] = block * (1.0 / slot_count)
-        back_ref[k * radial_count : (k + 1) * radial_count, :] = block * factor
-    turned = weights[...].T
-    lane = lax.broadcasted_iota(jnp.int32, turned.shape, 1)
-    for tile in range(pool_ref.shape[1] // lane.shape[1]):
-        picks = lane // SUBLANES + tile * (lane.shape[1] // SUBLANES)
-        pool_ref[:, tile * lane.shape[1] : (tile + 1) * lane.shape[1]] = jnp.take_along_axis(
-            turned, picks, axis=1
-        )
-    wave_weights(dims, gain, waves, amp, width, phi_ref, width_out_ref)
+        back_ref[k * radial_count : (k + 1) * radial_count, :] = (
+            radial_ref[...] * embed_ref[k : k + 1, :] * factor
+        )
+    wave_weights(dims, gain_ref, waves_ref, amp_ref, width_ref, phi_ref, width_out_ref)
 
 
 def short_forward_kernel(
@@ -177,9 +174,9 @@
     cells_ref,
     counts_ref,
     ids_ref,
-    pool_ref,
+    radial_ref,
+    embed_ref,
     mix_ref,
-    initial_ref,
     send_ref,
     vec_ref,
     kind_ref,
@@ -188,68 +185,84 @@
     slope_ref,
     table,
     lists,
+    codes,
     pooled,
+    weights,
+    kinds8,
 ):
-    own_channels, row_count, col_count = dims[:3]
+    own_channels, row_count, col_count = dims
     slot_count, atom_count = ids_ref.shape
-    species_count, radial_count = dims[3:]
-    channel_count = mix_ref.shape[0]
+    species_count, channel_count = embed_ref.shape
+    radial_count = radial_ref.shape[0]
     device_count = send_ref.shape[0]
     slots, _ = direction_slots(row_count, col_count)
-    own = cells_ref[neighbour_of((0, 0), row_count, col_count)]
+    own = slab_rows(cells_ref[neighbour_of((0, 0), row_count, col_count)], range(4), atom_count)
     for part in range(4):
-        table[part, 0:1, :] = own[part : part + 1]
+        table[part, 0:1, :] = own[part]
     for order, step in enumerate(DIRECTIONS):
         source = neighbour_of(step, row_count, col_count)
         list_row = 4 + slots[len(DIRECTIONS) - 1 - order]
-        block = cells_ref[source]
-        row = 8 + order
-        table[0, row : row + 1, :] = block[0:1] + step[0] * CELL_EDGE
-        table[1, row : row + 1, :] = block[1:2] + step[1] * CELL_EDGE
-        table[2, row : row + 1, :] = block[2:3]
-        table[3, row : row + 1, :] = block[3:4]
-        lists[order : order + 1, :] = block[list_row : list_row + 1].astype(jnp.int32)
+        block = slab_rows(cells_ref[source], (0, 1, 2, 3, list_row), atom_count)
+        row = slice(8 + order, 9 + order)
+        table[0, row, :] = block[0] + step[0] * CELL_EDGE
+        table[1, row, :] = block[1] + step[1] * CELL_EDGE
+        table[2, row, :] = block[2]
+        table[3, row, :] = block[3]
+        lists[order : order + 1, :] = block[4].astype(jnp.int32)
+    picks = lists[...]
+    for part in range(4):
+        table[part, 8:16, :] = jnp.take_along_axis(table[part, 8:16, :], picks, axis=1)
+    codes[8:16, :] = picks + atom_count * table[3, 8:16, :].astype(jnp.int32)
+    codes[0:1, :] = lax.broadcasted_iota(
+        jnp.int32, (1, atom_count), 1
+    ) + atom_count * own[3].astype(jnp.int32)
 
     ids = ids_ref[...]
     lane = ids & (atom_count - 1)
     source = ids // atom_count
     here = [source == order + 1 for order in range(len(DIRECTIONS))]
 
-    def picked(ref, first, places, start):
-        values = start
+    def picked(ref):
+        values = jnp.take_along_axis(jnp.broadcast_to(ref[0:1, :], ids.shape), lane, axis=1)
         for order in range(len(DIRECTIONS)):
-            wide = jnp.broadcast_to(ref[first + order : first + order + 1, :], ids.shape)
-            values = jnp.where(here[order], jnp.take_along_axis(wide, places, axis=1), values)
+            wide = jnp.broadcast_to(ref[8 + order : 9 + order, :], ids.shape)
+            values = jnp.where(here[order], jnp.take_along_axis(wide, lane, axis=1), values)
         return values
 
-    owner = picked(lists, 0, lane, lane)
-    owner_ref[...] = owner + source * atom_count
-    gathered = []
-    for part in range(4):
-        wide = jnp.broadcast_to(table[part, 0:1, :], ids.shape)
-        first = jnp.take_along_axis(wide, owner, axis=1)
-        gathered.append(picked(table.at[part], 8, owner, first))
+    gathered = [picked(table.at[part]) for part in range(3)]
+    code = picked(codes)
+    owner_ref[...] = (code & (atom_count - 1)) + source * atom_count
+    gathered.append((code // atom_count).astype(F32))
     slot = lax.broadcasted_iota(jnp.int32, ids.shape, 0)
     kind = jnp.where(slot < counts_ref[...], gathered[3], -1.0)
     kind_ref[...] = kind
     squared = jnp.zeros(ids.shape, F32)
     for part in range(3):
-        vector = gathered[part] - own[part : part + 1]
+        vector = gathered[part] - own[part]
         vec_ref[part] = vector
         squared = squared + vector * vector
     masks = [kind == float(k) for k in range(species_count)]
     for order in range(radial_count):
         basis = jnp.exp(squared * (-radial_rate(order)))
         for k in range(species_count):
-            spot = (k * radial_count + order) * SUBLANES
-            chosen = jnp.where(masks[k], basis, 0.0)
-            pooled[spot : spot + SUBLANES, :] = jnp.sum(
-                chosen.reshape(slot_count // SUBLANES, SUBLANES, atom_count), axis=0
+            spot = k * radial_count + order
+            pooled[spot : spot + 1, :] = jnp.sum(
+                jnp.where(masks[k], basis, 0.0), axis=0, keepdims=True
             )
-    aggregate = dot(pool_ref[...], pooled[...], 1, 0, GOOD)
-    before = dot(mix_ref[...], aggregate, 1, 0, GOOD)
+    for k in range(species_count):
+        weights[k * radial_count : (k + 1) * radial_count, :] = (
+            radial_ref[...] * embed_ref[k : k + 1, :] * (1.0 / slot_count)
+        )
+    kinds8[...] = jnp.zeros_like(kinds8)
+    kinds8[0:species_count, :] = embed_ref[...]
+    own_hot = (
+        lax.broadcasted_iota(jnp.int32, (kinds8.shape[0], atom_count), 0).astype(F32) == own[3]
+    ).astype(F32)
+    initial = dot(kinds8[...], own_hot, 0, 0, EXACT)
+    aggregate = dot(weights[...], pooled[...], 0, 0, GOOD)
+    before = dot(mix_ref[...], aggregate, 0, 0, GOOD)
     gate = 1.0 / (1.0 + jnp.exp(-before))
-    updated = initial_ref[...] + before * gate
+    updated = initial + before * gate
     slope_ref[...] = gate + before * gate * (1.0 - gate)
     for q in range(own_channels):
         low, high = q * device_count, min(channel_count, (q + 1) * device_count)
@@ -292,20 +305,21 @@
 
 def table_kernel(dims, cells_ref, axes_ref):
     col_count, chunk_count, lengths = dims
-    chunk, _, atom_count = cells_ref.shape
+    chunk = cells_ref.shape[0]
+    atom_count = axes_ref.shape[2] // chunk
     first_device = pl.program_id(0) * chunk if chunk_count > 1 else 0
     multiples = lax.broadcasted_iota(jnp.int32, (HARMONICS, atom_count), 0).astype(F32)
 
     def one(index, _):
         device = first_device + index
         spot = pl.ds(pl.multiple_of(index * atom_count, atom_count), atom_count)
-        block = cells_ref[index]
+        block = slab_rows(cells_ref[index], range(3), atom_count)
         corner_row = (device // col_count).astype(F32) * CELL_EDGE
         corner_col = (device % col_count).astype(F32) * CELL_EDGE
         turns = (
-            (block[0:1] + corner_row) * (1.0 / lengths[0]),
-            (block[1:2] + corner_col) * (1.0 / lengths[1]),
-            block[2:3] * (1.0 / lengths[2]),
+            (block[0] + corner_row) * (1.0 / lengths[0]),
+            (block[1] + corner_col) * (1.0 / lengths[1]),
+            block[2] * (1.0 / lengths[2]),
         )
         for axis in range(3):
             numbers = multiples + 1.0 if axis == 2 else multiples
@@ -391,7 +405,7 @@
 def wave_sums(own_channels, recv_ref, high_ref, low_ref, axes_ref, lifted):
     chunk, _, atom_count = recv_ref.shape
     lanes = own_channels * HARMONICS
-    group = math.gcd(chunk, 8)
+    group = math.gcd(chunk, 16)
     total = 0.0
     for first in range(0, chunk, group):
         devices = range(first, first + group)
@@ -663,7 +677,7 @@
     rows = (KMAX + 1) * HARMONICS
     lanes = own_channels * HARMONICS
     _, shared = direction_slots(row_count, col_count)
-    slab_first = round_up(4 + shared, 8)
+    slab_first = round_up(4 + shared, 2) // 2 * atom_count
     slab_features = round_up(own_channels, 4)
     chunk = math.gcd(device_count, 32)
     chunk_count = device_count // chunk
@@ -688,26 +702,7 @@
     ids = neighbours.reshape(slot_count, atom_count)
     ghosts = ghost_index.reshape(direction_count, ghost_count)
     mesh_counts = (row_count, col_count)
-    def fetched(*arrays):
-        return [pltpu.with_memory_space_constraint(x, pltpu.HBM) for x in arrays]
-
-    kept = pl.BlockSpec(memory_space=pltpu.HBM)
-    near = pl.BlockSpec(memory_space=pltpu.VMEM)
-    send, own_kinds = call(
-        functools.partial(pack_kernel, mesh_counts),
-        (shape(device_count, slab_first, atom_count), shape(1, atom_count)),
-        in_specs=[kept] * 3,
-        scratch_shapes=[
-            scratch(3, 1, atom_count),
-            pltpu.VMEM((1, atom_count), jnp.int32),
-            pltpu.VMEM(ghosts.shape, jnp.int32),
-            pltpu.SemaphoreType.DMA((3,)),
-        ],
-        name="pack",
-    )(*fetched(positions.reshape(3, 1, atom_count), species.reshape(1, atom_count), ghosts))
-    cells = exchange(send)
-
-    short_inputs = (
+    inputs = (
         counts.reshape(1, atom_count),
         ids,
         w_radial,
@@ -715,41 +710,36 @@
         w_mix,
         w_read,
         w_out.reshape(1, -1),
+        filter_gain,
+        wave_numbers,
+        amplitude.reshape(1, -1),
+        kernel_width.reshape(1, -1),
     )
-    wave_inputs = (filter_gain, wave_numbers, amplitude.reshape(1, -1), kernel_width.reshape(1, -1))
+    send, *inputs = call(
+        functools.partial(pack_kernel, mesh_counts, len(inputs)),
+        (shape(device_count, 2, slab_first),)
+        + tuple(jax.ShapeDtypeStruct(x.shape, x.dtype) for x in inputs),
+        in_specs=[pl.BlockSpec(memory_space=pltpu.HBM)] * (3 + len(inputs)),
+        scratch_shapes=[
+            scratch(3, 1, atom_count),
+            pltpu.VMEM((1, atom_count), jnp.int32),
+            pltpu.VMEM(ghosts.shape, jnp.int32),
+            pltpu.SemaphoreType.DMA((3,)),
+            pltpu.SemaphoreType.DMA((len(inputs),)),
+        ],
+        name="pack",
+    )(
+        *[
+            pltpu.with_memory_space_constraint(x, pltpu.HBM)
+            for x in (positions.reshape(3, 1, atom_count), species.reshape(1, atom_count), ghosts, *inputs)
+        ]
+    )
+    live, ids, w_radial, embedding, w_mix, w_read, w_out, *wave_inputs = inputs
+    cells = exchange(send)
+
     pooled_rows = species_count * radial_count
-    live, ids, _, _, w_mix, w_read, w_out, phi, width, pool, back, mix_turned, initial = call(
-        functools.partial(
-            prepare_kernel, (device_count, channel_count, own_channels, lengths, volume)
-        ),
-        tuple(jax.ShapeDtypeStruct(x.shape, x.dtype) for x in short_inputs)
-        + (
-            shape(4, rows, lanes),
-            shape(8, lanes),
-            shape(channel_count, round_up(pooled_rows * SUBLANES, channel_count)),
-            shape(pooled_rows, channel_count),
-            shape(channel_count, channel_count),
-            shape(channel_count, atom_count),
-        ),
-        in_specs=[near] + [kept] * (len(short_inputs) + len(wave_inputs)),
-        scratch_shapes=[pltpu.VMEM(x.shape, x.dtype) for x in wave_inputs]
-        + [
-            scratch(round_up(pooled_rows, 128), channel_count),
-            scratch(round_up(species_count, 8), channel_count),
-            pltpu.SemaphoreType.DMA((len(short_inputs) + len(wave_inputs),)),
-        ],
-        cost_estimate=pl.CostEstimate(
-            flops=2 * 4 * rows * filter_gain.shape[0] * 3 * lanes,
-            bytes_accessed=4 * filter_gain.size,
-            transcendentals=0,
-        ),
-        name="prepare",
-    )(own_kinds, *fetched(*short_inputs, *wave_inputs))
-
     send, vectors, kinds, owners, updated, slope = call(
-        functools.partial(
-            short_forward_kernel, (own_channels,) + mesh_counts + (species_count, radial_count)
-        ),
+        functools.partial(short_forward_kernel, (own_channels,) + mesh_counts),
         (
             shape(device_count, slab_features, atom_count),
             shape(3, slot_count, atom_count),
@@ -761,12 +751,28 @@
         scratch_shapes=[
             scratch(4, 16, atom_count),
             pltpu.VMEM((direction_count, atom_count), jnp.int32),
-            scratch(pooled_rows * SUBLANES, atom_count),
+            pltpu.VMEM((16, atom_count), jnp.int32),
+            scratch(pooled_rows, atom_count),
+            scratch(pooled_rows, channel_count),
+            scratch(round_up(species_count, 8), channel_count),
         ],
         name="short_forward",
-    )(cells, live, ids, pool, mix_turned, initial)
-    send, cells, updated = lax.optimization_barrier((send, cells, updated))
+    )(cells, live, ids, w_radial, embedding, w_mix)
+    send, cells, updated, *wave_inputs = lax.optimization_barrier((send, cells, updated, *wave_inputs))
     features = exchange(send)
+
+    phi, width, back = call(
+        functools.partial(
+            weights_kernel, (device_count, channel_count, own_channels, lengths, volume), slot_count
+        ),
+        (shape(4, rows, lanes), shape(8, lanes), shape(pooled_rows, channel_count)),
+        cost_estimate=pl.CostEstimate(
+            flops=2 * 4 * rows * filter_gain.shape[0] * 3 * lanes,
+            bytes_accessed=4 * filter_gain.size,
+            transcendentals=0,
+        ),
+        name="weights",
+    )(*wave_inputs, w_radial, embedding)
 
     axes_block = (6, HARMONICS, chunk * atom_count)
     if chunk_count == 1:
@@ -774,7 +780,7 @@
     else:
         table_options = dict(
             grid=(chunk_count,),
-            in_specs=[pl.BlockSpec((chunk, slab_first, atom_count), lambda i: (i, 0, 0))],
+            in_specs=[pl.BlockSpec((chunk, 2, slab_first), lambda i: (i, 0, 0))],
             out_specs=pl.BlockSpec(axes_block, lambda i: (0, 0, i)),
         )
     axes = call(
@@ -790,7 +796,7 @@
         updated, w_read, w_out
     )
 
-    features, dupd = lax.optimization_barrier((features, dupd))
+    features, dupd, phi = lax.optimization_barrier((features, dupd, phi))
 
     plane = pltpu.VMEM((4 * rows, chunk * atom_count), BF16)
     wave_scratch = [plane, plane, scratch(2 * lanes, chunk * atom_count)]

time: 55.9 us -> 54.7 us (0.979)
  blocking collectives: 9.3 us -> 24.5 us
  starting transfers between devices: 12.4 us -> 5.14 us
  waiting for transfers between devices: 17.1 us -> 10.4 us
  Pallas kernels: 16.1 us -> 13.7 us
    all_to_all x1 -> x2, blocking collectives: 9.3 us -> 24.5 us  [exchange(): return lax.all_to_all(slabs, AXES, 0, 0, tiled=True)]
    all_to_all x3 -> x2, starting transfers between devices: 12.4 us -> 5.14 us  [exchange(): return lax.all_to_all(slabs, AXES, 0, 0, tiled=True)]
    all_to_all x3 -> x2, waiting for transfers between devices: 17.1 us -> 10.4 us  [exchange(): return lax.all_to_all(slabs, AXES, 0, 0, tiled=True)]
    pallas_call x2, Pallas kernels: 4.61 us -> 2.47 us  [the longest x1 1.33 us: per_device(): call(functools.partial(pack_kernel, mesh_counts, len(inputs)), (shape(dev...]
  transfers between devices with their start and end apart: 3 -> 2, of which waited for: 3 -> 2; matrix products, arithmetic and copies ran while one was open for 0% -> 0% of each run, Pallas kernels for 12% -> 9%
where the time goes in v4:
time: 54.7 us; the launch traced here: 54.4 us
  blocking collectives  24.5 us (45%)
  Pallas kernels  13.7 us (25%)
  waiting for transfers between devices  10.4 us (19%)
  starting transfers between devices  5.14 us (9%)
  between operations  0.69 us (1%)
    all_to_all x2, blocking collectives, exchange(): return lax.all_to_all(slabs, AXES, 0, 0, tiled=True)  24.5 us
    all_to_all x2, waiting for transfers between devices, exchange(): return lax.all_to_all(slabs, AXES, 0, 0, tiled=True)  10.4 us
    all_to_all x2, starting transfers between devices, exchange(): return lax.all_to_all(slabs, AXES, 0, 0, tiled=True)  5.14 us
    pallas_call x1, Pallas kernels, per_device(): call(functools.partial(wave_kernel, wave_dims), (shape(device_count, slab...  3.21 us
    pallas_call x1, Pallas kernels, per_device(): call(functools.partial(wave_force_kernel, wave_dims), shape(device_count,...  2.5 us
    pallas_call x1, Pallas kernels, per_device(): call(functools.partial(short_forward_kernel, (own_channels,) + mesh_count...  2.17 us
    pallas_call x1, Pallas kernels, per_device(): call(functools.partial(short_back_kernel, (own_channels,) + mesh_counts +...  1.52 us
    pallas_call x1, Pallas kernels, per_device(): call(functools.partial(pack_kernel, mesh_counts, len(inputs)), (shape(dev...  1.33 us
  transfers between devices with their start and end apart: 2, of which 2 were waited for; matrix products, arithmetic and copies ran while one was open for 0% of the time, Pallas kernels for 9%

profile of v4, /device:TPU:0, one launch (start us, length us, event | category | flops | bytes accessed | tf_op | source)
XLA Modules:
  0.0 54.4 jit_solution(14444619294293710697)
XLA Ops:
  0.6 1.3 %pack.1 = (f32[32,2,384]{2,1,0:T(2,128)S(1)}, s32[1,128]{1,0:T(1,128)S(1)}, s32[64,128]{1,0:T(8,128)S(1)}, f32[16,128]{1,0:T(8,128)S(1)}, f32[6,128]{1,0:T(8,128...) custom-call(f32[3,1,128]{2,1,0:T(1,128)} %bitcast.13, ...), custom_call_target="tpu_custom_call" | custom-call | tf_op jit(solution)/shard_map/pack/pallas_call | solution.py:718
  2.0 15.2 %all_to_all.20.cells_ref = f32[32,2,384]{2,1,0:T(2,128)S(1)} all-to-all(f32[32,2,384]{2,1,0:T(2,128)S(1)} %get-tuple-element.37), channel_id=1, replica_groups=mesh['row'=16,'col'=2] {'row','col'}, dimensions={0} | all-to-all | bytes 196608 | tf_op jit(solution)/shard_map/all_to_all | solution.py:686
  17.2 2.2 %short_forward.1 = (f32[32,4,128]{2,1,0:T(4,128)}, f32[3,64,128]{2,1,0:T(8,128)S(1)}, f32[64,128]{1,0:T(8,128)S(1)}, s32[64,128]{1,0:T(8,128)S(1)}, f32[128,128]{1,0:T(8,128)S(1)}, /*index=5*/f32[128,128]{1,0:T(8,128)S(1)}) custom-call(f32[32,2,384]{2,1,0:T(2,128)S(1)} %all_to_all.20.cells_ref, s32[1,128]{1,0:T(1,128)S(1)} %get-tuple-element.38.counts_ref, ...), custom_call_target="tpu_custom_call" | custom-call | tf_op jit(solution)/shard_map/short_forward/pallas_call | solution.py:741
  19.4 2.6 %all-to-all-start.1 = ((f32[32,4,128]{2,1,0:T(4,128)}), f32[32,4,128]{2,1,0:T(4,128)S(1)}, u32[]{:S(2)}, u32[]{:S(2)}) async-start(f32[32,4,128]{2,1,0:T(4,128)} %get-tuple-element.49), calls=%async_computation.1 | async-start | bytes 131072 | tf_op jit(solution)/shard_map/all_to_all | solution.py:686
  21.9 0.4 readout.1.dupd_ref
  22.4 0.7 %tables.1.axes_ref = f32[6,8,4096]{2,1,0:T(8,128)S(1)} custom-call(f32[32,2,384]{2,1,0:T(2,128)S(1)} %all_to_all.20.cells_ref), custom_call_target="tpu_custom_call" | custom-call | flops 8192000 | bytes 819200 | tf_op jit(solution)/shard_map/tables/pallas_call | solution.py:786
  23.0 1.1 %weights.1 = (f32[4,56,32]{2,1,0:T(8,128)S(1)}, f32[8,32]{1,0:T(8,128)S(1)}, f32[96,128]{1,0:T(8,128)S(1)}) custom-call(f32[1000,128]{1,0:T(8,128)S(1)} %get-tuple-element.53.gain_ref, s32[3,1000]{1,0:T(4,128)S(1)} %get-tuple-element.54.waves_ref, f32[1,128]{1,0:T(1,128)S(1)} %get-tuple-element.55.amp_ref, f32[1,128]{1,0:T(1,128)S(1)} %get-tuple-element.56.width_ref, ...), custom_call_target="tpu_custom_call" | custom-call | flops 43008000 | bytes 512000 | tf_op jit(solution)/shard_map/weights/pallas_call | solution.py:764
  24.2 5.3 %all-to-all-done.1.recv_ref = f32[32,4,128]{2,1,0:T(4,128)S(1)} async-done(((f32[32,4,128]{2,1,0:T(4,128)}), f32[32,4,128]{2,1,0:T(4,128)S(1)}, u32[]{:S(2)}, u32[]{:S(2)}) %all-to-all-start.1) | async-done | bytes 65568 | tf_op jit(solution)/shard_map/all_to_all | solution.py:686
  29.5 3.2 %waves.1 = (f32[32,4,128]{2,1,0:T(4,128)}, f32[224,64]{1,0:T(8,128)S(1)}) custom-call(f32[32,4,128]{2,1,0:T(4,128)S(1)} %all-to-all-done.1.recv_ref, f32[6,8,4096]{2,1,0:T(8,128)S(1)} %tables.1.axes_ref, f32[4,56,32]{2,1,0:T(8,128)S(1)} %get-tuple-element.60.phi_ref), custom_call_target="tpu_custom_call" | custom-call | tf_op jit(solution)/shard_map/waves/pallas_call | solution.py:831
  32.7 2.6 %all-to-all-start.2 = ((f32[32,4,128]{2,1,0:T(4,128)}), f32[32,4,128]{2,1,0:T(4,128)S(1)}, u32[]{:S(2)}, u32[]{:S(2)}) async-start(f32[32,4,128]{2,1,0:T(4,128)} %get-tuple-element.61), calls=%async_computation.2 | async-start | bytes 131072 | tf_op jit(solution)/shard_map/all_to_all | solution.py:686
  35.3 2.5 %wave_forces.1.push_ref = f32[32,4,128]{2,1,0:T(4,128)S(1)} custom-call(f32[32,4,128]{2,1,0:T(4,128)S(1)} %all-to-all-done.1.recv_ref, f32[6,8,4096]{2,1,0:T(8,128)S(1)} %tables.1.axes_ref, f32[4,56,32]{2,1,0:T(8,128)S(1)} %get-tuple-element.60.phi_ref, f32[8,32]{1,0:T(8,128)S(1)} %get-tuple-element.68.width_ref, f32[224,64]{1,0:T(8,128)S(1)} %get-tuple-element.69.sums), custom_call_target="tpu_custom_call" | custom-call | flops 704643072 | bytes 819200 | tf_op jit(solution)/shard_map/wave_forces/pallas_call | solution.py:841
  37.8 5.1 %all-to-all-done.2.recv_ref = f32[32,4,128]{2,1,0:T(4,128)S(1)} async-done(((f32[32,4,128]{2,1,0:T(4,128)}), f32[32,4,128]{2,1,0:T(4,128)S(1)}, u32[]{:S(2)}, u32[]{:S(2)}) %all-to-all-start.2) | async-done | bytes 65568 | tf_op jit(solution)/shard_map/all_to_all | solution.py:686
  42.9 1.5 %short_back.1 = f32[32,4,128]{2,1,0:T(4,128)S(1)} custom-call(f32[32,4,128]{2,1,0:T(4,128)S(1)} %all-to-all-done.2.recv_ref, f32[3,64,128]{2,1,0:T(8,128)S(1)} %get-tuple-element.62.vec_ref, f32[64,128]{1,0:T(8,128)S(1)} %get-tuple-element.63.kind_ref, f32[128,128]{1,0:T(8,128)S(1)} %readout.1.dupd_ref, f32[128,128]{1,0:T(8,128)S(1)} %get-tuple-element.65.slope_ref, ...), custom_call_target="tpu_custom_call" | custom-call | tf_op jit(solution)/shard_map/short_back/pallas_call | solution.py:855
  44.5 9.3 %all_to_all.21.recv_ref = f32[32,4,128]{2,1,0:T(4,128)S(1)} all-to-all(f32[32,4,128]{2,1,0:T(4,128)S(1)} %short_back.1), channel_id=1, replica_groups=mesh['row'=16,'col'=2] {'row','col'}, dimensions={0} | all-to-all | bytes 131072 | tf_op jit(solution)/shard_map/all_to_all | solution.py:686
  53.8 0.7 %total.1 = (f32[3,1,128]{2,1,0:T(1,128)}, f32[3,3]{1,0:T(4,128)}) custom-call(f32[32,4,128]{2,1,0:T(4,128)S(1)} %all_to_all.21.recv_ref), custom_call_target="tpu_custom_call" | custom-call | tf_op jit(solution)/shard_map/total/pallas_call | solution.py:869
Async XLA Ops:
  19.4 10.2 %all-to-all-start.1 = ((f32[32,4,128]{2,1,0:T(4,128)}), f32[32,4,128]{2,1,0:T(4,128)S(1)}, u32[]{:S(2)}, u32[]{:S(2)}) async-start(f32[32,4,128]{2,1,0:T(4,128)} %get-tuple-element.49), calls=%async_computation.1 | async-start | bytes 131072 | tf_op jit(solution)/shard_map/all_to_all | solution.py:686
  32.7 10.2 %all-to-all-start.2 = ((f32[32,4,128]{2,1,0:T(4,128)}), f32[32,4,128]{2,1,0:T(4,128)S(1)}, u32[]{:S(2)}, u32[]{:S(2)}) async-start(f32[32,4,128]{2,1,0:T(4,128)} %get-tuple-element.61), calls=%async_computation.2 | async-start | bytes 131072 | tf_op jit(solution)/shard_map/all_to_all | solution.py:686

commit v5 on v4

--- a/solution.py
+++ b/solution.py
@@ -38,6 +38,11 @@
     return slots, max(seen.values())
 
 
+def tile_layout(own_channels):
+    shared = HARMONICS // own_channels
+    return shared, -(-KMAX // shared)
+
+
 def dot(lhs, rhs, lhs_dim, rhs_dim, precision=None):
     return lax.dot_general(
         lhs,
@@ -58,7 +63,8 @@
     me = lax.axis_index("row") * lax.axis_size("col") + lax.axis_index("col")
     wave_count = gain_ref.shape[0]
     rows = (KMAX + 1) * HARMONICS
-    lanes = own_channels * HARMONICS
+    together, tiles = tile_layout(own_channels)
+    lanes = tiles * HARMONICS
     place = lax.broadcasted_iota(jnp.int32, (8, channel_count), 0) * device_count + me
     chosen = (lax.broadcasted_iota(jnp.int32, (8, channel_count), 1) == place).astype(F32)
     own_gain = dot(chosen, gain_ref[...], 1, 1, EXACT)
@@ -67,10 +73,9 @@
     key = sign * rows + jnp.abs(first) * HARMONICS + jnp.abs(second)
     spots = lax.broadcasted_iota(jnp.int32, (4 * rows, wave_count), 0) == key
     onehot = jnp.where(spots, 1.0, 0.0).astype(BF16)
-    heights = lax.broadcasted_iota(jnp.int32, (HARMONICS, wave_count), 0) + 1 == third
-    blocks = [
-        jnp.where(heights, own_gain[q : q + 1, :], 0.0) for q in range(own_channels)
-    ]
+    mine = jnp.concatenate([own_gain[:own_channels]] * together, axis=0)
+    height = lax.broadcasted_iota(jnp.int32, (HARMONICS, wave_count), 0) // own_channels + 1
+    blocks = [jnp.where(height + tile * together == third, mine, 0.0) for tile in range(tiles)]
     wide = jnp.concatenate(blocks, axis=0)
     high = wide.astype(BF16)
     rest = wide - high.astype(F32)
@@ -78,13 +83,13 @@
     low = (rest - middle.astype(F32)).astype(BF16)
     summed = dot(onehot, high, 1, 1) + (dot(onehot, middle, 1, 1) + dot(onehot, low, 1, 1))
     lane = lax.broadcasted_iota(jnp.int32, (8, channel_count), 1)
-    wanted = jnp.minimum((lane // HARMONICS) * device_count + me, channel_count - 1)
+    wanted = jnp.minimum(lane % own_channels * device_count + me, channel_count - 1)
     amp = jnp.take_along_axis(jnp.broadcast_to(amp_ref[...], (8, channel_count)), wanted, axis=1)
     width = jnp.take_along_axis(
         jnp.broadcast_to(width_ref[...], (8, channel_count)), wanted, axis=1
     )
     amp, width = amp[0:1, :lanes], width[0:1, :lanes]
-    k1, k2, k3 = grid_numbers(rows, lanes, lengths)
+    k1, k2, k3 = grid_numbers(rows, lanes, own_channels, lengths)
     squared = k1 * k1 + k2 * k2 + k3 * k3
     base = amp * jnp.exp(-width * squared) * (1.0 / volume)
     for sign_id in range(4):
@@ -92,12 +97,12 @@
     width_out_ref[...] = jnp.broadcast_to(width, (8, lanes))
 
 
-def grid_numbers(rows, lanes, lengths):
+def grid_numbers(rows, lanes, own_channels, lengths):
     row_id = lax.broadcasted_iota(jnp.int32, (rows, lanes), 0)
     lane_id = lax.broadcasted_iota(jnp.int32, (rows, lanes), 1)
     k1 = (row_id // HARMONICS).astype(F32) * (2.0 * math.pi / lengths[0])
     k2 = (row_id % HARMONICS).astype(F32) * (2.0 * math.pi / lengths[1])
-    k3 = (lane_id % HARMONICS + 1).astype(F32) * (2.0 * math.pi / lengths[2])
+    k3 = (lane_id // own_channels + 1).astype(F32) * (2.0 * math.pi / lengths[2])
     return k1, k2, k3
 
 
@@ -153,9 +158,14 @@
     return copies
 
 
-def weights_kernel(
-    dims, slot_count, gain_ref, waves_ref, amp_ref, width_ref, radial_ref, embed_ref, phi_ref, width_out_ref, back_ref
-):
+def weights_kernel(dims, slot_count, table_dims, upd_ref, read_ref, out_ref, radial_ref, embed_ref, *refs):
+    cells, refs = refs[: len(refs) - 13 - bool(table_dims)], refs[len(refs) - 13 - bool(table_dims) :]
+    sources, (dupd_ref, back_ref, phi_ref, width_out_ref), refs = refs[:4], refs[4:8], refs[8:]
+    axes, targets, sems = refs[: len(refs) - 5], refs[-5:-1], refs[-1]
+    copies = start_copies(tuple(zip(sources, targets)), sems)
+    if table_dims:
+        table_kernel(table_dims, *cells, *axes)
+    readout_gradient(upd_ref, read_ref, out_ref, dupd_ref)
     species_count, channel_count = embed_ref.shape
     radial_count = radial_ref.shape[0]
     order_id = lax.broadcasted_iota(jnp.int32, (radial_count, channel_count), 0)
@@ -166,7 +176,9 @@
         back_ref[k * radial_count : (k + 1) * radial_count, :] = (
             radial_ref[...] * embed_ref[k : k + 1, :] * factor
         )
-    wave_weights(dims, gain_ref, waves_ref, amp_ref, width_ref, phi_ref, width_out_ref)
+    for copy in copies:
+        copy.wait()
+    wave_weights(dims, *targets, phi_ref, width_out_ref)
 
 
 def short_forward_kernel(
@@ -274,7 +286,7 @@
     upd_ref[...] = updated
 
 
-def readout_kernel(upd_ref, read_ref, out_ref, dupd_ref):
+def readout_gradient(upd_ref, read_ref, out_ref, dupd_ref):
     channel_count, atom_count = upd_ref.shape
     readout = dot(read_ref[...], upd_ref[...], 0, 0, GOOD)
     gate = 1.0 / (1.0 + jnp.exp(-readout))
@@ -331,13 +343,33 @@
     lax.fori_loop(0, chunk, one, 0, unroll=4)
 
 
-def wave_kernel(dims, recv_ref, axes_ref, phi_ref, send_ref, sums, high, low, lifted, coefficients):
+def wave_kernel(
+    dims,
+    recv_ref,
+    axes_ref,
+    phi_ref,
+    width_ref,
+    send_ref,
+    push_ref,
+    high,
+    low,
+    heights,
+    lifted,
+    sums,
+    coefficients,
+):
     own_channels, chunk_count, lengths = dims
-    planes = (high, low, axes_ref, lifted)
+    planes = (high, low, axes_ref, heights, lifted)
+
+    def back():
+        wave_back(own_channels, lengths, high, low, heights, lifted, coefficients, send_ref, push_ref)
+        virial = wave_virial(own_channels, lengths, sums, phi_ref, width_ref, (1, push_ref.shape[2]))
+        push_ref[:, 3, :] = jnp.broadcast_to(virial, (push_ref.shape[0], push_ref.shape[2]))
+
     if chunk_count == 1:
         sums[...] = wave_sums(own_channels, recv_ref, *planes)
         wave_coefficients(sums, phi_ref, coefficients)
-        wave_features(own_channels, *planes, coefficients, send_ref)
+        back()
         return
     phase, chunk_id = pl.program_id(0), pl.program_id(1)
 
@@ -357,38 +389,28 @@
 
     @pl.when(phase == 1)
     def _():
-        wave_features(own_channels, *planes, coefficients, send_ref)
-
-
-def wave_force_kernel(
-    dims, recv_ref, axes_ref, phi_ref, width_ref, sums, push_ref, high, low, lifted, coefficients
-):
-    own_channels, chunk_count, lengths = dims
-    planes = (high, low, axes_ref, lifted)
-    wave_planes(own_channels, recv_ref, *planes)
-    if chunk_count == 1:
-        wave_coefficients(sums, phi_ref, coefficients, True)
-    else:
-
-        @pl.when(pl.program_id(0) == 0)
-        def _():
-            wave_coefficients(sums, phi_ref, coefficients, True)
-
-    wave_back(own_channels, lengths, *planes, coefficients, push_ref)
-    virial = wave_virial(lengths, sums, phi_ref, width_ref, (1, push_ref.shape[2]))
-    push_ref[:, 3, :] = jnp.broadcast_to(virial, (push_ref.shape[0], push_ref.shape[2]))
-
-
-def wave_planes(own_channels, recv_ref, high_ref, low_ref, axes_ref, lifted, devices=None):
-    chunk, _, atom_count = recv_ref.shape
-    lanes = own_channels * HARMONICS
-    for index in devices or range(chunk):
+        back()
+
+
+def wave_planes(own_channels, recv_ref, high_ref, low_ref, axes_ref, heights, lifted, devices):
+    atom_count = recv_ref.shape[2]
+    together, tiles = tile_layout(own_channels)
+    lanes = tiles * HARMONICS
+    sublane = lax.broadcasted_iota(jnp.int32, (HARMONICS, atom_count), 0)
+    for index in devices:
         spot = slice(index * atom_count, (index + 1) * atom_count)
-        for q in range(own_channels):
-            feature = recv_ref[index, q : q + 1, :]
-            for part in range(2):
-                row = part * lanes + q * HARMONICS
-                lifted[row : row + HARMONICS, spot] = feature * axes_ref[4 + part, :, spot]
+        feature = jnp.concatenate([recv_ref[index, 0:own_channels, :]] * together, axis=0)
+        for part in range(2):
+            for tile in range(tiles):
+                first = tile * together
+                height = jnp.broadcast_to(axes_ref[4 + part, first : first + 1, spot], sublane.shape)
+                for n in range(1, together):
+                    height = jnp.where(
+                        sublane >= n * own_channels, axes_ref[4 + part, first + n : first + n + 1, spot], height
+                    )
+                row = part * lanes + tile * HARMONICS
+                heights[row : row + HARMONICS, spot] = height
+                lifted[row : row + HARMONICS, spot] = feature * height
         products = [
             axes_ref[first_axis, m : m + 1, spot] * axes_ref[second_axis, :, spot]
             for first_axis, second_axis in ((0, 2), (0, 3), (1, 2), (1, 3))
@@ -402,14 +424,14 @@
             low_ref[rows, spot] = (both - high.astype(F32)).astype(BF16)
 
 
-def wave_sums(own_channels, recv_ref, high_ref, low_ref, axes_ref, lifted):
+def wave_sums(own_channels, recv_ref, high_ref, low_ref, axes_ref, heights, lifted):
     chunk, _, atom_count = recv_ref.shape
-    lanes = own_channels * HARMONICS
+    lanes = lifted.shape[0] // 2
     group = math.gcd(chunk, 16)
     total = 0.0
     for first in range(0, chunk, group):
         devices = range(first, first + group)
-        wave_planes(own_channels, recv_ref, high_ref, low_ref, axes_ref, lifted, devices)
+        wave_planes(own_channels, recv_ref, high_ref, low_ref, axes_ref, heights, lifted, devices)
         spot = slice(first * atom_count, (first + group) * atom_count)
         values = lifted[:, spot]
         high = values.astype(BF16)
@@ -435,7 +457,7 @@
         yield s1, s2, phi * real, phi * imag, real, imag
 
 
-def wave_virial(lengths, sums_ref, phi_ref, width_ref, shape):
+def wave_virial(own_channels, lengths, sums_ref, phi_ref, width_ref, shape):
     _, rows, lanes = phi_ref.shape
     even = first_odd = second_odd = both_odd = jnp.zeros((rows, lanes), F32)
     for s1, s2, dreal, dimag, real, imag in wave_blocks(sums_ref, phi_ref):
@@ -445,7 +467,7 @@
         second_odd = second_odd + s2 * power
         both_odd = both_odd + s1 * s2 * power
     width = width_ref[0:1, :]
-    k1, k2, k3 = grid_numbers(rows, lanes, lengths)
+    k1, k2, k3 = grid_numbers(rows, lanes, own_channels, lengths)
 
     def total_of(values):
         return jnp.sum(jnp.sum(values, axis=0, keepdims=True), axis=1, keepdims=True)
@@ -463,7 +485,7 @@
     return virial_row(terms, shape)
 
 
-def wave_coefficients(sums_ref, phi_ref, coefficients_ref, gradients=False):
+def wave_coefficients(sums_ref, phi_ref, coefficients_ref):
     _, rows, lanes = phi_ref.shape
     zero = jnp.zeros((rows, lanes), F32)
     d_cc_c = d_cc_s = d_cs_c = d_cs_s = d_sc_c = d_sc_s = d_ss_c = d_ss_s = zero
@@ -479,14 +501,13 @@
         ],
         axis=0,
     )
-    if gradients:
-        cc, cs, sc, ss = (values[p * rows : (p + 1) * rows] for p in range(4))
-        row_id = lax.broadcasted_iota(jnp.int32, (rows, 2 * lanes), 0)
-        m1 = (row_id // HARMONICS).astype(F32)
-        m2 = (row_id % HARMONICS).astype(F32)
-        along_x = jnp.concatenate([m1 * sc, m1 * ss, -m1 * cc, -m1 * cs], axis=0)
-        along_y = jnp.concatenate([m2 * cs, -m2 * cc, m2 * ss, -m2 * sc], axis=0)
-        values = jnp.concatenate([values, along_x, along_y], axis=1)
+    cc, cs, sc, ss = (values[p * rows : (p + 1) * rows] for p in range(4))
+    row_id = lax.broadcasted_iota(jnp.int32, (rows, 2 * lanes), 0)
+    m1 = (row_id // HARMONICS).astype(F32)
+    m2 = (row_id % HARMONICS).astype(F32)
+    along_x = jnp.concatenate([m1 * sc, m1 * ss, -m1 * cc, -m1 * cs], axis=0)
+    along_y = jnp.concatenate([m2 * cs, -m2 * cc, m2 * ss, -m2 * sc], axis=0)
+    values = jnp.concatenate([values, along_x, along_y], axis=1)
     turned = values.T
     high = turned.astype(BF16)
     count = turned.shape[0]
@@ -501,43 +522,36 @@
     return main[:count] + (main[count:] + dot(values[:count], low_ref[...], 1, 0))
 
 
-def wave_features(own_channels, high_ref, low_ref, axes_ref, lifted, coefficients, send_ref):
-    chunk, _, atom_count = send_ref.shape
-    lanes = own_channels * HARMONICS
-    result = wave_spread(high_ref, low_ref, coefficients)
-    for index in range(chunk):
-        spot = slice(index * atom_count, (index + 1) * atom_count)
-        cos_z, sin_z = axes_ref[4, :, spot], axes_ref[5, :, spot]
-        for q in range(own_channels):
-            a, b = q * HARMONICS, lanes + q * HARMONICS
-            piece = result[a : a + HARMONICS, spot] * cos_z + result[b : b + HARMONICS, spot] * sin_z
-            send_ref[index, q : q + 1, :] = jnp.sum(piece, axis=0, keepdims=True)
-
-
-def wave_back(own_channels, lengths, high_ref, low_ref, axes_ref, lifted, coefficients, push_ref):
+def wave_back(own_channels, lengths, high_ref, low_ref, heights, lifted, coefficients, send_ref, push_ref):
     chunk, _, atom_count = push_ref.shape
-    lanes = own_channels * HARMONICS
-    numbers = lax.broadcasted_iota(jnp.int32, (HARMONICS, atom_count), 0).astype(F32) + 1.0
+    together, tiles = tile_layout(own_channels)
+    lanes = tiles * HARMONICS
+    sublane = lax.broadcasted_iota(jnp.int32, (HARMONICS, atom_count), 0)
+    numbers = [(sublane // own_channels + 1 + tile * together).astype(F32) for tile in range(tiles)]
     result = wave_spread(high_ref, low_ref, coefficients)
     for index in range(chunk):
         spot = slice(index * atom_count, (index + 1) * atom_count)
         part = result[:, spot]
-        grad_x = jnp.zeros((HARMONICS, atom_count), F32)
-        grad_y = grad_x
-        grad_z = grad_x
-        for q in range(own_channels):
-            a, b = q * HARMONICS, lanes + q * HARMONICS
+        feature = grad_x = grad_y = grad_z = jnp.zeros((HARMONICS, atom_count), F32)
+        for tile in range(tiles):
+            a, b = tile * HARMONICS, lanes + tile * HARMONICS
+            on_cos, on_sin = part[a : a + HARMONICS], part[b : b + HARMONICS]
+            feature = feature + on_cos * heights[a : a + HARMONICS, spot] + on_sin * heights[b : b + HARMONICS, spot]
             lift_cos = lifted[a : a + HARMONICS, spot]
             lift_sin = lifted[b : b + HARMONICS, spot]
-            grad_z = grad_z + part[b : b + HARMONICS] * lift_cos - part[a : a + HARMONICS] * lift_sin
+            grad_z = grad_z + numbers[tile] * (on_sin * lift_cos - on_cos * lift_sin)
             a, b = a + 2 * lanes, b + 2 * lanes
             grad_x = grad_x + part[a : a + HARMONICS] * lift_cos + part[b : b + HARMONICS] * lift_sin
             a, b = a + 2 * lanes, b + 2 * lanes
             grad_y = grad_y + part[a : a + HARMONICS] * lift_cos + part[b : b + HARMONICS] * lift_sin
+        total = feature[0:own_channels]
+        for n in range(1, together):
+            total = total + feature[n * own_channels : (n + 1) * own_channels]
+        send_ref[index, 0:own_channels, :] = total
         pieces = (
             grad_x * (2.0 * math.pi / lengths[0]),
             grad_y * (2.0 * math.pi / lengths[1]),
-            grad_z * numbers * (2.0 * math.pi / lengths[2]),
+            grad_z * (2.0 * math.pi / lengths[2]),
         )
         for row, piece in enumerate(pieces):
             push_ref[index, row : row + 1, :] = jnp.sum(piece, axis=0, keepdims=True)
@@ -675,7 +689,7 @@
     lengths = (CELL_EDGE * row_count, CELL_EDGE * col_count, HEIGHT)
     volume = lengths[0] * lengths[1] * lengths[2]
     rows = (KMAX + 1) * HARMONICS
-    lanes = own_channels * HARMONICS
+    lanes = tile_layout(own_channels)[1] * HARMONICS
     _, shared = direction_slots(row_count, col_count)
     slab_first = round_up(4 + shared, 2) // 2 * atom_count
     slab_features = round_up(own_channels, 4)
@@ -710,16 +724,19 @@
         w_mix,
         w_read,
         w_out.reshape(1, -1),
-        filter_gain,
-        wave_numbers,
-        amplitude.reshape(1, -1),
-        kernel_width.reshape(1, -1),
     )
+    wave_inputs = (filter_gain, wave_numbers, amplitude.reshape(1, -1), kernel_width.reshape(1, -1))
+
+    def fetched(*arrays):
+        return [pltpu.with_memory_space_constraint(x, pltpu.HBM) for x in arrays]
+
+    kept = pl.BlockSpec(memory_space=pltpu.HBM)
+    near = pl.BlockSpec(memory_space=pltpu.VMEM)
     send, *inputs = call(
         functools.partial(pack_kernel, mesh_counts, len(inputs)),
         (shape(device_count, 2, slab_first),)
         + tuple(jax.ShapeDtypeStruct(x.shape, x.dtype) for x in inputs),
-        in_specs=[pl.BlockSpec(memory_space=pltpu.HBM)] * (3 + len(inputs)),
+        in_specs=[kept] * (3 + len(inputs)),
         scratch_shapes=[
             scratch(3, 1, atom_count),
             pltpu.VMEM((1, atom_count), jnp.int32),
@@ -728,13 +745,8 @@
             pltpu.SemaphoreType.DMA((len(inputs),)),
         ],
         name="pack",
-    )(
-        *[
-            pltpu.with_memory_space_constraint(x, pltpu.HBM)
-            for x in (positions.reshape(3, 1, atom_count), species.reshape(1, atom_count), ghosts, *inputs)
-        ]
-    )
-    live, ids, w_radial, embedding, w_mix, w_read, w_out, *wave_inputs = inputs
+    )(*fetched(positions.reshape(3, 1, atom_count), species.reshape(1, atom_count), ghosts, *inputs))
+    live, ids, w_radial, embedding, w_mix, w_read, w_out = inputs
     cells = exchange(send)
 
     pooled_rows = species_count * radial_count
@@ -758,51 +770,56 @@
         ],
         name="short_forward",
     )(cells, live, ids, w_radial, embedding, w_mix)
-    send, cells, updated, *wave_inputs = lax.optimization_barrier((send, cells, updated, *wave_inputs))
+    send, cells, updated = lax.optimization_barrier((send, cells, updated))
     features = exchange(send)
 
-    phi, width, back = call(
+    axes_block = (6, HARMONICS, chunk * atom_count)
+    axes_shape = shape(6, HARMONICS, device_count * atom_count)
+    table_dims = (col_count, chunk_count, lengths)
+    cells_inputs, axes_outputs = (), ()
+    if chunk_count == 1:
+        cells_inputs, axes_outputs = (cells,), (axes_shape,)
+    dupd, back, phi, width, *axes = call(
         functools.partial(
-            weights_kernel, (device_count, channel_count, own_channels, lengths, volume), slot_count
+            weights_kernel,
+            (device_count, channel_count, own_channels, lengths, volume),
+            slot_count,
+            table_dims if chunk_count == 1 else None,
         ),
-        (shape(4, rows, lanes), shape(8, lanes), shape(pooled_rows, channel_count)),
+        (
+            shape(channel_count, atom_count),
+            shape(pooled_rows, channel_count),
+            shape(4, rows, lanes),
+            shape(8, lanes),
+        )
+        + axes_outputs,
+        in_specs=[near] * (5 + len(cells_inputs)) + [kept] * len(wave_inputs),
+        scratch_shapes=[pltpu.VMEM(x.shape, x.dtype) for x in wave_inputs]
+        + [pltpu.SemaphoreType.DMA((len(wave_inputs),))],
         cost_estimate=pl.CostEstimate(
             flops=2 * 4 * rows * filter_gain.shape[0] * 3 * lanes,
             bytes_accessed=4 * filter_gain.size,
             transcendentals=0,
         ),
         name="weights",
-    )(*wave_inputs, w_radial, embedding)
-
-    axes_block = (6, HARMONICS, chunk * atom_count)
-    if chunk_count == 1:
-        table_options = {}
-    else:
-        table_options = dict(
-            grid=(chunk_count,),
-            in_specs=[pl.BlockSpec((chunk, 2, slab_first), lambda i: (i, 0, 0))],
-            out_specs=pl.BlockSpec(axes_block, lambda i: (0, 0, i)),
-        )
-    axes = call(
-        functools.partial(table_kernel, (col_count, chunk_count, lengths)),
-        shape(6, HARMONICS, device_count * atom_count),
-        cost_estimate=pl.CostEstimate(
-            flops=2000 * device_count * atom_count, bytes_accessed=200 * device_count * atom_count, transcendentals=0
-        ),
-        name="tables",
-        **table_options,
-    )(cells)
-    dupd = call(readout_kernel, shape(channel_count, atom_count), name="readout")(
-        updated, w_read, w_out
-    )
-
-    features, dupd, phi = lax.optimization_barrier((features, dupd, phi))
+    )(updated, w_read, w_out, w_radial, embedding, *cells_inputs, *fetched(*wave_inputs))
+    if chunk_count > 1:
+        axes = [
+            call(
+                functools.partial(table_kernel, table_dims),
+                axes_shape,
+                grid=(chunk_count,),
+                in_specs=[pl.BlockSpec((chunk, 2, slab_first), lambda i: (i, 0, 0))],
+                out_specs=pl.BlockSpec(axes_block, lambda i: (0, 0, i)),
+                name="tables",
+            )(cells)
+        ]
+    features, dupd, back = lax.optimization_barrier((features, dupd, back))
 
     plane = pltpu.VMEM((4 * rows, chunk * atom_count), BF16)
-    wave_scratch = [plane, plane, scratch(2 * lanes, chunk * atom_count)]
-    sums_shape = (4 * rows, 2 * lanes)
+    wave_scratch = [plane, plane] + [scratch(2 * lanes, chunk * atom_count)] * 2
     features_block = (chunk, slab_features, atom_count)
-    wave_options, force_options = {}, {}
+    wave_options = {}
     if chunk_count > 1:
         wave_options = dict(
             grid=(2, chunk_count),
@@ -810,47 +827,23 @@
                 pl.BlockSpec(features_block, lambda p, i: (i, 0, 0)),
                 pl.BlockSpec(axes_block, lambda p, i: (0, 0, i)),
                 pl.BlockSpec((4, rows, lanes), lambda p, i: (0, 0, 0)),
+                pl.BlockSpec((8, lanes), lambda p, i: (0, 0)),
             ],
             out_specs=(
                 pl.BlockSpec(features_block, lambda p, i: (i * p, 0, 0)),
-                pl.BlockSpec(sums_shape, lambda p, i: (0, 0)),
+                pl.BlockSpec((chunk, 4, atom_count), lambda p, i: (i * p, 0, 0)),
             ),
         )
-        force_options = dict(
-            grid=(chunk_count,),
-            in_specs=[
-                pl.BlockSpec(features_block, lambda i: (i, 0, 0)),
-                pl.BlockSpec(axes_block, lambda i: (0, 0, i)),
-                pl.BlockSpec((4, rows, lanes), lambda i: (0, 0, 0)),
-                pl.BlockSpec((8, lanes), lambda i: (0, 0)),
-                pl.BlockSpec(sums_shape, lambda i: (0, 0)),
-            ],
-            out_specs=pl.BlockSpec((chunk, 4, atom_count), lambda i: (i, 0, 0)),
-        )
-    wave_dims = (own_channels, chunk_count, lengths)
-    send, sums = call(
-        functools.partial(wave_kernel, wave_dims),
-        (shape(device_count, slab_features, atom_count), shape(*sums_shape)),
-        vmem=20,
-        scratch_shapes=wave_scratch + [pltpu.VMEM((4 * lanes, 4 * rows), BF16)],
+    send, push = call(
+        functools.partial(wave_kernel, (own_channels, chunk_count, lengths)),
+        (shape(device_count, slab_features, atom_count), shape(device_count, 4, atom_count)),
+        vmem=32,
+        scratch_shapes=wave_scratch
+        + [scratch(4 * rows, 2 * lanes), pltpu.VMEM((12 * lanes, 4 * rows), BF16)],
         name="waves",
         **wave_options,
-    )(features, axes, phi)
+    )(features, *axes, phi, width)
     gradients = exchange(send)
-
-    push = call(
-        functools.partial(wave_force_kernel, wave_dims),
-        shape(device_count, 4, atom_count),
-        vmem=32,
-        scratch_shapes=wave_scratch + [pltpu.VMEM((12 * lanes, 4 * rows), BF16)],
-        cost_estimate=pl.CostEstimate(
-            flops=24 * lanes * 4 * rows * device_count * atom_count,
-            bytes_accessed=200 * device_count * atom_count,
-            transcendentals=0,
-        ),
-        name="wave_forces",
-        **force_options,
-    )(features, axes, phi, width, sums)
 
     send = call(
         functools.partial(

time: 54.7 us -> 53.5 us (0.978)
  blocking collectives: 24.5 us -> 33.8 us
  waiting for transfers between devices: 10.4 us -> 5.3 us
  Pallas kernels: 13.7 us -> 10.8 us
  starting transfers between devices: 5.14 us -> 2.57 us
    all_to_all x2 -> x3, blocking collectives: 24.5 us -> 33.8 us  [exchange(): return lax.all_to_all(slabs, AXES, 0, 0, tiled=True)]
    all_to_all x2 -> x1, waiting for transfers between devices: 10.4 us -> 5.3 us  [exchange(): return lax.all_to_all(slabs, AXES, 0, 0, tiled=True)]
    pallas_call x4 -> x1, Pallas kernels: 6.81 us -> 3.11 us  [per_device(): call(functools.partial(wave_kernel, (own_channels, chunk_count, lengths))...]
    all_to_all x2 -> x1, starting transfers between devices: 5.14 us -> 2.57 us  [exchange(): return lax.all_to_all(slabs, AXES, 0, 0, tiled=True)]
    pallas_call x1, Pallas kernels: 1.14 us -> 2.3 us  [per_device(): call(functools.partial(weights_kernel, (device_count, channel_count, own_...]
  transfers between devices with their start and end apart: 2 -> 1, of which waited for: 2 -> 1; matrix products, arithmetic and copies ran while one was open for 0% -> 0% of each run, Pallas kernels for 9% -> 4%
where the time goes in v5:
time: 53.5 us; the launch traced here: 53.2 us
  blocking collectives  33.8 us (63%)
  Pallas kernels  10.8 us (20%)
  waiting for transfers between devices  5.3 us (10%)
  starting transfers between devices  2.57 us (5%)
  between operations  0.67 us (1%)
    all_to_all x3, blocking collectives, exchange(): return lax.all_to_all(slabs, AXES, 0, 0, tiled=True)  33.8 us
    all_to_all x1, waiting for transfers between devices, exchange(): return lax.all_to_all(slabs, AXES, 0, 0, tiled=True)  5.3 us
    pallas_call x1, Pallas kernels, per_device(): call(functools.partial(wave_kernel, (own_channels, chunk_count, lengths))...  3.11 us
    all_to_all x1, starting transfers between devices, exchange(): return lax.all_to_all(slabs, AXES, 0, 0, tiled=True)  2.57 us
    pallas_call x1, Pallas kernels, per_device(): call(functools.partial(weights_kernel, (device_count, channel_count, own_...  2.3 us
    pallas_call x1, Pallas kernels, per_device(): call(functools.partial(short_forward_kernel, (own_channels,) + mesh_count...  2.17 us
    pallas_call x1, Pallas kernels, per_device(): call(functools.partial(short_back_kernel, (own_channels,) + mesh_counts +...  1.51 us
  transfers between devices with their start and end apart: 1, of which 1 were waited for; matrix products, arithmetic and copies ran while one was open for 0% of the time, Pallas kernels for 4%

profile of v5, /device:TPU:0, one launch (start us, length us, event | category | flops | bytes accessed | tf_op | source)
XLA Modules:
  0.0 53.2 jit_solution(2841059244465069296)
XLA Ops:
  0.6 1.1 %pack.1 = (f32[32,2,384]{2,1,0:T(2,128)S(1)}, s32[1,128]{1,0:T(1,128)S(1)}, s32[64,128]{1,0:T(8,128)S(1)}, f32[16,128]{1,0:T(8,128)S(1)}, f32[6,128]{1,0:T(8,128...) custom-call(f32[3,1,128]{2,1,0:T(1,128)} %bitcast.13, s32[1,128]{1,0:T(1,128)} %bitcast.14, ...), custom_call_target="tpu_custom_call" | custom-call | tf_op jit(solution)/shard_map/pack/pallas_call | solution.py:735
  1.7 15.2 %all_to_all.20.cells_ref.refs_0_ = f32[32,2,384]{2,1,0:T(2,128)S(1)} all-to-all(f32[32,2,384]{2,1,0:T(2,128)S(1)} %get-tuple-element.31), channel_id=1, replica_groups=mesh['row'=16,'col'=2] {'row','col'}, dimensions={0} | all-to-all | bytes 196608 | tf_op jit(solution)/shard_map/all_to_all | solution.py:700
  16.9 2.2 %short_forward.1 = (f32[32,4,128]{2,1,0:T(4,128)}, f32[3,64,128]{2,1,0:T(8,128)S(1)}, f32[64,128]{1,0:T(8,128)S(1)}, s32[64,128]{1,0:T(8,128)S(1)}, f32[128,128]{1,0:T(8,128)S(1)}, /*index=5*/f32[128,128]{1,0:T(8,128)S(1)}) custom-call(f32[32,2,384]{2,1,0:T(2,128)S(1)} %all_to_all.20.cells_ref.refs_0_, s32[1,128]{1,0:T(1,128)S(1)} %get-tuple-element.32.counts_ref, ...), custom_call_target="tpu_custom_call" | custom-call | tf_op jit(solution)/shard_map/short_forward/pallas_call | solution.py:753
  19.1 2.6 %all-to-all-start.1 = ((f32[32,4,128]{2,1,0:T(4,128)}), f32[32,4,128]{2,1,0:T(4,128)S(1)}, u32[]{:S(2)}, u32[]{:S(2)}) async-start(f32[32,4,128]{2,1,0:T(4,128)} %get-tuple-element.39), calls=%async_computation.1 | async-start | bytes 131072 | tf_op jit(solution)/shard_map/all_to_all | solution.py:700
  21.7 2.3 %weights.1 = (f32[128,128]{1,0:T(8,128)S(1)}, f32[96,128]{1,0:T(8,128)S(1)}, f32[4,56,24]{2,1,0:T(8,128)S(1)}, f32[8,24]{1,0:T(8,128)S(1)}, f32[6,8,4096]{2,1,0:T(8,128)S(1)}) custom-call(f32[128,128]{1,0:T(8,128)S(1)} %get-tuple-element.40.upd_ref, f32[128,128]{1,0:T(8,128)S(1)} %get-tuple-element.41.read_ref, f32[1,128]{1,0:T(1,128)S(1)} %get-tuple-element.42.out_ref, ...), custom_call_target="tpu_custom_call" | custom-call | flops 32256000 | bytes 512000 | tf_op jit(solution)/shard_map/weights/pallas_call | solution.py:782
  24.0 5.3 %all-to-all-done.1.recv_ref = f32[32,4,128]{2,1,0:T(4,128)S(1)} async-done(((f32[32,4,128]{2,1,0:T(4,128)}), f32[32,4,128]{2,1,0:T(4,128)S(1)}, u32[]{:S(2)}, u32[]{:S(2)}) %all-to-all-start.1) | async-done | bytes 65568 | tf_op jit(solution)/shard_map/all_to_all | solution.py:700
  29.3 3.1 %waves.1 = (f32[32,4,128]{2,1,0:T(4,128)S(1)}, f32[32,4,128]{2,1,0:T(4,128)S(1)}) custom-call(f32[32,4,128]{2,1,0:T(4,128)S(1)} %all-to-all-done.1.recv_ref, f32[6,8,4096]{2,1,0:T(8,128)S(1)} %get-tuple-element.47.axes_ref, f32[4,56,24]{2,1,0:T(8,128)S(1)} %get-tuple-element.48.phi_ref, f32[8,24]{1,0:T(8,128)S(1)} %get-tuple-element.49.width_ref), custom_call_target="tpu_custom_call" | custom-call | tf_op jit(solution)/shard_map/waves/pallas_call | solution.py:837
  32.4 9.3 %all_to_all.21.recv_ref = f32[32,4,128]{2,1,0:T(4,128)S(1)} all-to-all(f32[32,4,128]{2,1,0:T(4,128)S(1)} %get-tuple-element.50), channel_id=1, replica_groups=mesh['row'=16,'col'=2] {'row','col'}, dimensions={0} | all-to-all | bytes 131072 | tf_op jit(solution)/shard_map/all_to_all | solution.py:700
  41.7 1.5 %short_back.1 = f32[32,4,128]{2,1,0:T(4,128)S(1)} custom-call(f32[32,4,128]{2,1,0:T(4,128)S(1)} %all_to_all.21.recv_ref, f32[3,64,128]{2,1,0:T(8,128)S(1)} %get-tuple-element.51.vec_ref, f32[64,128]{1,0:T(8,128)S(1)} %get-tuple-element.52.kind_ref, f32[128,128]{1,0:T(8,128)S(1)} %get-tuple-element.53.dupd_ref, f32[128,128]{1,0:T(8,128)S(1)} %get-tuple-element.54.slope_ref, ...), custom_call_target="tpu_custom_call" | custom-call | tf_op jit(solution)/shard_map/short_back/pallas_call | solution.py:848
  43.2 9.3 %all_to_all.22.recv_ref = f32[32,4,128]{2,1,0:T(4,128)S(1)} all-to-all(f32[32,4,128]{2,1,0:T(4,128)S(1)} %short_back.1), channel_id=1, replica_groups=mesh['row'=16,'col'=2] {'row','col'}, dimensions={0} | all-to-all | bytes 131072 | tf_op jit(solution)/shard_map/all_to_all | solution.py:700
  52.5 0.7 %total.1 = (f32[3,1,128]{2,1,0:T(1,128)}, f32[3,3]{1,0:T(4,128)}) custom-call(f32[32,4,128]{2,1,0:T(4,128)S(1)} %all_to_all.22.recv_ref), custom_call_target="tpu_custom_call" | custom-call | tf_op jit(solution)/shard_map/total/pallas_call | solution.py:862
Async XLA Ops:
  19.1 10.2 %all-to-all-start.1 = ((f32[32,4,128]{2,1,0:T(4,128)}), f32[32,4,128]{2,1,0:T(4,128)S(1)}, u32[]{:S(2)}, u32[]{:S(2)}) async-start(f32[32,4,128]{2,1,0:T(4,128)} %get-tuple-element.39), calls=%async_computation.1 | async-start | bytes 131072 | tf_op jit(solution)/shard_map/all_to_all | solution.py:700

commit v6 on v5

--- a/solution.py
+++ b/solution.py
@@ -158,27 +158,24 @@
     return copies
 
 
-def weights_kernel(dims, slot_count, table_dims, upd_ref, read_ref, out_ref, radial_ref, embed_ref, *refs):
-    cells, refs = refs[: len(refs) - 13 - bool(table_dims)], refs[len(refs) - 13 - bool(table_dims) :]
-    sources, (dupd_ref, back_ref, phi_ref, width_out_ref), refs = refs[:4], refs[4:8], refs[8:]
-    axes, targets, sems = refs[: len(refs) - 5], refs[-5:-1], refs[-1]
+def weights_kernel(dims, table_dims, upd_ref, mixed_ref, *refs):
+    cells, refs = refs[: len(refs) - 17 - bool(table_dims)], refs[len(refs) - 17 - bool(table_dims) :]
+    sources, (dupd_ref, back_ref, phi_ref, width_out_ref), refs = refs[:6], refs[6:10], refs[10:]
+    axes, targets, sems = refs[: len(refs) - 7], refs[-7:-1], refs[-1]
     copies = start_copies(tuple(zip(sources, targets)), sems)
     if table_dims:
         table_kernel(table_dims, *cells, *axes)
-    readout_gradient(upd_ref, read_ref, out_ref, dupd_ref)
-    species_count, channel_count = embed_ref.shape
-    radial_count = radial_ref.shape[0]
-    order_id = lax.broadcasted_iota(jnp.int32, (radial_count, channel_count), 0)
-    factor = jnp.zeros((radial_count, channel_count), F32)
+    pooled_rows, channel_count = mixed_ref.shape
+    radial_count = dims[5]
+    order_id = lax.broadcasted_iota(jnp.int32, (pooled_rows, channel_count), 0) % radial_count
+    factor = jnp.zeros((pooled_rows, channel_count), F32)
     for order in range(radial_count):
-        factor = jnp.where(order_id == order, -2.0 * radial_rate(order) / slot_count, factor)
-    for k in range(species_count):
-        back_ref[k * radial_count : (k + 1) * radial_count, :] = (
-            radial_ref[...] * embed_ref[k : k + 1, :] * factor
-        )
+        factor = jnp.where(order_id == order, -2.0 * radial_rate(order), factor)
+    back_ref[...] = mixed_ref[...] * factor
     for copy in copies:
         copy.wait()
-    wave_weights(dims, *targets, phi_ref, width_out_ref)
+    readout_gradient(upd_ref, targets[0], targets[1], dupd_ref)
+    wave_weights(dims[:5], *targets[2:], phi_ref, width_out_ref)
 
 
 def short_forward_kernel(
@@ -195,6 +192,7 @@
     owner_ref,
     upd_ref,
     slope_ref,
+    mixed_ref,
     table,
     lists,
     codes,
@@ -208,6 +206,12 @@
     radial_count = radial_ref.shape[0]
     device_count = send_ref.shape[0]
     slots, _ = direction_slots(row_count, col_count)
+    for k in range(species_count):
+        weights[k * radial_count : (k + 1) * radial_count, :] = (
+            radial_ref[...] * embed_ref[k : k + 1, :] * (1.0 / slot_count)
+        )
+    weights[...] = dot(weights[...], mix_ref[...], 1, 0, EXACT)
+    mixed_ref[...] = weights[...]
     own = slab_rows(cells_ref[neighbour_of((0, 0), row_count, col_count)], range(4), atom_count)
     for part in range(4):
         table[part, 0:1, :] = own[part]
@@ -261,18 +265,13 @@
             pooled[spot : spot + 1, :] = jnp.sum(
                 jnp.where(masks[k], basis, 0.0), axis=0, keepdims=True
             )
-    for k in range(species_count):
-        weights[k * radial_count : (k + 1) * radial_count, :] = (
-            radial_ref[...] * embed_ref[k : k + 1, :] * (1.0 / slot_count)
-        )
     kinds8[...] = jnp.zeros_like(kinds8)
     kinds8[0:species_count, :] = embed_ref[...]
     own_hot = (
         lax.broadcasted_iota(jnp.int32, (kinds8.shape[0], atom_count), 0).astype(F32) == own[3]
     ).astype(F32)
     initial = dot(kinds8[...], own_hot, 0, 0, EXACT)
-    aggregate = dot(weights[...], pooled[...], 0, 0, GOOD)
-    before = dot(mix_ref[...], aggregate, 0, 0, GOOD)
+    before = dot(weights[...], pooled[...], 0, 0, GOOD)
     gate = 1.0 / (1.0 + jnp.exp(-before))
     updated = initial + before * gate
     slope_ref[...] = gate + before * gate * (1.0 - gate)
@@ -351,18 +350,17 @@
     width_ref,
     send_ref,
     push_ref,
-    high,
-    low,
+    planes_ref,
     heights,
     lifted,
     sums,
     coefficients,
 ):
     own_channels, chunk_count, lengths = dims
-    planes = (high, low, axes_ref, heights, lifted)
+    planes = (planes_ref, axes_ref, heights, lifted)
 
     def back():
-        wave_back(own_channels, lengths, high, low, heights, lifted, coefficients, send_ref, push_ref)
+        wave_back(own_channels, lengths, planes_ref, heights, lifted, coefficients, send_ref, push_ref)
         virial = wave_virial(own_channels, lengths, sums, phi_ref, width_ref, (1, push_ref.shape[2]))
         push_ref[:, 3, :] = jnp.broadcast_to(virial, (push_ref.shape[0], push_ref.shape[2]))
 
@@ -392,11 +390,12 @@
         back()
 
 
-def wave_planes(own_channels, recv_ref, high_ref, low_ref, axes_ref, heights, lifted, devices):
+def wave_planes(own_channels, recv_ref, planes_ref, axes_ref, heights, lifted, devices):
     atom_count = recv_ref.shape[2]
     together, tiles = tile_layout(own_channels)
     lanes = tiles * HARMONICS
     sublane = lax.broadcasted_iota(jnp.int32, (HARMONICS, atom_count), 0)
+    count = planes_ref.shape[0] // 2
     for index in devices:
         spot = slice(index * atom_count, (index + 1) * atom_count)
         feature = jnp.concatenate([recv_ref[index, 0:own_channels, :]] * together, axis=0)
@@ -420,24 +419,26 @@
             both = jnp.concatenate(products[2 * pair : 2 * pair + 2], axis=0)
             high = both.astype(BF16)
             rows = slice(2 * HARMONICS * pair, 2 * HARMONICS * (pair + 1))
-            high_ref[rows, spot] = high
-            low_ref[rows, spot] = (both - high.astype(F32)).astype(BF16)
-
-
-def wave_sums(own_channels, recv_ref, high_ref, low_ref, axes_ref, heights, lifted):
+            planes_ref[rows, spot] = high
+            rows = slice(count + rows.start, count + rows.stop)
+            planes_ref[rows, spot] = (both - high.astype(F32)).astype(BF16)
+
+
+def wave_sums(own_channels, recv_ref, planes_ref, axes_ref, heights, lifted):
     chunk, _, atom_count = recv_ref.shape
     lanes = lifted.shape[0] // 2
     group = math.gcd(chunk, 16)
+    count = planes_ref.shape[0] // 2
     total = 0.0
     for first in range(0, chunk, group):
         devices = range(first, first + group)
-        wave_planes(own_channels, recv_ref, high_ref, low_ref, axes_ref, heights, lifted, devices)
+        wave_planes(own_channels, recv_ref, planes_ref, axes_ref, heights, lifted, devices)
         spot = slice(first * atom_count, (first + group) * atom_count)
         values = lifted[:, spot]
         high = values.astype(BF16)
         low = (values - high.astype(F32)).astype(BF16)
-        main = dot(high_ref[:, spot], jnp.concatenate([high, low], axis=0), 1, 1)
-        total = total + main[:, : 2 * lanes] + (main[:, 2 * lanes :] + dot(low_ref[:, spot], high, 1, 1))
+        main = dot(planes_ref[0:count, spot], jnp.concatenate([high, low], axis=0), 1, 1)
+        total = total + main[:, : 2 * lanes] + (main[:, 2 * lanes :] + dot(planes_ref[count:, spot], high, 1, 1))
     return total
 
 
@@ -515,20 +516,20 @@
     coefficients_ref[count:, :] = (turned - high.astype(F32)).astype(BF16)
 
 
-def wave_spread(high_ref, low_ref, coefficients):
+def wave_spread(planes_ref, coefficients):
     values = coefficients[...]
     count = values.shape[0] // 2
-    main = dot(values, high_ref[...], 1, 0)
-    return main[:count] + (main[count:] + dot(values[:count], low_ref[...], 1, 0))
-
-
-def wave_back(own_channels, lengths, high_ref, low_ref, heights, lifted, coefficients, send_ref, push_ref):
+    both = jnp.concatenate([values[:count], values[:count]], axis=1)
+    return dot(both, planes_ref[...], 1, 0) + dot(values[count:], planes_ref[0 : values.shape[1], :], 1, 0)
+
+
+def wave_back(own_channels, lengths, planes_ref, heights, lifted, coefficients, send_ref, push_ref):
     chunk, _, atom_count = push_ref.shape
     together, tiles = tile_layout(own_channels)
     lanes = tiles * HARMONICS
     sublane = lax.broadcasted_iota(jnp.int32, (HARMONICS, atom_count), 0)
     numbers = [(sublane // own_channels + 1 + tile * together).astype(F32) for tile in range(tiles)]
-    result = wave_spread(high_ref, low_ref, coefficients)
+    result = wave_spread(planes_ref, coefficients)
     for index in range(chunk):
         spot = slice(index * atom_count, (index + 1) * atom_count)
         part = result[:, spot]
@@ -575,7 +576,6 @@
     slope_ref,
     owner_ref,
     back_ref,
-    mix_ref,
     push_ref,
     send_ref,
     fgrad,
@@ -584,15 +584,14 @@
 ):
     own_channels, row_count, col_count, species_count, radial_count = dims
     slot_count, atom_count = owner_ref.shape
-    channel_count = mix_ref.shape[0]
+    channel_count = back_ref.shape[1]
     device_count = send_ref.shape[0]
     table_rows = round_up(len(DIRECTIONS) + 1, 16)
     for q in range(own_channels):
         low, high = q * device_count, min(channel_count, (q + 1) * device_count)
         fgrad[low:high, :] = recv_ref[0 : high - low, q, :]
     dbefore = (fgrad[...] + dupd_ref[...]) * slope_ref[...]
-    daggregate = dot(mix_ref[...], dbefore, 1, 0, GOOD)
-    dpool[...] = dot(back_ref[...], daggregate, 1, 0, GOOD)
+    dpool[...] = dot(back_ref[...], dbefore, 1, 0, GOOD)
     vectors = [vec_ref[part] for part in range(3)]
     squared = vectors[0] * vectors[0] + vectors[1] * vectors[1] + vectors[2] * vectors[2]
     kind = kind_ref[...]
@@ -722,10 +721,15 @@
         w_radial,
         embedding,
         w_mix,
+    )
+    wave_inputs = (
         w_read,
         w_out.reshape(1, -1),
+        filter_gain,
+        wave_numbers,
+        amplitude.reshape(1, -1),
+        kernel_width.reshape(1, -1),
     )
-    wave_inputs = (filter_gain, wave_numbers, amplitude.reshape(1, -1), kernel_width.reshape(1, -1))
 
     def fetched(*arrays):
         return [pltpu.with_memory_space_constraint(x, pltpu.HBM) for x in arrays]
@@ -746,11 +750,11 @@
         ],
         name="pack",
     )(*fetched(positions.reshape(3, 1, atom_count), species.reshape(1, atom_count), ghosts, *inputs))
-    live, ids, w_radial, embedding, w_mix, w_read, w_out = inputs
+    live, ids, w_radial, embedding, w_mix = inputs
     cells = exchange(send)
 
     pooled_rows = species_count * radial_count
-    send, vectors, kinds, owners, updated, slope = call(
+    send, vectors, kinds, owners, updated, slope, mixed = call(
         functools.partial(short_forward_kernel, (own_channels,) + mesh_counts),
         (
             shape(device_count, slab_features, atom_count),
@@ -759,6 +763,7 @@
             jax.ShapeDtypeStruct((slot_count, atom_count), jnp.int32),
             shape(channel_count, atom_count),
             shape(channel_count, atom_count),
+            shape(pooled_rows, channel_count),
         ),
         scratch_shapes=[
             scratch(4, 16, atom_count),
@@ -770,7 +775,7 @@
         ],
         name="short_forward",
     )(cells, live, ids, w_radial, embedding, w_mix)
-    send, cells, updated = lax.optimization_barrier((send, cells, updated))
+    send, cells, updated, mixed = lax.optimization_barrier((send, cells, updated, mixed))
     features = exchange(send)
 
     axes_block = (6, HARMONICS, chunk * atom_count)
@@ -782,8 +787,7 @@
     dupd, back, phi, width, *axes = call(
         functools.partial(
             weights_kernel,
-            (device_count, channel_count, own_channels, lengths, volume),
-            slot_count,
+            (device_count, channel_count, own_channels, lengths, volume, radial_count),
             table_dims if chunk_count == 1 else None,
         ),
         (
@@ -793,7 +797,7 @@
             shape(8, lanes),
         )
         + axes_outputs,
-        in_specs=[near] * (5 + len(cells_inputs)) + [kept] * len(wave_inputs),
+        in_specs=[near] * (2 + len(cells_inputs)) + [kept] * len(wave_inputs),
         scratch_shapes=[pltpu.VMEM(x.shape, x.dtype) for x in wave_inputs]
         + [pltpu.SemaphoreType.DMA((len(wave_inputs),))],
         cost_estimate=pl.CostEstimate(
@@ -802,7 +806,7 @@
             transcendentals=0,
         ),
         name="weights",
-    )(updated, w_read, w_out, w_radial, embedding, *cells_inputs, *fetched(*wave_inputs))
+    )(updated, mixed, *cells_inputs, *fetched(*wave_inputs))
     if chunk_count > 1:
         axes = [
             call(
@@ -816,8 +820,8 @@
         ]
     features, dupd, back = lax.optimization_barrier((features, dupd, back))
 
-    plane = pltpu.VMEM((4 * rows, chunk * atom_count), BF16)
-    wave_scratch = [plane, plane] + [scratch(2 * lanes, chunk * atom_count)] * 2
+    plane = pltpu.VMEM((8 * rows, chunk * atom_count), BF16)
+    wave_scratch = [plane] + [scratch(2 * lanes, chunk * atom_count)] * 2
     features_block = (chunk, slab_features, atom_count)
     wave_options = {}
     if chunk_count > 1:
@@ -856,7 +860,7 @@
             scratch(6, slot_count, atom_count),
         ],
         name="short_back",
-    )(gradients, vectors, kinds, dupd, slope, owners, back, w_mix, push)
+    )(gradients, vectors, kinds, dupd, slope, owners, back, push)
     returned = exchange(send)
 
     forces, virial = call(

time: 53.5 us -> 53.2 us (level)
  transfers between devices with their start and end apart: 1 -> 1, of which waited for: 1 -> 1; matrix products, arithmetic and copies ran while one was open for 0% -> 0% of each run, Pallas kernels for 4% -> 5%
where the time goes in v6:
time: 53.2 us; the launch traced here: 52.9 us
  blocking collectives  33.8 us (64%)
  Pallas kernels  10.9 us (20%)
  waiting for transfers between devices  4.98 us (9%)
  starting transfers between devices  2.57 us (5%)
  between operations  0.67 us (1%)
    all_to_all x3, blocking collectives, exchange(): return lax.all_to_all(slabs, AXES, 0, 0, tiled=True)  33.8 us
    all_to_all x1, waiting for transfers between devices, exchange(): return lax.all_to_all(slabs, AXES, 0, 0, tiled=True)  4.98 us
    pallas_call x1, Pallas kernels, per_device(): call(functools.partial(wave_kernel, (own_channels, chunk_count, lengths))...  3.11 us
    pallas_call x1, Pallas kernels, per_device(): call(functools.partial(weights_kernel, (device_count, channel_count, own_...  2.62 us
    all_to_all x1, starting transfers between devices, exchange(): return lax.all_to_all(slabs, AXES, 0, 0, tiled=True)  2.57 us
    pallas_call x1, Pallas kernels, per_device(): call(functools.partial(short_forward_kernel, (own_channels,) + mesh_count...  2.07 us
    pallas_call x1, Pallas kernels, per_device(): call(functools.partial(short_back_kernel, (own_channels,) + mesh_counts +...  1.37 us
  transfers between devices with their start and end apart: 1, of which 1 were waited for; matrix products, arithmetic and copies ran while one was open for 0% of the time, Pallas kernels for 5%

profile of v6, /device:TPU:0, one launch (start us, length us, event | category | flops | bytes accessed | tf_op | source)
XLA Modules:
  0.0 52.9 jit_solution(16019643902817547968)
XLA Ops:
  0.6 1.0 %pack.1 = (f32[32,2,384]{2,1,0:T(2,128)S(1)}, s32[1,128]{1,0:T(1,128)S(1)}, s32[64,128]{1,0:T(8,128)S(1)}, f32[16,128]{1,0:T(8,128)S(1)}, f32[6,128]{1,0:T(8,128)S(1)}, /*index=5*/f32[128,128]{1,0:T(8,128)S(1)}) custom-call(f32[3,1,128]{2,1,0:T(1,128)} %bitcast.13, s32[1,128]{1,0:T(1,128)} %bitcast.14, s32[8,128]{1,0:T(8,128)} %bitcast.12, ...), custom_call_target="tpu_custom_call" | custom-call | tf_op jit(solution)/shard_map/pack/pallas_call | solution.py:739
  1.7 15.2 %all_to_all.20.cells_ref.refs_0_ = f32[32,2,384]{2,1,0:T(2,128)S(1)} all-to-all(f32[32,2,384]{2,1,0:T(2,128)S(1)} %get-tuple-element.31), channel_id=1, replica_groups=mesh['row'=16,'col'=2] {'row','col'}, dimensions={0} | all-to-all | bytes 196608 | tf_op jit(solution)/shard_map/all_to_all | solution.py:699
  16.9 2.1 %short_forward.1 = (f32[32,4,128]{2,1,0:T(4,128)}, f32[3,64,128]{2,1,0:T(8,128)S(1)}, f32[64,128]{1,0:T(8,128)S(1)}, s32[64,128]{1,0:T(8,128)S(1)}, f32[128,128]...) custom-call(f32[32,2,384]{2,1,0:T(2,128)S(1)} %all_to_all.20.cells_ref.refs_0_, ...), custom_call_target="tpu_custom_call" | custom-call | tf_op jit(solution)/shard_map/short_forward/pallas_call | solution.py:757
  18.9 2.6 %all-to-all-start.1 = ((f32[32,4,128]{2,1,0:T(4,128)}), f32[32,4,128]{2,1,0:T(4,128)S(1)}, u32[]{:S(2)}, u32[]{:S(2)}) async-start(f32[32,4,128]{2,1,0:T(4,128)} %get-tuple-element.40), calls=%async_computation.1 | async-start | bytes 131072 | tf_op jit(solution)/shard_map/all_to_all | solution.py:699
  21.5 2.6 %weights.1 = (f32[128,128]{1,0:T(8,128)S(1)}, f32[96,128]{1,0:T(8,128)S(1)}, f32[4,56,24]{2,1,0:T(8,128)S(1)}, f32[8,24]{1,0:T(8,128)S(1)}, f32[6,8,4096]{2,1,0:T(8,128)S(1)}) custom-call(f32[128,128]{1,0:T(8,128)S(1)} %get-tuple-element.41.upd_ref, f32[96,128]{1,0:T(8,128)S(1)} %get-tuple-element.42.mixed_ref, ...), custom_call_target="tpu_custom_call" | custom-call | flops 32256000 | bytes 512000 | tf_op jit(solution)/shard_map/weights/pallas_call | solution.py:787
  24.1 5.0 %all-to-all-done.1.recv_ref = f32[32,4,128]{2,1,0:T(4,128)S(1)} async-done(((f32[32,4,128]{2,1,0:T(4,128)}), f32[32,4,128]{2,1,0:T(4,128)S(1)}, u32[]{:S(2)}, u32[]{:S(2)}) %all-to-all-start.1) | async-done | bytes 65568 | tf_op jit(solution)/shard_map/all_to_all | solution.py:699
  29.1 3.1 %waves.1 = (f32[32,4,128]{2,1,0:T(4,128)S(1)}, f32[32,4,128]{2,1,0:T(4,128)S(1)}) custom-call(f32[32,4,128]{2,1,0:T(4,128)S(1)} %all-to-all-done.1.recv_ref, f32[6,8,4096]{2,1,0:T(8,128)S(1)} %get-tuple-element.47.axes_ref, f32[4,56,24]{2,1,0:T(8,128)S(1)} %get-tuple-element.48.phi_ref, f32[8,24]{1,0:T(8,128)S(1)} %get-tuple-element.49.width_ref), custom_call_target="tpu_custom_call" | custom-call | tf_op jit(solution)/shard_map/waves/pallas_call | solution.py:841
  32.2 9.3 %all_to_all.21.recv_ref = f32[32,4,128]{2,1,0:T(4,128)S(1)} all-to-all(f32[32,4,128]{2,1,0:T(4,128)S(1)} %get-tuple-element.50), channel_id=1, replica_groups=mesh['row'=16,'col'=2] {'row','col'}, dimensions={0} | all-to-all | bytes 131072 | tf_op jit(solution)/shard_map/all_to_all | solution.py:699
  41.6 1.4 %short_back.1 = f32[32,4,128]{2,1,0:T(4,128)S(1)} custom-call(f32[32,4,128]{2,1,0:T(4,128)S(1)} %all_to_all.21.recv_ref, f32[3,64,128]{2,1,0:T(8,128)S(1)} %get-tuple-element.51.vec_ref, f32[64,128]{1,0:T(8,128)S(1)} %get-tuple-element.52.kind_ref, f32[128,128]{1,0:T(8,128)S(1)} %get-tuple-element.53.dupd_ref, f32[128,128]{1,0:T(8,128)S(1)} %get-tuple-element.54.slope_ref, ...), custom_call_target="tpu_custom_call" | custom-call | tf_op jit(solution)/shard_map/short_back/pallas_call | solution.py:852
  42.9 9.3 %all_to_all.22.recv_ref = f32[32,4,128]{2,1,0:T(4,128)S(1)} all-to-all(f32[32,4,128]{2,1,0:T(4,128)S(1)} %short_back.1), channel_id=1, replica_groups=mesh['row'=16,'col'=2] {'row','col'}, dimensions={0} | all-to-all | bytes 131072 | tf_op jit(solution)/shard_map/all_to_all | solution.py:699
  52.2 0.7 %total.1 = (f32[3,1,128]{2,1,0:T(1,128)}, f32[3,3]{1,0:T(4,128)}) custom-call(f32[32,4,128]{2,1,0:T(4,128)S(1)} %all_to_all.22.recv_ref), custom_call_target="tpu_custom_call" | custom-call | tf_op jit(solution)/shard_map/total/pallas_call | solution.py:866
Async XLA Ops:
  18.9 10.2 %all-to-all-start.1 = ((f32[32,4,128]{2,1,0:T(4,128)}), f32[32,4,128]{2,1,0:T(4,128)S(1)}, u32[]{:S(2)}, u32[]{:S(2)}) async-start(f32[32,4,128]{2,1,0:T(4,128)} %get-tuple-element.40), calls=%async_computation.1 | async-start | bytes 131072 | tf_op jit(solution)/shard_map/all_to_all | solution.py:699

commit v7 on v6

--- a/solution.py
+++ b/solution.py
@@ -66,22 +66,23 @@
     together, tiles = tile_layout(own_channels)
     lanes = tiles * HARMONICS
     place = lax.broadcasted_iota(jnp.int32, (8, channel_count), 0) * device_count + me
-    chosen = (lax.broadcasted_iota(jnp.int32, (8, channel_count), 1) == place).astype(F32)
-    own_gain = dot(chosen, gain_ref[...], 1, 1, EXACT)
+    chosen = (lax.broadcasted_iota(jnp.int32, (8, channel_count), 1) == place).astype(F32).astype(BF16)
     first, second, third = waves_ref[0:1, :], waves_ref[1:2, :], waves_ref[2:3, :]
     sign = jnp.where(first < 0, 2, 0) + jnp.where(second < 0, 1, 0)
     key = sign * rows + jnp.abs(first) * HARMONICS + jnp.abs(second)
     spots = lax.broadcasted_iota(jnp.int32, (4 * rows, wave_count), 0) == key
     onehot = jnp.where(spots, 1.0, 0.0).astype(BF16)
-    mine = jnp.concatenate([own_gain[:own_channels]] * together, axis=0)
     height = lax.broadcasted_iota(jnp.int32, (HARMONICS, wave_count), 0) // own_channels + 1
-    blocks = [jnp.where(height + tile * together == third, mine, 0.0) for tile in range(tiles)]
-    wide = jnp.concatenate(blocks, axis=0)
-    high = wide.astype(BF16)
-    rest = wide - high.astype(F32)
-    middle = rest.astype(BF16)
-    low = (rest - middle.astype(F32)).astype(BF16)
-    summed = dot(onehot, high, 1, 1) + (dot(onehot, middle, 1, 1) + dot(onehot, low, 1, 1))
+    here = [height + tile * together == third for tile in range(tiles)]
+    rest = gain_ref[...]
+    summed = 0.0
+    for _ in range(3):
+        part = rest.astype(BF16)
+        rest = rest - part.astype(F32)
+        mine = dot(chosen, part, 1, 1)
+        mine = jnp.concatenate([mine[:own_channels]] * together, axis=0)
+        wide = jnp.concatenate([jnp.where(spots, mine, 0.0) for spots in here], axis=0)
+        summed = summed + dot(onehot, wide.astype(BF16), 1, 1)
     lane = lax.broadcasted_iota(jnp.int32, (8, channel_count), 1)
     wanted = jnp.minimum(lane % own_channels * device_count + me, channel_count - 1)
     amp = jnp.take_along_axis(jnp.broadcast_to(amp_ref[...], (8, channel_count)), wanted, axis=1)
@@ -172,9 +173,11 @@
     for order in range(radial_count):
         factor = jnp.where(order_id == order, -2.0 * radial_rate(order), factor)
     back_ref[...] = mixed_ref[...] * factor
-    for copy in copies:
+    for copy in copies[:2]:
         copy.wait()
     readout_gradient(upd_ref, targets[0], targets[1], dupd_ref)
+    for copy in copies[2:]:
+        copy.wait()
     wave_weights(dims[:5], *targets[2:], phi_ref, width_out_ref)
 
 
@@ -213,22 +216,27 @@
     weights[...] = dot(weights[...], mix_ref[...], 1, 0, EXACT)
     mixed_ref[...] = weights[...]
     own = slab_rows(cells_ref[neighbour_of((0, 0), row_count, col_count)], range(4), atom_count)
-    for part in range(4):
+    domains, places = [], []
+    for step in DIRECTIONS:
+        key = (step[0] % row_count, step[1] % col_count)
+        if key not in domains:
+            domains.append(key)
+        places.append(domains.index(key))
+    for part in range(3):
         table[part, 0:1, :] = own[part]
+    for place, key in enumerate(domains):
+        block = slab_rows(cells_ref[neighbour_of(key, row_count, col_count)], range(3), atom_count)
+        for part in range(3):
+            table[part, 8 + place : 9 + place, :] = block[part]
     for order, step in enumerate(DIRECTIONS):
+        list_row = 4 + slots[len(DIRECTIONS) - 1 - order]
         source = neighbour_of(step, row_count, col_count)
-        list_row = 4 + slots[len(DIRECTIONS) - 1 - order]
-        block = slab_rows(cells_ref[source], (0, 1, 2, 3, list_row), atom_count)
-        row = slice(8 + order, 9 + order)
-        table[0, row, :] = block[0] + step[0] * CELL_EDGE
-        table[1, row, :] = block[1] + step[1] * CELL_EDGE
-        table[2, row, :] = block[2]
-        table[3, row, :] = block[3]
-        lists[order : order + 1, :] = block[4].astype(jnp.int32)
+        kinds_row, list_values = slab_rows(cells_ref[source], (3, list_row), atom_count)
+        table[3, 8 + order : 9 + order, :] = kinds_row
+        lists[order : order + 1, :] = list_values.astype(jnp.int32)
     picks = lists[...]
-    for part in range(4):
-        table[part, 8:16, :] = jnp.take_along_axis(table[part, 8:16, :], picks, axis=1)
-    codes[8:16, :] = picks + atom_count * table[3, 8:16, :].astype(jnp.int32)
+    ghost_kinds = jnp.take_along_axis(table[3, 8:16, :], picks, axis=1)
+    codes[8:16, :] = picks + atom_count * ghost_kinds.astype(jnp.int32)
     codes[0:1, :] = lax.broadcasted_iota(
         jnp.int32, (1, atom_count), 1
     ) + atom_count * own[3].astype(jnp.int32)
@@ -236,18 +244,29 @@
     ids = ids_ref[...]
     lane = ids & (atom_count - 1)
     source = ids // atom_count
-    here = [source == order + 1 for order in range(len(DIRECTIONS))]
-
-    def picked(ref):
-        values = jnp.take_along_axis(jnp.broadcast_to(ref[0:1, :], ids.shape), lane, axis=1)
-        for order in range(len(DIRECTIONS)):
-            wide = jnp.broadcast_to(ref[8 + order : 9 + order, :], ids.shape)
-            values = jnp.where(here[order], jnp.take_along_axis(wide, lane, axis=1), values)
+
+    def picked(ref, index, marks):
+        values = jnp.take_along_axis(jnp.broadcast_to(ref[0:1, :], ids.shape), index, axis=1)
+        for place, mark in enumerate(marks):
+            wide = jnp.broadcast_to(ref[8 + place : 9 + place, :], ids.shape)
+            values = jnp.where(mark, jnp.take_along_axis(wide, index, axis=1), values)
         return values
 
-    gathered = [picked(table.at[part]) for part in range(3)]
-    code = picked(codes)
-    owner_ref[...] = (code & (atom_count - 1)) + source * atom_count
+    marks = [source == order + 1 for order in range(len(DIRECTIONS))]
+    code = picked(codes, lane, marks)
+    owner = code & (atom_count - 1)
+    owner_ref[...] = owner + source * atom_count
+    merged = []
+    for place in range(len(domains)):
+        mine = [mark for mark, other in zip(marks, places) if other == place]
+        merged.append(functools.reduce(jnp.logical_or, mine))
+    gathered = [picked(table.at[part], owner, merged) for part in range(3)]
+    for axis in range(2):
+        shift = jnp.zeros(ids.shape, F32)
+        for mark, step in zip(marks, DIRECTIONS):
+            if step[axis]:
+                shift = jnp.where(mark, step[axis] * CELL_EDGE, shift)
+        gathered[axis] = gathered[axis] + shift
     gathered.append((code // atom_count).astype(F32))
     slot = lax.broadcasted_iota(jnp.int32, ids.shape, 0)
     kind = jnp.where(slot < counts_ref[...], gathered[3], -1.0)

time: 53.2 us -> 53 us (level)
  transfers between devices with their start and end apart: 1 -> 1, of which waited for: 1 -> 1; matrix products, arithmetic and copies ran while one was open for 0% -> 0% of each run, Pallas kernels for 5% -> 4%
where the time goes in v7:
time: 53 us; the launch traced here: 52.7 us
  blocking collectives  33.8 us (64%)
  Pallas kernels  10.4 us (20%)
  waiting for transfers between devices  5.32 us (10%)
  starting transfers between devices  2.57 us (5%)
  between operations  0.67 us (1%)
    all_to_all x3, blocking collectives, exchange(): return lax.all_to_all(slabs, AXES, 0, 0, tiled=True)  33.8 us
    all_to_all x1, waiting for transfers between devices, exchange(): return lax.all_to_all(slabs, AXES, 0, 0, tiled=True)  5.32 us
    pallas_call x1, Pallas kernels, per_device(): call(functools.partial(wave_kernel, (own_channels, chunk_count, lengths))...  3.1 us
    all_to_all x1, starting transfers between devices, exchange(): return lax.all_to_all(slabs, AXES, 0, 0, tiled=True)  2.57 us
    pallas_call x1, Pallas kernels, per_device(): call(functools.partial(weights_kernel, (device_count, channel_count, own_...  2.28 us
    pallas_call x1, Pallas kernels, per_device(): call(functools.partial(short_forward_kernel, (own_channels,) + mesh_count...  1.92 us
    pallas_call x1, Pallas kernels, per_device(): call(functools.partial(short_back_kernel, (own_channels,) + mesh_counts +...  1.36 us
  transfers between devices with their start and end apart: 1, of which 1 were waited for; matrix products, arithmetic and copies ran while one was open for 0% of the time, Pallas kernels for 4%

profile of v7, /device:TPU:0, one launch (start us, length us, event | category | flops | bytes accessed | tf_op | source)
XLA Modules:
  0.0 52.7 jit_solution(6478527969820945994)
XLA Ops:
  0.6 1.0 %pack.1 = (f32[32,2,384]{2,1,0:T(2,128)S(1)}, s32[1,128]{1,0:T(1,128)S(1)}, s32[64,128]{1,0:T(8,128)S(1)}, f32[16,128]{1,0:T(8,128)S(1)}, f32[6,128]{1,0:T(8,128)S(1)}, /*index=5*/f32[128,128]{1,0:T(8,128)S(1)}) custom-call(f32[3,1,128]{2,1,0:T(1,128)} %bitcast.13, s32[1,128]{1,0:T(1,128)} %bitcast.14, s32[8,128]{1,0:T(8,128)} %bitcast.12, ...), custom_call_target="tpu_custom_call" | custom-call | tf_op jit(solution)/shard_map/pack/pallas_call | solution.py:758
  1.7 15.2 %all_to_all.20.cells_ref.refs_0_ = f32[32,2,384]{2,1,0:T(2,128)S(1)} all-to-all(f32[32,2,384]{2,1,0:T(2,128)S(1)} %get-tuple-element.31), channel_id=1, replica_groups=mesh['row'=16,'col'=2] {'row','col'}, dimensions={0} | all-to-all | bytes 196608 | tf_op jit(solution)/shard_map/all_to_all | solution.py:718
  16.9 1.9 %short_forward.1 = (f32[32,4,128]{2,1,0:T(4,128)}, f32[3,64,128]{2,1,0:T(8,128)S(1)}, f32[64,128]{1,0:T(8,128)S(1)}, s32[64,128]{1,0:T(8,128)S(1)}, f32[128,128]...) custom-call(f32[32,2,384]{2,1,0:T(2,128)S(1)} %all_to_all.20.cells_ref.refs_0_, ...), custom_call_target="tpu_custom_call" | custom-call | tf_op jit(solution)/shard_map/short_forward/pallas_call | solution.py:776
  18.8 2.6 %all-to-all-start.1 = ((f32[32,4,128]{2,1,0:T(4,128)}), f32[32,4,128]{2,1,0:T(4,128)S(1)}, u32[]{:S(2)}, u32[]{:S(2)}) async-start(f32[32,4,128]{2,1,0:T(4,128)} %get-tuple-element.40), calls=%async_computation.1 | async-start | bytes 131072 | tf_op jit(solution)/shard_map/all_to_all | solution.py:718
  21.4 2.3 %weights.1 = (f32[128,128]{1,0:T(8,128)S(1)}, f32[96,128]{1,0:T(8,128)S(1)}, f32[4,56,24]{2,1,0:T(8,128)S(1)}, f32[8,24]{1,0:T(8,128)S(1)}, f32[6,8,4096]{2,1,0:T(8,128)S(1)}) custom-call(f32[128,128]{1,0:T(8,128)S(1)} %get-tuple-element.41.upd_ref, f32[96,128]{1,0:T(8,128)S(1)} %get-tuple-element.42.mixed_ref, ...), custom_call_target="tpu_custom_call" | custom-call | flops 32256000 | bytes 512000 | tf_op jit(solution)/shard_map/weights/pallas_call | solution.py:806
  23.7 5.3 %all-to-all-done.1.recv_ref = f32[32,4,128]{2,1,0:T(4,128)S(1)} async-done(((f32[32,4,128]{2,1,0:T(4,128)}), f32[32,4,128]{2,1,0:T(4,128)S(1)}, u32[]{:S(2)}, u32[]{:S(2)}) %all-to-all-start.1) | async-done | bytes 65568 | tf_op jit(solution)/shard_map/all_to_all | solution.py:718
  29.0 3.1 %waves.1 = (f32[32,4,128]{2,1,0:T(4,128)S(1)}, f32[32,4,128]{2,1,0:T(4,128)S(1)}) custom-call(f32[32,4,128]{2,1,0:T(4,128)S(1)} %all-to-all-done.1.recv_ref, f32[6,8,4096]{2,1,0:T(8,128)S(1)} %get-tuple-element.47.axes_ref, f32[4,56,24]{2,1,0:T(8,128)S(1)} %get-tuple-element.48.phi_ref, f32[8,24]{1,0:T(8,128)S(1)} %get-tuple-element.49.width_ref), custom_call_target="tpu_custom_call" | custom-call | tf_op jit(solution)/shard_map/waves/pallas_call | solution.py:860
  32.1 9.3 %all_to_all.21.recv_ref = f32[32,4,128]{2,1,0:T(4,128)S(1)} all-to-all(f32[32,4,128]{2,1,0:T(4,128)S(1)} %get-tuple-element.50), channel_id=1, replica_groups=mesh['row'=16,'col'=2] {'row','col'}, dimensions={0} | all-to-all | bytes 131072 | tf_op jit(solution)/shard_map/all_to_all | solution.py:718
  41.4 1.4 %short_back.1 = f32[32,4,128]{2,1,0:T(4,128)S(1)} custom-call(f32[32,4,128]{2,1,0:T(4,128)S(1)} %all_to_all.21.recv_ref, f32[3,64,128]{2,1,0:T(8,128)S(1)} %get-tuple-element.51.vec_ref, f32[64,128]{1,0:T(8,128)S(1)} %get-tuple-element.52.kind_ref, f32[128,128]{1,0:T(8,128)S(1)} %get-tuple-element.53.dupd_ref, f32[128,128]{1,0:T(8,128)S(1)} %get-tuple-element.54.slope_ref, ...), custom_call_target="tpu_custom_call" | custom-call | tf_op jit(solution)/shard_map/short_back/pallas_call | solution.py:871
  42.8 9.3 %all_to_all.22.recv_ref = f32[32,4,128]{2,1,0:T(4,128)S(1)} all-to-all(f32[32,4,128]{2,1,0:T(4,128)S(1)} %short_back.1), channel_id=1, replica_groups=mesh['row'=16,'col'=2] {'row','col'}, dimensions={0} | all-to-all | bytes 131072 | tf_op jit(solution)/shard_map/all_to_all | solution.py:718
  52.1 0.7 %total.1 = (f32[3,1,128]{2,1,0:T(1,128)}, f32[3,3]{1,0:T(4,128)}) custom-call(f32[32,4,128]{2,1,0:T(4,128)S(1)} %all_to_all.22.recv_ref), custom_call_target="tpu_custom_call" | custom-call | tf_op jit(solution)/shard_map/total/pallas_call | solution.py:885
Async XLA Ops:
  18.8 10.2 %all-to-all-start.1 = ((f32[32,4,128]{2,1,0:T(4,128)}), f32[32,4,128]{2,1,0:T(4,128)S(1)}, u32[]{:S(2)}, u32[]{:S(2)}) async-start(f32[32,4,128]{2,1,0:T(4,128)} %get-tuple-element.40), calls=%async_computation.1 | async-start | bytes 131072 | tf_op jit(solution)/shard_map/all_to_all | solution.py:718

commit v8 on v7

--- a/solution.py
+++ b/solution.py
@@ -160,12 +160,14 @@
 
 
 def weights_kernel(dims, table_dims, upd_ref, mixed_ref, *refs):
-    cells, refs = refs[: len(refs) - 17 - bool(table_dims)], refs[len(refs) - 17 - bool(table_dims) :]
+    cells, refs = refs[: bool(table_dims)], refs[bool(table_dims) :]
     sources, (dupd_ref, back_ref, phi_ref, width_out_ref), refs = refs[:6], refs[6:10], refs[10:]
     axes, targets, sems = refs[: len(refs) - 7], refs[-7:-1], refs[-1]
     copies = start_copies(tuple(zip(sources, targets)), sems)
     if table_dims:
-        table_kernel(table_dims, *cells, *axes)
+        table_kernel(table_dims, *cells, axes[0])
+        if len(axes) > 1:
+            wave_planes(axes[1], axes[0], range(axes[1].shape[1] // upd_ref.shape[1]))
     pooled_rows, channel_count = mixed_ref.shape
     radial_count = dims[5]
     order_id = lax.broadcasted_iota(jnp.int32, (pooled_rows, channel_count), 0) % radial_count
@@ -361,30 +363,19 @@
     lax.fori_loop(0, chunk, one, 0, unroll=4)
 
 
-def wave_kernel(
-    dims,
-    recv_ref,
-    axes_ref,
-    phi_ref,
-    width_ref,
-    send_ref,
-    push_ref,
-    planes_ref,
-    heights,
-    lifted,
-    sums,
-    coefficients,
-):
-    own_channels, chunk_count, lengths = dims
-    planes = (planes_ref, axes_ref, heights, lifted)
+def wave_kernel(dims, recv_ref, axes_ref, phi_ref, width_ref, *refs):
+    own_channels, chunk_count, lengths, ready = dims
+    made, (send_ref, push_ref, *planes), (heights, lifted, sums, coefficients) = refs[:ready], refs[ready:-4], refs[-4:]
+    planes = (*made, *planes)
+    parts = (planes, ready, axes_ref, heights, lifted)
 
     def back():
-        wave_back(own_channels, lengths, planes_ref, heights, lifted, coefficients, send_ref, push_ref)
+        wave_back(own_channels, lengths, planes, heights, lifted, coefficients, send_ref, push_ref)
         virial = wave_virial(own_channels, lengths, sums, phi_ref, width_ref, (1, push_ref.shape[2]))
         push_ref[:, 3, :] = jnp.broadcast_to(virial, (push_ref.shape[0], push_ref.shape[2]))
 
     if chunk_count == 1:
-        sums[...] = wave_sums(own_channels, recv_ref, *planes)
+        sums[...] = wave_sums(own_channels, recv_ref, *parts)
         wave_coefficients(sums, phi_ref, coefficients)
         back()
         return
@@ -394,7 +385,7 @@
     def _():
         sums[...] = jnp.zeros_like(sums)
 
-    part = wave_sums(own_channels, recv_ref, *planes)
+    part = wave_sums(own_channels, recv_ref, *parts)
 
     @pl.when(phase == 0)
     def _():
@@ -409,12 +400,31 @@
         back()
 
 
-def wave_planes(own_channels, recv_ref, planes_ref, axes_ref, heights, lifted, devices):
+def wave_planes(planes_ref, axes_ref, devices):
+    atom_count = planes_ref.shape[1] // len(devices)
+    count = planes_ref.shape[0] // 2
+    for place, index in enumerate(devices):
+        spot = slice(index * atom_count, (index + 1) * atom_count)
+        target = slice(place * atom_count, (place + 1) * atom_count)
+        products = [
+            axes_ref[first_axis, m : m + 1, spot] * axes_ref[second_axis, :, spot]
+            for first_axis, second_axis in ((0, 2), (0, 3), (1, 2), (1, 3))
+            for m in range(KMAX + 1)
+        ]
+        for pair in range(len(products) // 2):
+            both = jnp.concatenate(products[2 * pair : 2 * pair + 2], axis=0)
+            high = both.astype(BF16)
+            rows = slice(2 * HARMONICS * pair, 2 * HARMONICS * (pair + 1))
+            planes_ref[rows, target] = high
+            rows = slice(count + rows.start, count + rows.stop)
+            planes_ref[rows, target] = (both - high.astype(F32)).astype(BF16)
+
+
+def wave_lift(own_channels, recv_ref, axes_ref, heights, lifted, devices):
     atom_count = recv_ref.shape[2]
     together, tiles = tile_layout(own_channels)
     lanes = tiles * HARMONICS
     sublane = lax.broadcasted_iota(jnp.int32, (HARMONICS, atom_count), 0)
-    count = planes_ref.shape[0] // 2
     for index in devices:
         spot = slice(index * atom_count, (index + 1) * atom_count)
         feature = jnp.concatenate([recv_ref[index, 0:own_channels, :]] * together, axis=0)
@@ -429,35 +439,27 @@
                 row = part * lanes + tile * HARMONICS
                 heights[row : row + HARMONICS, spot] = height
                 lifted[row : row + HARMONICS, spot] = feature * height
-        products = [
-            axes_ref[first_axis, m : m + 1, spot] * axes_ref[second_axis, :, spot]
-            for first_axis, second_axis in ((0, 2), (0, 3), (1, 2), (1, 3))
-            for m in range(KMAX + 1)
-        ]
-        for pair in range(len(products) // 2):
-            both = jnp.concatenate(products[2 * pair : 2 * pair + 2], axis=0)
-            high = both.astype(BF16)
-            rows = slice(2 * HARMONICS * pair, 2 * HARMONICS * (pair + 1))
-            planes_ref[rows, spot] = high
-            rows = slice(count + rows.start, count + rows.stop)
-            planes_ref[rows, spot] = (both - high.astype(F32)).astype(BF16)
-
-
-def wave_sums(own_channels, recv_ref, planes_ref, axes_ref, heights, lifted):
+
+
+def plane_groups(chunk, planes):
+    each = chunk // len(planes)
+    return [(ref, range(place * each, (place + 1) * each)) for place, ref in enumerate(planes)]
+
+
+def wave_sums(own_channels, recv_ref, planes, ready, axes_ref, heights, lifted):
     chunk, _, atom_count = recv_ref.shape
     lanes = lifted.shape[0] // 2
-    group = math.gcd(chunk, 16)
-    count = planes_ref.shape[0] // 2
     total = 0.0
-    for first in range(0, chunk, group):
-        devices = range(first, first + group)
-        wave_planes(own_channels, recv_ref, planes_ref, axes_ref, heights, lifted, devices)
-        spot = slice(first * atom_count, (first + group) * atom_count)
-        values = lifted[:, spot]
+    for place, (ref, devices) in enumerate(plane_groups(chunk, planes)):
+        wave_lift(own_channels, recv_ref, axes_ref, heights, lifted, devices)
+        if place >= ready:
+            wave_planes(ref, axes_ref, devices)
+        count = ref.shape[0] // 2
+        values = lifted[:, devices[0] * atom_count : (devices[-1] + 1) * atom_count]
         high = values.astype(BF16)
         low = (values - high.astype(F32)).astype(BF16)
-        main = dot(planes_ref[0:count, spot], jnp.concatenate([high, low], axis=0), 1, 1)
-        total = total + main[:, : 2 * lanes] + (main[:, 2 * lanes :] + dot(planes_ref[count:, spot], high, 1, 1))
+        main = dot(ref[0:count, :], jnp.concatenate([high, low], axis=0), 1, 1)
+        total = total + main[:, : 2 * lanes] + (main[:, 2 * lanes :] + dot(ref[count:, :], high, 1, 1))
     return total
 
 
@@ -542,16 +544,19 @@
     return dot(both, planes_ref[...], 1, 0) + dot(values[count:], planes_ref[0 : values.shape[1], :], 1, 0)
 
 
-def wave_back(own_channels, lengths, planes_ref, heights, lifted, coefficients, send_ref, push_ref):
+def wave_back(own_channels, lengths, planes, heights, lifted, coefficients, send_ref, push_ref):
     chunk, _, atom_count = push_ref.shape
     together, tiles = tile_layout(own_channels)
     lanes = tiles * HARMONICS
     sublane = lax.broadcasted_iota(jnp.int32, (HARMONICS, atom_count), 0)
     numbers = [(sublane // own_channels + 1 + tile * together).astype(F32) for tile in range(tiles)]
-    result = wave_spread(planes_ref, coefficients)
-    for index in range(chunk):
+    spread = []
+    for ref, devices in plane_groups(chunk, planes):
+        result = wave_spread(ref, coefficients)
+        spread += [(result, place, index) for place, index in enumerate(devices)]
+    for result, place, index in spread:
         spot = slice(index * atom_count, (index + 1) * atom_count)
-        part = result[:, spot]
+        part = result[:, place * atom_count : (place + 1) * atom_count]
         feature = grad_x = grad_y = grad_z = jnp.zeros((HARMONICS, atom_count), F32)
         for tile in range(tiles):
             a, b = tile * HARMONICS, lanes + tile * HARMONICS
@@ -798,11 +803,14 @@
     features = exchange(send)
 
     axes_block = (6, HARMONICS, chunk * atom_count)
+    ready = int(chunk_count == 1 and chunk % 2 == 0)
     axes_shape = shape(6, HARMONICS, device_count * atom_count)
     table_dims = (col_count, chunk_count, lengths)
     cells_inputs, axes_outputs = (), ()
     if chunk_count == 1:
         cells_inputs, axes_outputs = (cells,), (axes_shape,)
+        if ready:
+            axes_outputs += (jax.ShapeDtypeStruct((8 * rows, chunk // 2 * atom_count), BF16),)
     dupd, back, phi, width, *axes = call(
         functools.partial(
             weights_kernel,
@@ -839,7 +847,7 @@
         ]
     features, dupd, back = lax.optimization_barrier((features, dupd, back))
 
-    plane = pltpu.VMEM((8 * rows, chunk * atom_count), BF16)
+    plane = pltpu.VMEM((8 * rows, chunk // (1 + ready) * atom_count), BF16)
     wave_scratch = [plane] + [scratch(2 * lanes, chunk * atom_count)] * 2
     features_block = (chunk, slab_features, atom_count)
     wave_options = {}
@@ -858,14 +866,14 @@
             ),
         )
     send, push = call(
-        functools.partial(wave_kernel, (own_channels, chunk_count, lengths)),
+        functools.partial(wave_kernel, (own_channels, chunk_count, lengths, ready)),
         (shape(device_count, slab_features, atom_count), shape(device_count, 4, atom_count)),
         vmem=32,
         scratch_shapes=wave_scratch
         + [scratch(4 * rows, 2 * lanes), pltpu.VMEM((12 * lanes, 4 * rows), BF16)],
         name="waves",
         **wave_options,
-    )(features, *axes, phi, width)
+    )(features, axes[0], phi, width, *axes[1:])
     gradients = exchange(send)
 
     send = call(

time: 53 us -> 52.8 us (level)
  transfers between devices with their start and end apart: 1 -> 1, of which waited for: 1 -> 1; matrix products, arithmetic and copies ran while one was open for 0% -> 0% of each run, Pallas kernels for 4% -> 5%
where the time goes in v8:
time: 52.8 us; the launch traced here: 52.5 us
  blocking collectives  33.8 us (64%)
  Pallas kernels  10.5 us (20%)
  waiting for transfers between devices  4.96 us (9%)
  starting transfers between devices  2.57 us (5%)
  between operations  0.67 us (1%)
    all_to_all x3, blocking collectives, exchange(): return lax.all_to_all(slabs, AXES, 0, 0, tiled=True)  33.8 us
    all_to_all x1, waiting for transfers between devices, exchange(): return lax.all_to_all(slabs, AXES, 0, 0, tiled=True)  4.96 us
    pallas_call x1, Pallas kernels, per_device(): call(functools.partial(wave_kernel, (own_channels, chunk_count, lengths,...  2.87 us
    pallas_call x1, Pallas kernels, per_device(): call(functools.partial(weights_kernel, (device_count, channel_count, own_...  2.64 us
    all_to_all x1, starting transfers between devices, exchange(): return lax.all_to_all(slabs, AXES, 0, 0, tiled=True)  2.57 us
    pallas_call x1, Pallas kernels, per_device(): call(functools.partial(short_forward_kernel, (own_channels,) + mesh_count...  1.92 us
    pallas_call x1, Pallas kernels, per_device(): call(functools.partial(short_back_kernel, (own_channels,) + mesh_counts +...  1.37 us
  transfers between devices with their start and end apart: 1, of which 1 were waited for; matrix products, arithmetic and copies ran while one was open for 0% of the time, Pallas kernels for 5%

profile of v8, /device:TPU:0, one launch (start us, length us, event | category | flops | bytes accessed | tf_op | source)
XLA Modules:
  0.0 52.5 jit_solution(12601359597675824366)
XLA Ops:
  0.6 1.0 %pack.1 = (f32[32,2,384]{2,1,0:T(2,128)S(1)}, s32[1,128]{1,0:T(1,128)S(1)}, s32[64,128]{1,0:T(8,128)S(1)}, f32[16,128]{1,0:T(8,128)S(1)}, f32[6,128]{1,0:T(8,128)S(1)}, /*index=5*/f32[128,128]{1,0:T(8,128)S(1)}) custom-call(f32[3,1,128]{2,1,0:T(1,128)} %bitcast.13, s32[1,128]{1,0:T(1,128)} %bitcast.14, s32[8,128]{1,0:T(8,128)} %bitcast.12, ...), custom_call_target="tpu_custom_call" | custom-call | tf_op jit(solution)/shard_map/pack/pallas_call | solution.py:763
  1.7 15.2 %all_to_all.20.cells_ref.refs_0_ = f32[32,2,384]{2,1,0:T(2,128)S(1)} all-to-all(f32[32,2,384]{2,1,0:T(2,128)S(1)} %get-tuple-element.32), channel_id=1, replica_groups=mesh['row'=16,'col'=2] {'row','col'}, dimensions={0} | all-to-all | bytes 196608 | tf_op jit(solution)/shard_map/all_to_all | solution.py:723
  16.9 1.9 %short_forward.1 = (f32[32,4,128]{2,1,0:T(4,128)}, f32[3,64,128]{2,1,0:T(8,128)S(1)}, f32[64,128]{1,0:T(8,128)S(1)}, s32[64,128]{1,0:T(8,128)S(1)}, f32[128,128]...) custom-call(f32[32,2,384]{2,1,0:T(2,128)S(1)} %all_to_all.20.cells_ref.refs_0_, ...), custom_call_target="tpu_custom_call" | custom-call | tf_op jit(solution)/shard_map/short_forward/pallas_call | solution.py:781
  18.8 2.6 %all-to-all-start.1 = ((f32[32,4,128]{2,1,0:T(4,128)}), f32[32,4,128]{2,1,0:T(4,128)S(1)}, u32[]{:S(2)}, u32[]{:S(2)}) async-start(f32[32,4,128]{2,1,0:T(4,128)} %get-tuple-element.41), calls=%async_computation.1 | async-start | bytes 131072 | tf_op jit(solution)/shard_map/all_to_all | solution.py:723
  21.4 2.6 %weights.1 = (f32[128,128]{1,0:T(8,128)S(1)}, f32[96,128]{1,0:T(8,128)S(1)}, f32[4,56,24]{2,1,0:T(8,128)S(1)}, f32[8,24]{1,0:T(8,128)S(1)}, f32[6,8,4096]{2,1,0:T(8,128)S(1)}, /*index=5*/bf16[448,2048]{1,0:T(8,128)(2,1)S(1)}) custom-call(f32[128,128]{1,0:T(8,128)S(1)} %get-tuple-element.42.upd_ref, f32[96,128]{1,0:T(8,128)S(1)} %get-tuple-element.43.mixed_ref, ...), custom_call_target="tpu_custom_call" | custom-call | flops 32256000 | bytes 512000 | tf_op jit(solution)/shard_map/weights/pallas_call | solution.py:814
  24.0 5.0 %all-to-all-done.1.recv_ref = f32[32,4,128]{2,1,0:T(4,128)S(1)} async-done(((f32[32,4,128]{2,1,0:T(4,128)}), f32[32,4,128]{2,1,0:T(4,128)S(1)}, u32[]{:S(2)}, u32[]{:S(2)}) %all-to-all-start.1) | async-done | bytes 65568 | tf_op jit(solution)/shard_map/all_to_all | solution.py:723
  29.0 2.9 %waves.1 = (f32[32,4,128]{2,1,0:T(4,128)S(1)}, f32[32,4,128]{2,1,0:T(4,128)S(1)}) custom-call(f32[32,4,128]{2,1,0:T(4,128)S(1)} %all-to-all-done.1.recv_ref, f32[6,8,4096]{2,1,0:T(8,128)S(1)} %get-tuple-element.48.axes_ref, f32[4,56,24]{2,1,0:T(8,128)S(1)} %get-tuple-element.49.phi_ref, f32[8,24]{1,0:T(8,128)S(1)} %get-tuple-element.50.width_ref, ...), custom_call_target="tpu_custom_call" | custom-call | tf_op jit(solution)/shard_map/waves/pallas_call | solution.py:868
  31.9 9.3 %all_to_all.21.recv_ref = f32[32,4,128]{2,1,0:T(4,128)S(1)} all-to-all(f32[32,4,128]{2,1,0:T(4,128)S(1)} %get-tuple-element.52), channel_id=1, replica_groups=mesh['row'=16,'col'=2] {'row','col'}, dimensions={0} | all-to-all | bytes 131072 | tf_op jit(solution)/shard_map/all_to_all | solution.py:723
  41.2 1.4 %short_back.1 = f32[32,4,128]{2,1,0:T(4,128)S(1)} custom-call(f32[32,4,128]{2,1,0:T(4,128)S(1)} %all_to_all.21.recv_ref, f32[3,64,128]{2,1,0:T(8,128)S(1)} %get-tuple-element.53.vec_ref, f32[64,128]{1,0:T(8,128)S(1)} %get-tuple-element.54.kind_ref, f32[128,128]{1,0:T(8,128)S(1)} %get-tuple-element.55.dupd_ref, f32[128,128]{1,0:T(8,128)S(1)} %get-tuple-element.56.slope_ref, ...), custom_call_target="tpu_custom_call" | custom-call | tf_op jit(solution)/shard_map/short_back/pallas_call | solution.py:879
  42.5 9.3 %all_to_all.22.recv_ref = f32[32,4,128]{2,1,0:T(4,128)S(1)} all-to-all(f32[32,4,128]{2,1,0:T(4,128)S(1)} %short_back.1), channel_id=1, replica_groups=mesh['row'=16,'col'=2] {'row','col'}, dimensions={0} | all-to-all | bytes 131072 | tf_op jit(solution)/shard_map/all_to_all | solution.py:723
  51.8 0.7 %total.1 = (f32[3,1,128]{2,1,0:T(1,128)}, f32[3,3]{1,0:T(4,128)}) custom-call(f32[32,4,128]{2,1,0:T(4,128)S(1)} %all_to_all.22.recv_ref), custom_call_target="tpu_custom_call" | custom-call | tf_op jit(solution)/shard_map/total/pallas_call | solution.py:893
Async XLA Ops:
  18.8 10.2 %all-to-all-start.1 = ((f32[32,4,128]{2,1,0:T(4,128)}), f32[32,4,128]{2,1,0:T(4,128)S(1)}, u32[]{:S(2)}, u32[]{:S(2)}) async-start(f32[32,4,128]{2,1,0:T(4,128)} %get-tuple-element.41), calls=%async_computation.1 | async-start | bytes 131072 | tf_op jit(solution)/shard_map/all_to_all | solution.py:723

commit v9 on v8

--- a/solution.py
+++ b/solution.py
@@ -578,8 +578,14 @@
             grad_y * (2.0 * math.pi / lengths[1]),
             grad_z * (2.0 * math.pi / lengths[2]),
         )
-        for row, piece in enumerate(pieces):
-            push_ref[index, row : row + 1, :] = jnp.sum(piece, axis=0, keepdims=True)
+        first, second, third = (piece + pltpu.roll(piece, HARMONICS // 2, 0) for piece in pieces)
+        first = jnp.where(sublane < HARMONICS // 2, first, second)
+        first = first + pltpu.roll(first, 2, 0)
+        third = third + pltpu.roll(third, 2, 0)
+        first = jnp.where(sublane % 4 >= 2, first, third)
+        first = first + pltpu.roll(first, 1, 0)
+        for row, place in enumerate((3, 7, 1)):
+            push_ref[index, row : row + 1, :] = first[place : place + 1]
 
 
 def virial_row(terms, shape):

time: 52.8 us -> 52.8 us (level)
  no operation moved by 1% of the time
where the time goes in v9:
time: 52.8 us; the launch traced here: 52.5 us
  blocking collectives  33.8 us (64%)
  Pallas kernels  10.5 us (20%)
  waiting for transfers between devices  4.96 us (9%)
  starting transfers between devices  2.57 us (5%)
  between operations  0.67 us (1%)
    all_to_all x3, blocking collectives, exchange(): return lax.all_to_all(slabs, AXES, 0, 0, tiled=True)  33.8 us
    all_to_all x1, waiting for transfers between devices, exchange(): return lax.all_to_all(slabs, AXES, 0, 0, tiled=True)  4.96 us
    pallas_call x1, Pallas kernels, per_device(): call(functools.partial(wave_kernel, (own_channels, chunk_count, lengths,...  2.87 us
    pallas_call x1, Pallas kernels, per_device(): call(functools.partial(weights_kernel, (device_count, channel_count, own_...  2.64 us
    all_to_all x1, starting transfers between devices, exchange(): return lax.all_to_all(slabs, AXES, 0, 0, tiled=True)  2.57 us
    pallas_call x1, Pallas kernels, per_device(): call(functools.partial(short_forward_kernel, (own_channels,) + mesh_count...  1.92 us
    pallas_call x1, Pallas kernels, per_device(): call(functools.partial(short_back_kernel, (own_channels,) + mesh_counts +...  1.37 us
  transfers between devices with their start and end apart: 1, of which 1 were waited for; matrix products, arithmetic and copies ran while one was open for 0% of the time, Pallas kernels for 5%

profile of v9, /device:TPU:0, one launch (start us, length us, event | category | flops | bytes accessed | tf_op | source)
XLA Modules:
  0.0 52.5 jit_solution(12642211754759052580)
XLA Ops:
  0.6 1.0 %pack.1 = (f32[32,2,384]{2,1,0:T(2,128)S(1)}, s32[1,128]{1,0:T(1,128)S(1)}, s32[64,128]{1,0:T(8,128)S(1)}, f32[16,128]{1,0:T(8,128)S(1)}, f32[6,128]{1,0:T(8,128)S(1)}, /*index=5*/f32[128,128]{1,0:T(8,128)S(1)}) custom-call(f32[3,1,128]{2,1,0:T(1,128)} %bitcast.13, s32[1,128]{1,0:T(1,128)} %bitcast.14, s32[8,128]{1,0:T(8,128)} %bitcast.12, ...), custom_call_target="tpu_custom_call" | custom-call | tf_op jit(solution)/shard_map/pack/pallas_call | solution.py:769
  1.7 15.2 %all_to_all.20.cells_ref.refs_0_ = f32[32,2,384]{2,1,0:T(2,128)S(1)} all-to-all(f32[32,2,384]{2,1,0:T(2,128)S(1)} %get-tuple-element.32), channel_id=1, replica_groups=mesh['row'=16,'col'=2] {'row','col'}, dimensions={0} | all-to-all | bytes 196608 | tf_op jit(solution)/shard_map/all_to_all | solution.py:729
  16.9 1.9 %short_forward.1 = (f32[32,4,128]{2,1,0:T(4,128)}, f32[3,64,128]{2,1,0:T(8,128)S(1)}, f32[64,128]{1,0:T(8,128)S(1)}, s32[64,128]{1,0:T(8,128)S(1)}, f32[128,128]...) custom-call(f32[32,2,384]{2,1,0:T(2,128)S(1)} %all_to_all.20.cells_ref.refs_0_, ...), custom_call_target="tpu_custom_call" | custom-call | tf_op jit(solution)/shard_map/short_forward/pallas_call | solution.py:787
  18.8 2.6 %all-to-all-start.1 = ((f32[32,4,128]{2,1,0:T(4,128)}), f32[32,4,128]{2,1,0:T(4,128)S(1)}, u32[]{:S(2)}, u32[]{:S(2)}) async-start(f32[32,4,128]{2,1,0:T(4,128)} %get-tuple-element.41), calls=%async_computation.1 | async-start | bytes 131072 | tf_op jit(solution)/shard_map/all_to_all | solution.py:729
  21.4 2.6 %weights.1 = (f32[128,128]{1,0:T(8,128)S(1)}, f32[96,128]{1,0:T(8,128)S(1)}, f32[4,56,24]{2,1,0:T(8,128)S(1)}, f32[8,24]{1,0:T(8,128)S(1)}, f32[6,8,4096]{2,1,0:T(8,128)S(1)}, /*index=5*/bf16[448,2048]{1,0:T(8,128)(2,1)S(1)}) custom-call(f32[128,128]{1,0:T(8,128)S(1)} %get-tuple-element.42.upd_ref, f32[96,128]{1,0:T(8,128)S(1)} %get-tuple-element.43.mixed_ref, ...), custom_call_target="tpu_custom_call" | custom-call | flops 32256000 | bytes 512000 | tf_op jit(solution)/shard_map/weights/pallas_call | solution.py:820
  24.0 5.0 %all-to-all-done.1.recv_ref = f32[32,4,128]{2,1,0:T(4,128)S(1)} async-done(((f32[32,4,128]{2,1,0:T(4,128)}), f32[32,4,128]{2,1,0:T(4,128)S(1)}, u32[]{:S(2)}, u32[]{:S(2)}) %all-to-all-start.1) | async-done | bytes 65568 | tf_op jit(solution)/shard_map/all_to_all | solution.py:729
  29.0 2.9 %waves.1 = (f32[32,4,128]{2,1,0:T(4,128)S(1)}, f32[32,4,128]{2,1,0:T(4,128)S(1)}) custom-call(f32[32,4,128]{2,1,0:T(4,128)S(1)} %all-to-all-done.1.recv_ref, f32[6,8,4096]{2,1,0:T(8,128)S(1)} %get-tuple-element.48.axes_ref, f32[4,56,24]{2,1,0:T(8,128)S(1)} %get-tuple-element.49.phi_ref, f32[8,24]{1,0:T(8,128)S(1)} %get-tuple-element.50.width_ref, ...), custom_call_target="tpu_custom_call" | custom-call | tf_op jit(solution)/shard_map/waves/pallas_call | solution.py:874
  31.9 9.3 %all_to_all.21.recv_ref = f32[32,4,128]{2,1,0:T(4,128)S(1)} all-to-all(f32[32,4,128]{2,1,0:T(4,128)S(1)} %get-tuple-element.52), channel_id=1, replica_groups=mesh['row'=16,'col'=2] {'row','col'}, dimensions={0} | all-to-all | bytes 131072 | tf_op jit(solution)/shard_map/all_to_all | solution.py:729
  41.2 1.4 %short_back.1 = f32[32,4,128]{2,1,0:T(4,128)S(1)} custom-call(f32[32,4,128]{2,1,0:T(4,128)S(1)} %all_to_all.21.recv_ref, f32[3,64,128]{2,1,0:T(8,128)S(1)} %get-tuple-element.53.vec_ref, f32[64,128]{1,0:T(8,128)S(1)} %get-tuple-element.54.kind_ref, f32[128,128]{1,0:T(8,128)S(1)} %get-tuple-element.55.dupd_ref, f32[128,128]{1,0:T(8,128)S(1)} %get-tuple-element.56.slope_ref, ...), custom_call_target="tpu_custom_call" | custom-call | tf_op jit(solution)/shard_map/short_back/pallas_call | solution.py:885
  42.5 9.3 %all_to_all.22.recv_ref = f32[32,4,128]{2,1,0:T(4,128)S(1)} all-to-all(f32[32,4,128]{2,1,0:T(4,128)S(1)} %short_back.1), channel_id=1, replica_groups=mesh['row'=16,'col'=2] {'row','col'}, dimensions={0} | all-to-all | bytes 131072 | tf_op jit(solution)/shard_map/all_to_all | solution.py:729
  51.8 0.7 %total.1 = (f32[3,1,128]{2,1,0:T(1,128)}, f32[3,3]{1,0:T(4,128)}) custom-call(f32[32,4,128]{2,1,0:T(4,128)S(1)} %all_to_all.22.recv_ref), custom_call_target="tpu_custom_call" | custom-call | tf_op jit(solution)/shard_map/total/pallas_call | solution.py:899
Async XLA Ops:
  18.8 10.2 %all-to-all-start.1 = ((f32[32,4,128]{2,1,0:T(4,128)}), f32[32,4,128]{2,1,0:T(4,128)S(1)}, u32[]{:S(2)}, u32[]{:S(2)}) async-start(f32[32,4,128]{2,1,0:T(4,128)} %get-tuple-element.41), calls=%async_computation.1 | async-start | bytes 131072 | tf_op jit(solution)/shard_map/all_to_all | solution.py:729

commit v10 on v9

--- a/solution.py
+++ b/solution.py
@@ -215,7 +215,7 @@
         weights[k * radial_count : (k + 1) * radial_count, :] = (
             radial_ref[...] * embed_ref[k : k + 1, :] * (1.0 / slot_count)
         )
-    weights[...] = dot(weights[...], mix_ref[...], 1, 0, EXACT)
+    weights[...] = dot(weights[...], mix_ref[...], 1, 0, GOOD)
     mixed_ref[...] = weights[...]
     own = slab_rows(cells_ref[neighbour_of((0, 0), row_count, col_count)], range(4), atom_count)
     domains, places = [], []

time: 52.8 us -> 52.8 us (level)
  no operation moved by 1% of the time
where the time goes in v10:
time: 52.8 us; the launch traced here: 52.5 us
  blocking collectives  33.8 us (64%)
  Pallas kernels  10.5 us (20%)
  waiting for transfers between devices  4.95 us (9%)
  starting transfers between devices  2.57 us (5%)
  between operations  0.67 us (1%)
    all_to_all x3, blocking collectives, exchange(): return lax.all_to_all(slabs, AXES, 0, 0, tiled=True)  33.8 us
    all_to_all x1, waiting for transfers between devices, exchange(): return lax.all_to_all(slabs, AXES, 0, 0, tiled=True)  4.95 us
    pallas_call x1, Pallas kernels, per_device(): call(functools.partial(wave_kernel, (own_channels, chunk_count, lengths,...  2.86 us
    pallas_call x1, Pallas kernels, per_device(): call(functools.partial(weights_kernel, (device_count, channel_count, own_...  2.64 us
    all_to_all x1, starting transfers between devices, exchange(): return lax.all_to_all(slabs, AXES, 0, 0, tiled=True)  2.57 us
    pallas_call x1, Pallas kernels, per_device(): call(functools.partial(short_forward_kernel, (own_channels,) + mesh_count...  1.9 us
    pallas_call x1, Pallas kernels, per_device(): call(functools.partial(short_back_kernel, (own_channels,) + mesh_counts +...  1.37 us
  transfers between devices with their start and end apart: 1, of which 1 were waited for; matrix products, arithmetic and copies ran while one was open for 0% of the time, Pallas kernels for 5%

profile of v10, /device:TPU:0, one launch (start us, length us, event | category | flops | bytes accessed | tf_op | source)
XLA Modules:
  0.0 52.5 jit_solution(18036819259481173614)
XLA Ops:
  0.6 1.0 %pack.1 = (f32[32,2,384]{2,1,0:T(2,128)S(1)}, s32[1,128]{1,0:T(1,128)S(1)}, s32[64,128]{1,0:T(8,128)S(1)}, f32[16,128]{1,0:T(8,128)S(1)}, f32[6,128]{1,0:T(8,128)S(1)}, /*index=5*/f32[128,128]{1,0:T(8,128)S(1)}) custom-call(f32[3,1,128]{2,1,0:T(1,128)} %bitcast.13, s32[1,128]{1,0:T(1,128)} %bitcast.14, s32[8,128]{1,0:T(8,128)} %bitcast.12, ...), custom_call_target="tpu_custom_call" | custom-call | tf_op jit(solution)/shard_map/pack/pallas_call | solution.py:769
  1.7 15.2 %all_to_all.20.cells_ref.refs_0_ = f32[32,2,384]{2,1,0:T(2,128)S(1)} all-to-all(f32[32,2,384]{2,1,0:T(2,128)S(1)} %get-tuple-element.32), channel_id=1, replica_groups=mesh['row'=16,'col'=2] {'row','col'}, dimensions={0} | all-to-all | bytes 196608 | tf_op jit(solution)/shard_map/all_to_all | solution.py:729
  16.9 1.9 %short_forward.1 = (f32[32,4,128]{2,1,0:T(4,128)}, f32[3,64,128]{2,1,0:T(8,128)S(1)}, f32[64,128]{1,0:T(8,128)S(1)}, s32[64,128]{1,0:T(8,128)S(1)}, f32[128,128]...) custom-call(f32[32,2,384]{2,1,0:T(2,128)S(1)} %all_to_all.20.cells_ref.refs_0_, ...), custom_call_target="tpu_custom_call" | custom-call | tf_op jit(solution)/shard_map/short_forward/pallas_call | solution.py:787
  18.8 2.6 %all-to-all-start.1 = ((f32[32,4,128]{2,1,0:T(4,128)}), f32[32,4,128]{2,1,0:T(4,128)S(1)}, u32[]{:S(2)}, u32[]{:S(2)}) async-start(f32[32,4,128]{2,1,0:T(4,128)} %get-tuple-element.41), calls=%async_computation.1 | async-start | bytes 131072 | tf_op jit(solution)/shard_map/all_to_all | solution.py:729
  21.4 2.6 %weights.1 = (f32[128,128]{1,0:T(8,128)S(1)}, f32[96,128]{1,0:T(8,128)S(1)}, f32[4,56,24]{2,1,0:T(8,128)S(1)}, f32[8,24]{1,0:T(8,128)S(1)}, f32[6,8,4096]{2,1,0:T(8,128)S(1)}, /*index=5*/bf16[448,2048]{1,0:T(8,128)(2,1)S(1)}) custom-call(f32[128,128]{1,0:T(8,128)S(1)} %get-tuple-element.42.upd_ref, f32[96,128]{1,0:T(8,128)S(1)} %get-tuple-element.43.mixed_ref, ...), custom_call_target="tpu_custom_call" | custom-call | flops 32256000 | bytes 512000 | tf_op jit(solution)/shard_map/weights/pallas_call | solution.py:820
  24.0 5.0 %all-to-all-done.1.recv_ref = f32[32,4,128]{2,1,0:T(4,128)S(1)} async-done(((f32[32,4,128]{2,1,0:T(4,128)}), f32[32,4,128]{2,1,0:T(4,128)S(1)}, u32[]{:S(2)}, u32[]{:S(2)}) %all-to-all-start.1) | async-done | bytes 65568 | tf_op jit(solution)/shard_map/all_to_all | solution.py:729
  29.0 2.9 %waves.1 = (f32[32,4,128]{2,1,0:T(4,128)S(1)}, f32[32,4,128]{2,1,0:T(4,128)S(1)}) custom-call(f32[32,4,128]{2,1,0:T(4,128)S(1)} %all-to-all-done.1.recv_ref, f32[6,8,4096]{2,1,0:T(8,128)S(1)} %get-tuple-element.48.axes_ref, f32[4,56,24]{2,1,0:T(8,128)S(1)} %get-tuple-element.49.phi_ref, f32[8,24]{1,0:T(8,128)S(1)} %get-tuple-element.50.width_ref, ...), custom_call_target="tpu_custom_call" | custom-call | tf_op jit(solution)/shard_map/waves/pallas_call | solution.py:874
  31.8 9.3 %all_to_all.21.recv_ref = f32[32,4,128]{2,1,0:T(4,128)S(1)} all-to-all(f32[32,4,128]{2,1,0:T(4,128)S(1)} %get-tuple-element.52), channel_id=1, replica_groups=mesh['row'=16,'col'=2] {'row','col'}, dimensions={0} | all-to-all | bytes 131072 | tf_op jit(solution)/shard_map/all_to_all | solution.py:729
  41.1 1.4 %short_back.1 = f32[32,4,128]{2,1,0:T(4,128)S(1)} custom-call(f32[32,4,128]{2,1,0:T(4,128)S(1)} %all_to_all.21.recv_ref, f32[3,64,128]{2,1,0:T(8,128)S(1)} %get-tuple-element.53.vec_ref, f32[64,128]{1,0:T(8,128)S(1)} %get-tuple-element.54.kind_ref, f32[128,128]{1,0:T(8,128)S(1)} %get-tuple-element.55.dupd_ref, f32[128,128]{1,0:T(8,128)S(1)} %get-tuple-element.56.slope_ref, ...), custom_call_target="tpu_custom_call" | custom-call | tf_op jit(solution)/shard_map/short_back/pallas_call | solution.py:885
  42.5 9.3 %all_to_all.22.recv_ref = f32[32,4,128]{2,1,0:T(4,128)S(1)} all-to-all(f32[32,4,128]{2,1,0:T(4,128)S(1)} %short_back.1), channel_id=1, replica_groups=mesh['row'=16,'col'=2] {'row','col'}, dimensions={0} | all-to-all | bytes 131072 | tf_op jit(solution)/shard_map/all_to_all | solution.py:729
  51.8 0.7 %total.1 = (f32[3,1,128]{2,1,0:T(1,128)}, f32[3,3]{1,0:T(4,128)}) custom-call(f32[32,4,128]{2,1,0:T(4,128)S(1)} %all_to_all.22.recv_ref), custom_call_target="tpu_custom_call" | custom-call | tf_op jit(solution)/shard_map/total/pallas_call | solution.py:899
Async XLA Ops:
  18.8 10.2 %all-to-all-start.1 = ((f32[32,4,128]{2,1,0:T(4,128)}), f32[32,4,128]{2,1,0:T(4,128)S(1)}, u32[]{:S(2)}, u32[]{:S(2)}) async-start(f32[32,4,128]{2,1,0:T(4,128)} %get-tuple-element.41), calls=%async_computation.1 | async-start | bytes 131072 | tf_op jit(solution)/shard_map/all_to_all | solution.py:729
